TPU v7x, 128 devices: a whole 4x4x4 slice. The times are simulated.
128 devices in a mesh: curve: 128 (over x, y, z, core).
Axes of the slice: x: 4, y: 4, z: 4, core: 2. Of those that a mesh axis runs over, the one named last changes fastest.
Arguments:
- sea_state: float32 [3, 25, 131072], P(None, None, 'curve'), may hold values from -6 to 6
- water_depth: float32 [25, 131072], P(None, 'curve'), may hold values from 0.25 to 4
- neighbours: int32 [4, 131072], P(None, 'curve'), may hold values from -1 to 1023, as said below
- neighbour_owner: int32 [4, 131072], P(None, 'curve'), may hold values from -1 to 127, as said below
- clusters: int32 [131072], P('curve'), may hold values from 0 to 1, as said below
- block_swap: int32 [4096], P('curve'), may hold values from 0 to 1, as said below
Outputs:
- moved_state: float32 [3, 25, 131072], P(None, None, 'curve')
Inputs may be any that keep to these rules, and one draw needn't show every extreme that they name: Entry f of a cell is the position, within its owner's block, of its neighbour across face f (0 west, 1 east, 2 south, 3 north), -1 at a wall or the domain's edge; if a names b across face f, b names a across face f xor 1. Cell l of a device lies at row l // 32 and column l % 32 of the device's square block; faces between blocks of two devices are never walls; the cells along one edge of a block have their neighbours beyond it on one device, another one for each edge. `neighbour_owner`: entry f is the device that holds the neighbour across face f, -1 exactly where neighbours is -1. A neighbour on another device lies 1 or 64 devices away along the curve, and both distances occur. `clusters`: 0: the cell takes two half steps; 1: one whole step. `block_swap`: A block and its partner carry the same value; it is 0 where the partner would lie outside the curve.
All inputs are finite; a program needn't handle non-finite values.
Results may differ from a plain program's by a relative error of at most 0.0001.
Values sent between devices are 32-bit elements; how exact they have to be, the bound alone decides.
No kernel may reach another device: no remote copies, remote signals or barrier semaphores. Data moves between devices by JAX's collectives and lax.ppermute only.
A program may use at most 64 MiB of HBM per device.

v0:
```python
import math

import jax
import jax.numpy as jnp
import numpy as np
from jax import lax
from jax.sharding import PartitionSpec as P

BS = 32


LAMBDA_STEP = 0.06
LIFT_SCALE = 10.0
HIGHEST = lax.Precision.HIGHEST
FACE_NODES = ((0, 5, 10, 15, 20), (4, 9, 14, 19, 24), (0, 1, 2, 3, 4), (20, 21, 22, 23, 24))
NORMALS = ((-1.0, 0.0), (1.0, 0.0), (0.0, -1.0), (0.0, 1.0))


def passed_along(shard, axis, by):
    peers = lax.axis_size(axis)
    pairs = [(i, i + by) for i in range(peers) if 0 <= i + by < peers]
    return lax.ppermute(shard, axis, pairs)


def derivative_matrix():
    points = np.array([-1.0, -np.sqrt(3.0 / 7.0), 0.0, np.sqrt(3.0 / 7.0), 1.0])
    weights = []
    for column in range(5):
        product = 1.0
        for other_point in range(5):
            if other_point != column:
                product = product * (points[column] - points[other_point])
        weights.append(1.0 / product)
    matrix = np.zeros((5, 5))
    for row_index in range(5):
        for column in range(5):
            if row_index != column:
                matrix[row_index, column] = (
                    weights[column] / weights[row_index] / (points[row_index] - points[column])
                )
        matrix[row_index, row_index] = -np.sum(matrix[row_index])
    return matrix


def operator_tables():
    deriv_small = derivative_matrix()
    identity = np.eye(5)
    lift_table = np.zeros((4, 25, 5))
    for face_index in range(4):
        for node_index in range(5):
            lift_table[face_index, FACE_NODES[face_index][node_index], node_index] = 1.0
    deriv_x = jnp.asarray(np.kron(identity, deriv_small), dtype=jnp.float32)
    deriv_y = jnp.asarray(np.kron(deriv_small, identity), dtype=jnp.float32)
    return (deriv_x, deriv_y, jnp.asarray(lift_table, dtype=jnp.float32))


def face_trace(values_in, face_index):
    if face_index == 0:
        return values_in[..., 0::5, :]
    if face_index == 1:
        return values_in[..., 4::5, :]
    if face_index == 2:
        return values_in[..., 0:5, :]
    return values_in[..., 20:25, :]


def product_of(matrix, field):
    return jnp.dot(matrix, field, preferred_element_type=jnp.float32, precision=HIGHEST)


def operate(fields, water_depth, deriv_x, deriv_y):
    grad_x = product_of(deriv_x, fields[0])
    grad_y = product_of(deriv_y, fields[0])
    spread = product_of(deriv_x, fields[1]) + product_of(deriv_y, fields[2])
    return -LAMBDA_STEP * jnp.stack([spread, water_depth * grad_x, water_depth * grad_y])


def taylor_list(fields, water_depth, deriv_x, deriv_y):
    result = [fields]
    for term_order in range(3):
        result.append(operate(result[-1], water_depth, deriv_x, deriv_y))
    return result


def integrate(taylor_terms, time_start, time_end):
    accumulated = jnp.zeros_like(taylor_terms[0])
    for term_order in range(4):
        factor = (time_end ** (term_order + 1) - time_start ** (term_order + 1)) / math.factorial(
            term_order + 1
        )
        accumulated = accumulated + factor * taylor_terms[term_order]
    return accumulated


def surface_term(fields, outer_list, water_depth, depth_list, wall_mask, lift_table):
    accumulated = jnp.zeros_like(fields)
    for face_index in range(4):
        normal_x, normal_y = NORMALS[face_index]
        inner_trace = face_trace(fields, face_index)
        depth_inner = face_trace(water_depth, face_index)
        mirror = jnp.stack(
            [
                inner_trace[0],
                inner_trace[1] * (1.0 - 2.0 * abs(normal_x)),
                inner_trace[2] * (1.0 - 2.0 * abs(normal_y)),
            ]
        )
        outer_trace = jnp.where(
            wall_mask[face_index][None, None, :], mirror, outer_list[face_index]
        )
        depth_outer = jnp.where(wall_mask[face_index][None, :], depth_inner, depth_list[face_index])
        wave_speed = jnp.sqrt(jnp.maximum(depth_inner, depth_outer))
        trace_jump = outer_trace - inner_trace
        jump_normal = trace_jump[1] * normal_x + trace_jump[2] * normal_y
        correction = (
            LAMBDA_STEP
            * LIFT_SCALE
            * 0.5
            * jnp.stack(
                [
                    wave_speed * trace_jump[0] - jump_normal,
                    wave_speed * trace_jump[1] - depth_inner * trace_jump[0] * normal_x,
                    wave_speed * trace_jump[2] - depth_inner * trace_jump[0] * normal_y,
                ]
            )
        )
        accumulated = accumulated + jnp.einsum(
            "nk,vkc->vnc", lift_table[face_index], correction, precision=HIGHEST
        )
    return accumulated


def edge_rows(own_faces, block_side):
    result = []
    for face_index in range(4):
        edge_grid = own_faces[face_index].reshape(
            own_faces[face_index].shape[0], block_side, block_side
        )
        if face_index == 0:
            result.append(edge_grid[:, :, 0])
        elif face_index == 1:
            result.append(edge_grid[:, :, block_side - 1])
        elif face_index == 2:
            result.append(edge_grid[:, 0, :])
        else:
            result.append(edge_grid[:, block_side - 1, :])
    return result


def deliver(own_faces, owners, peer_list, block_side, first_round):
    edges_out = edge_rows(own_faces, block_side)
    row_count = edges_out[0].shape[0]
    devices = lax.axis_size("curve")
    target = jnp.arange(devices, dtype=jnp.int32)[None, :, None]
    outgoing = jnp.zeros((row_count, devices, block_side), jnp.float32)
    for face_index in range(4):
        outgoing = jnp.where(
            target == peer_list[face_index], edges_out[face_index][:, None, :], outgoing
        )
    if first_round:
        received = lax.all_to_all(outgoing, "curve", split_axis=1, concat_axis=1, tiled=True)
    else:
        received = lax.all_to_all(outgoing, "curve", split_axis=1, concat_axis=1, tiled=True)
    flat_rows = received.reshape(row_count, devices * block_side)
    slot_list = [owners[face_index] for face_index in range(4)]
    return (flat_rows, slot_list)


def assemble(own_faces, flat_rows, slot_list, neighbours, owners, device_index, slots, block_side):
    result = []
    for face_index in range(4):
        local_index = jnp.clip(neighbours[face_index], 0, slots - 1)
        relative = jnp.maximum(neighbours[face_index], 0)
        if face_index < 2:
            edge_position = relative // block_side
        else:
            edge_position = relative % block_side
        remote_index = jnp.clip(
            slot_list[face_index] * block_side + edge_position, 0, flat_rows.shape[1] - 1
        )
        near_local = jnp.take(own_faces[face_index ^ 1], local_index, axis=1)
        near_remote = jnp.take(flat_rows, remote_index, axis=1)
        result.append(
            jnp.where((owners[face_index] == device_index)[None, :], near_local, near_remote)
        )
    return result


def local(sea_state, water_depth, neighbours, neighbour_owner, clusters, block_swap):
    deriv_x, deriv_y, lift_table = operator_tables()
    slots = sea_state.shape[-1]
    block_side = BS
    device_index = lax.axis_index("curve")
    wall_mask = [neighbours[face_index] < 0 for face_index in range(4)]
    owners = [neighbour_owner[face_index] for face_index in range(4)]
    peer_list = [
        jnp.max(
            jnp.where(
                wall_mask[face_index] | (owners[face_index] == device_index), -1, owners[face_index]
            )
        )
        for face_index in range(4)
    ]
    fine_mask = (clusters == 0)[None, None, :]
    taylor_terms = taylor_list(sea_state, water_depth, deriv_x, deriv_y)
    first_half = integrate(taylor_terms, 0.0, 0.5)
    second_half = integrate(taylor_terms, 0.5, 1.0)
    coarse_second = jnp.where(fine_mask, 0.0, second_half)
    own_first = [
        jnp.concatenate(
            [
                face_trace(first_half, face_index).reshape(15, slots),
                face_trace(coarse_second, face_index).reshape(15, slots),
                face_trace(water_depth, face_index),
            ],
            axis=0,
        )
        for face_index in range(4)
    ]
    flat_rows, slot_list = deliver(own_first, owners, peer_list, block_side, True)
    near_one = assemble(
        own_first, flat_rows, slot_list, neighbours, owners, device_index, slots, block_side
    )
    near_first = [values[0:15].reshape(3, 5, slots) for values in near_one]
    near_coarse = [values[15:30].reshape(3, 5, slots) for values in near_one]
    near_depth = [values[30:35] for values in near_one]
    middle = (
        sea_state
        + operate(first_half, water_depth, deriv_x, deriv_y)
        + surface_term(first_half, near_first, water_depth, near_depth, wall_mask, lift_table)
    )
    late_half = integrate(taylor_list(middle, water_depth, deriv_x, deriv_y), 0.0, 0.5)
    fine_late = jnp.where(fine_mask, late_half, 0.0)
    own_second = [face_trace(fine_late, face_index).reshape(15, slots) for face_index in range(4)]
    flat_late, slot_late = deliver(own_second, owners, peer_list, block_side, False)
    near_two = assemble(
        own_second, flat_late, slot_late, neighbours, owners, device_index, slots, block_side
    )
    near_late = [
        near_coarse[face_index] + near_two[face_index].reshape(3, 5, slots)
        for face_index in range(4)
    ]
    fine_state = (
        middle
        + operate(late_half, water_depth, deriv_x, deriv_y)
        + surface_term(late_half, near_late, water_depth, near_depth, wall_mask, lift_table)
    )
    whole_step = first_half + second_half
    near_whole = [near_first[face_index] + near_late[face_index] for face_index in range(4)]
    coarse_state = (
        sea_state
        + operate(whole_step, water_depth, deriv_x, deriv_y)
        + surface_term(whole_step, near_whole, water_depth, near_depth, wall_mask, lift_table)
    )
    updated = jnp.where(fine_mask, fine_state, coarse_state)
    grouped = updated.reshape(3, 25, block_side, block_side)
    swap_mask = (block_swap > 0)[None, None, :, None]
    from_before = passed_along(grouped, "curve", 1)
    from_after = passed_along(grouped, "curve", -1)
    position = jnp.arange(block_side, dtype=jnp.int32)[None, None, :, None]
    merged = jnp.where((device_index + position) % 2 == 0, from_after, from_before)
    moved = jnp.where(swap_mask, merged, grouped)
    return moved.reshape(3, 25, slots)


def solution(mesh):
    return jax.shard_map(
        local,
        mesh=mesh,
        in_specs=(
            P(None, None, "curve"),
            P(None, "curve"),
            P(None, "curve"),
            P(None, "curve"),
            P("curve"),
            P("curve"),
        ),
        out_specs=P(None, None, "curve"),
        check_vma=False,
    )
```

profile of v0, /device:TPU:6, one launch (start us, length us, event | category | flops | bytes accessed | tf_op | source)
XLA Modules:
  0.0 243.8 jit_solution(3414376986517210366)
XLA Ops:
  25.0 3.5 %reshape.450 = f32[128,1,1120]{2,1,0:T(1,128)} reshape(f32[128,32,35]{2,1,0:T(8,128)S(1)} %fusion.202) | data formatting | bytes 1146880
  28.6 10.5 %all-to-all-start = ((f32[128,1,1120]{2,1,0:T(1,128)}), f32[128,1,1120]{2,1,0:T(1,128)S(1)}, u32[]{:S(2)}, u32[]{:S(2)}) async-start(f32[128,1,1120]{2,1,0:T(1,128)} %reshape.450), calls=%async_computation | async-start | bytes 1179648 | tf_op jit(solution)/shard_map/all_to_all | solution.py:161
  56.6 2.8 %gather_fusion = f32[1024,35]{1,0:T(8,128)S(1)} fusion(f32[35,1024]{0,1:T(8,128)S(1)} %copy.90, s32[1024]{0:T(1024)S(1)} %fusion.152), kind=kCustom, calls=%fused_computation.clone | custom fusion | bytes 290816 | tf_op jit(solution)/shard_map/jit(_take)/gather | solution.py:181
  60.5 2.8 %gather_fusion.2 = f32[1024,35]{1,0:T(8,128)S(1)} fusion(f32[35,1024]{0,1:T(8,128)S(1)} %copy.97, s32[1024]{0:T(1024)S(1)} %fusion.153), kind=kCustom, calls=%fused_computation.4.clone | custom fusion | bytes 290816 | tf_op jit(solution)/shard_map/jit(_take)/gather | solution.py:181
  65.4 2.8 %gather_fusion.6 = f32[1024,35]{1,0:T(8,128)S(1)} fusion(f32[35,1024]{0,1:T(8,128)S(1)} %copy.103, s32[1024]{0:T(1024)S(1)} %fusion.155), kind=kCustom, calls=%fused_computation.6.clone | custom fusion | bytes 290816 | tf_op jit(solution)/shard_map/jit(_take)/gather | solution.py:181
  69.3 2.8 %gather_fusion.4 = f32[1024,35]{1,0:T(8,128)S(1)} fusion(f32[35,1024]{0,1:T(8,128)S(1)} %copy.100, s32[1024]{0:T(1024)S(1)} %fusion.154), kind=kCustom, calls=%fused_computation.5.clone | custom fusion | bytes 290816 | tf_op jit(solution)/shard_map/jit(_take)/gather | solution.py:181
  79.6 3.1 %reduce.24 = f32[128,1120]{1,0:T(8,128)} reduce(f32[128,1,1120]{2,1,0:T(1,128)S(1)} %all-to-all-done, f32[]{:T(128)} %broadcast.550), dimensions={1}, to_apply=%all_to_all.6.reduce_sub_computation | reduce | bytes 1146884 | tf_op jit(solution)/shard_map/all_to_all | solution.py:161
  82.7 3.7 %reshape.451 = f32[128,32,35]{2,1,0:T(8,128)S(1)} reshape(f32[128,1120]{1,0:T(8,128)} %reduce.24) | data formatting | bytes 1146880
  86.5 4.0 %gather_fusion.1 = f32[1024,35]{1,0:T(8,128)} fusion(f32[35,4096]{0,1:T(8,128)S(1)} %bitcast.635, s32[1024]{0:T(1024)S(1)} %copy-done.97), kind=kCustom, calls=%fused_computation.1.clone | custom fusion | bytes 290816 | tf_op jit(solution)/shard_map/jit(_take)/gather | solution.py:182
  96.2 4.0 %gather_fusion.3 = f32[1024,35]{1,0:T(8,128)} fusion(f32[35,4096]{0,1:T(8,128)S(1)} %bitcast.636, s32[1024]{0:T(1024)S(1)} %copy-done.99), kind=kCustom, calls=%fused_computation.7.clone | custom fusion | bytes 290816 | tf_op jit(solution)/shard_map/jit(_take)/gather | solution.py:182
  112.8 4.0 %gather_fusion.7 = f32[1024,35]{1,0:T(8,128)} fusion(f32[35,4096]{0,1:T(8,128)S(1)} %bitcast.637, s32[1024]{0:T(1024)S(1)} %copy-done.87), kind=kCustom, calls=%fused_computation.9.clone | custom fusion | bytes 290816 | tf_op jit(solution)/shard_map/jit(_take)/gather | solution.py:182
  122.0 4.0 %gather_fusion.5 = f32[1024,35]{1,0:T(8,128)} fusion(f32[35,4096]{0,1:T(8,128)S(1)} %bitcast.638, s32[1024]{0:T(1024)S(1)} %copy-done.85), kind=kCustom, calls=%fused_computation.8.clone | custom fusion | bytes 290816 | tf_op jit(solution)/shard_map/jit(_take)/gather | solution.py:182
  143.4 9.8 %all-to-all-start.1 = ((f32[128,1,480]{2,1,0:T(1,128)}), f32[128,1,480]{2,1,0:T(1,128)S(1)}, u32[]{:S(2)}, u32[]{:S(2)}) async-start(f32[128,1,480]{2,1,0:T(1,128)} %reshape.452), calls=%async_computation.1 | async-start | bytes 524288 | tf_op jit(solution)/shard_map/all_to_all | solution.py:163
  156.6 2.8 %gather_fusion.8 = f32[1024,15]{1,0:T(8,128)S(1)} fusion(f32[15,1024]{0,1:T(8,128)S(1)} %copy.106, s32[1024]{0:T(1024)S(1)} %copy-done.90), kind=kCustom, calls=%fused_computation.2.clone | custom fusion | bytes 126976 | tf_op jit(solution)/shard_map/jit(_take)/gather | solution.py:181
  160.5 2.8 %gather_fusion.10 = f32[1024,15]{1,0:T(8,128)S(1)} fusion(f32[15,1024]{0,1:T(8,128)S(1)} %copy.110, s32[1024]{0:T(1024)S(1)} %copy-done.92), kind=kCustom, calls=%fused_computation.10.clone | custom fusion | bytes 126976 | tf_op jit(solution)/shard_map/jit(_take)/gather | solution.py:181
  164.3 2.8 %gather_fusion.14 = f32[1024,15]{1,0:T(8,128)S(1)} fusion(f32[15,1024]{0,1:T(8,128)S(1)} %copy.116, s32[1024]{0:T(1024)S(1)} %copy-done.94), kind=kCustom, calls=%fused_computation.12.clone | custom fusion | bytes 126976 | tf_op jit(solution)/shard_map/jit(_take)/gather | solution.py:181
  168.2 2.8 %gather_fusion.12 = f32[1024,15]{1,0:T(8,128)S(1)} fusion(f32[15,1024]{0,1:T(8,128)S(1)} %copy.113, s32[1024]{0:T(1024)S(1)} %copy-done.96), kind=kCustom, calls=%fused_computation.11.clone | custom fusion | bytes 126976 | tf_op jit(solution)/shard_map/jit(_take)/gather | solution.py:181
  177.1 4.0 %gather_fusion.9 = f32[1024,15]{1,0:T(8,128)} fusion(f32[15,4096]{0,1:T(8,128)S(1)} %bitcast.639, s32[1024]{0:T(1024)S(1)} %copy-done.98), kind=kCustom, calls=%fused_computation.3.clone | custom fusion | bytes 126976 | tf_op jit(solution)/shard_map/jit(_take)/gather | solution.py:182
  181.2 4.0 %gather_fusion.11 = f32[1024,15]{1,0:T(8,128)} fusion(f32[15,4096]{0,1:T(8,128)S(1)} %bitcast.640, s32[1024]{0:T(1024)S(1)} %copy-done.100), kind=kCustom, calls=%fused_computation.13.clone | custom fusion | bytes 126976 | tf_op jit(solution)/shard_map/jit(_take)/gather | solution.py:182
  185.2 4.0 %gather_fusion.15 = f32[1024,15]{1,0:T(8,128)} fusion(f32[15,4096]{0,1:T(8,128)S(1)} %bitcast.641, s32[1024]{0:T(1024)S(1)} %copy-done.88), kind=kCustom, calls=%fused_computation.15.clone | custom fusion | bytes 126976 | tf_op jit(solution)/shard_map/jit(_take)/gather | solution.py:182
  189.1 4.0 %gather_fusion.13 = f32[1024,15]{1,0:T(8,128)} fusion(f32[15,4096]{0,1:T(8,128)S(1)} %bitcast.642, s32[1024]{0:T(1024)S(1)} %copy-done.86), kind=kCustom, calls=%fused_computation.14.clone | custom fusion | bytes 126976 | tf_op jit(solution)/shard_map/jit(_take)/gather | solution.py:182
  212.1 7.6 %collective-permute-start = (f32[3,25,32,32]{3,2,1,0:T(8,128)S(1)}, f32[3,25,32,32]{3,2,1,0:T(8,128)S(1)}, u32[]{:S(2)}, u32[]{:S(2)}) collective-permute-start(f32[3,25,32,32]{3,2,1,0:T(8,128)S(1)} %reshape.256), channel_id=1, source_target_pairs={{1,0},{2,1},{3,2},{4,3},{5,4},{6,5},{7,6},{8,7},{9,8},{10,9},{11,1... | collective-permute-start | bytes 921608 | tf_op jit(solution)/shard_map/ppermute | solution.py:22
  221.7 12.3 %collective-permute-done = f32[3,25,32,32]{3,2,1,0:T(8,128)S(1)} collective-permute-done((f32[3,25,32,32]{3,2,1,0:T(8,128)S(1)}, f32[3,25,32,32]{3,2,1,0:T(8,128)S(1)}, u32[]{:S(2)}, u32[]{:S(2)}) %collective-permute-start) | collective-permute-done | bytes 307232 | tf_op jit(solution)/shard_map/ppermute | solution.py:22
  234.0 8.0 %collective-permute-done.1 = f32[3,25,32,32]{3,2,1,0:T(8,128)S(1)} collective-permute-done((f32[3,25,32,32]{3,2,1,0:T(8,128)S(1)}, f32[3,25,32,32]{3,2,1,0:T(8,128)S(1)}, u32[]{:S(2)}, u32[]{:S(2)}) %collective-permute-start.1) | collective-permute-done | bytes 307232 | tf_op jit(solution)/shard_map/ppermute | solution.py:22
  (513 shorter events, 128.1 us)
Async XLA Ops:
  24.9 19.4 %copy-start.110 = (s32[1,1024]{1,0:T(1,128)S(1)}, s32[1,1024]{1,0:T(1,128)}, u32[]{:S(2)}) copy-start(s32[1,1024]{1,0:T(1,128)} %copy-done.109) | copy-start | bytes 12292
  24.9 20.7 %copy-start.107 = (s32[1,1024]{1,0:T(1,128)S(1)}, s32[1,1024]{1,0:T(1,128)}, u32[]{:S(2)}) copy-start(s32[1,1024]{1,0:T(1,128)} %get-tuple-element.132) | copy-start | bytes 12292
  28.5 17.7 %copy-start.7 = (f32[3,5,1024]{2,1,0:T(8,128)S(1)}, f32[3,5,1024]{2,1,0:T(8,128)}, u32[]{:S(2)}) copy-start(f32[3,5,1024]{2,1,0:T(8,128)} %copy-done.6) | copy-start | bytes 184324
  28.5 18.4 %copy-start.33 = (f32[3,5,1024]{2,1,0:T(8,128)S(1)}, f32[3,5,1024]{2,1,0:T(8,128)}, u32[]{:S(2)}) copy-start(f32[3,5,1024]{2,1,0:T(8,128)} %copy-done.32) | copy-start | bytes 184324
  28.5 19.0 %copy-start.35 = (f32[3,5,1024]{2,1,0:T(8,128)S(1)}, f32[3,5,1024]{2,1,0:T(8,128)}, u32[]{:S(2)}) copy-start(f32[3,5,1024]{2,1,0:T(8,128)} %copy-done.34) | copy-start | bytes 184324
  28.5 19.6 %copy-start.29 = (f32[3,5,1024]{2,1,0:T(8,128)S(1)}, f32[3,5,1024]{2,1,0:T(8,128)}, u32[]{:S(2)}) copy-start(f32[3,5,1024]{2,1,0:T(8,128)} %copy-done.28) | copy-start | bytes 184324
  28.5 20.3 %copy-start.31 = (f32[3,5,1024]{2,1,0:T(8,128)S(1)}, f32[3,5,1024]{2,1,0:T(8,128)}, u32[]{:S(2)}) copy-start(f32[3,5,1024]{2,1,0:T(8,128)} %copy-done.30) | copy-start | bytes 184324
  28.5 20.9 %copy-start.106 = (s32[1,1024]{1,0:T(1,128)S(1)}, s32[1,1024]{1,0:T(1,128)}, u32[]{:S(2)}) copy-start(s32[1,1024]{1,0:T(1,128)} %get-tuple-element.126) | copy-start | bytes 12292
  28.5 20.9 %copy-start.104 = (s32[1,1024]{1,0:T(1,128)S(1)}, s32[1,1024]{1,0:T(1,128)}, u32[]{:S(2)}) copy-start(s32[1,1024]{1,0:T(1,128)} %copy-done.103) | copy-start | bytes 12292
  28.5 20.9 %copy-start.116 = (s32[1,1024]{1,0:T(1,128)S(1)}, s32[1,1024]{1,0:T(1,128)}, u32[]{:S(2)}) copy-start(s32[1,1024]{1,0:T(1,128)} %copy-done.115) | copy-start | bytes 12292
  28.6 21.5 %copy-start.105 = (s32[1,1024]{1,0:T(1,128)S(1)}, s32[1,1024]{1,0:T(1,128)}, u32[]{:S(2)}) copy-start(s32[1,1024]{1,0:T(1,128)} %get-tuple-element.128) | copy-start | bytes 12292
  28.6 21.5 %copy-start.102 = (s32[1,1024]{1,0:T(1,128)S(1)}, s32[1,1024]{1,0:T(1,128)}, u32[]{:S(2)}) copy-start(s32[1,1024]{1,0:T(1,128)} %copy-done.101) | copy-start | bytes 12292
  28.6 21.5 %copy-start.114 = (s32[1,1024]{1,0:T(1,128)S(1)}, s32[1,1024]{1,0:T(1,128)}, u32[]{:S(2)}) copy-start(s32[1,1024]{1,0:T(1,128)} %copy-done.113) | copy-start | bytes 12292
  28.6 50.4 %all-to-all-start = ((f32[128,1,1120]{2,1,0:T(1,128)}), f32[128,1,1120]{2,1,0:T(1,128)S(1)}, u32[]{:S(2)}, u32[]{:S(2)}) async-start(f32[128,1,1120]{2,1,0:T(1,128)} %reshape.450), calls=%async_computation | async-start | bytes 1179648 | tf_op jit(solution)/shard_map/all_to_all | solution.py:161
  50.1 19.2 %copy-start.95 = (s32[1024]{0:T(1024)}, s32[1024]{0:T(1024)S(1)}, u32[]{:S(2)}) copy-start(s32[1024]{0:T(1024)S(1)} %fusion.154) | copy-start | bytes 12292
  53.5 21.3 %copy-start.20 = (f32[3,5,1024]{2,1,0:T(8,128)}, f32[3,5,1024]{2,1,0:T(8,128)S(1)}, u32[]{:S(2)}) copy-start(f32[3,5,1024]{2,1,0:T(8,128)S(1)} %slice.697) | copy-start | bytes 184324
  53.5 21.9 %copy-start.18 = (f32[3,5,1024]{2,1,0:T(8,128)}, f32[3,5,1024]{2,1,0:T(8,128)S(1)}, u32[]{:S(2)}) copy-start(f32[3,5,1024]{2,1,0:T(8,128)S(1)} %slice.704) | copy-start | bytes 184324
  136.9 34.9 %copy-start.2 = (f32[3,25,1024]{2,1,0:T(8,128)}, f32[3,25,1024]{2,1,0:T(8,128)S(1)}, u32[]{:S(2)}) copy-start(f32[3,25,1024]{2,1,0:T(8,128)S(1)} %get-tuple-element.20) | copy-start | bytes 921604
  143.4 29.1 %all-to-all-start.1 = ((f32[128,1,480]{2,1,0:T(1,128)}), f32[128,1,480]{2,1,0:T(1,128)S(1)}, u32[]{:S(2)}, u32[]{:S(2)}) async-start(f32[128,1,480]{2,1,0:T(1,128)} %reshape.452), calls=%async_computation.1 | async-start | bytes 524288 | tf_op jit(solution)/shard_map/all_to_all | solution.py:163
  177.1 17.4 %copy-start.132 = (pred[1024]{0:T(1024)(128)(4,1)S(1)}, pred[1024]{0:T(1024)(128)(4,1)}, u32[]{:S(2)}) copy-start(pred[1024]{0:T(1024)(128)(4,1)} %compare_and_fusion.6) | copy-start | bytes 3076
  177.1 19.7 %copy-start.133 = (pred[1024]{0:T(1024)(128)(4,1)S(1)}, pred[1024]{0:T(1024)(128)(4,1)}, u32[]{:S(2)}) copy-start(pred[1024]{0:T(1024)(128)(4,1)} %compare_and_fusion.4) | copy-start | bytes 3076
  177.1 19.7 %copy-start.135 = (pred[1024]{0:T(1024)(128)(4,1)S(1)}, pred[1024]{0:T(1024)(128)(4,1)}, u32[]{:S(2)}) copy-start(pred[1024]{0:T(1024)(128)(4,1)} %compare_and_fusion.5) | copy-start | bytes 3076
  212.1 21.9 %collective-permute-start = (f32[3,25,32,32]{3,2,1,0:T(8,128)S(1)}, f32[3,25,32,32]{3,2,1,0:T(8,128)S(1)}, u32[]{:S(2)}, u32[]{:S(2)}) collective-permute-start(f32[3,25,32,32]{3,2,1,0:T(8,128)S(1)} %reshape.256), channel_id=1, source_target_pairs={{1,0},{2,1},{3,2},{4,3},{5,4},{6,5},{7,6},{8,7},{9,8},{10,9},{11,1... | collective-permute-start | bytes 921608 | tf_op jit(solution)/shard_map/ppermute | solution.py:22
  219.8 22.3 %collective-permute-start.1 = (f32[3,25,32,32]{3,2,1,0:T(8,128)S(1)}, f32[3,25,32,32]{3,2,1,0:T(8,128)S(1)}, u32[]{:S(2)}, u32[]{:S(2)}) collective-permute-start(f32[3,25,32,32]{3,2,1,0:T(8,128)S(1)} %reshape.256), channel_id=1, source_target_pairs={{0,1},{1,2},{2,3},{3,4},{4,5},{5,6},{6,7},{7,8},{8,9},{9,10},{10,1... | collective-permute-start | bytes 921608 | tf_op jit(solution)/shard_map/ppermute | solution.py:22
  (125 other events, 898.1 us)
where the time goes:
time: 246 us; the launch traced here: 244 us
  local copies, waits for them, and re-layouts  111 us (45%)
  other arithmetic  50.8 us (21%)
  starting transfers between devices  29.8 us (12%)
  matrix products  29 us (12%)
  waiting for transfers between devices  20.3 us (8%)
  between operations  2.66 us (1%)
    gather x16, local copies, waits for them, and re-layouts, assemble(): near_remote = jnp.take(flat_rows, remote_index, axis=1)  44.3 us
    gather x16, local copies, waits for them, and re-layouts, assemble(): near_local = jnp.take(own_faces[face_index ^ 1], local_index, axis=1)  29.1 us
    dot_general x36, matrix products, product_of(): jnp.dot(matrix, field, preferred_element_type=jnp.float32, precision=HIGH...  22.6 us
    ppermute x2, waiting for transfers between devices, passed_along(): return lax.ppermute(shard, axis, pairs)  20.3 us
    all_to_all x2, starting transfers between devices, deliver(): lax.all_to_all(outgoing, 'curve', split_axis=1, concat_axis=1, tiled=True)  20.3 us
    unnamed x296, local copies, waits for them, and re-layouts  12.9 us
    ppermute x2, starting transfers between devices, passed_along(): return lax.ppermute(shard, axis, pairs)  9.55 us
    another operation x11, other arithmetic, surface_term(): jnp.stack([wave_speed * trace_jump[0] - jump_normal, wave_speed * trace_j...  7.5 us
  transfers between devices with their start and end apart: 4, of which 2 were waited for; matrix products, arithmetic and copies ran while one was open for 24% of the time, Pallas kernels for 0%

commit v1 on v0

v1 whole, which is shorter than its diff:
```python
import math

import jax
import jax.numpy as jnp
import numpy as np
from jax import lax
from jax.experimental import pallas as pl
from jax.experimental.pallas import tpu as pltpu
from jax.sharding import PartitionSpec as P

F32 = jnp.float32
FACES = ((0, 5, 10, 15, 20), (4, 9, 14, 19, 24), (0, 1, 2, 3, 4), (20, 21, 22, 23, 24))
EDGE = tuple(sorted({n for face in FACES for n in face}))
PLACE = {n: i for i, n in enumerate(EDGE)}
LIFT = 0.06 * 10.0 * 0.5
HALF = [0.5 ** (k + 1) / math.factorial(k + 1) for k in range(4)]
WHOLE = [1.0 / math.factorial(k + 1) for k in range(4)]
AT_DEPTH, AT_FLAG, AT_X, AT_X2, AT_Y, AT_Y2, PLANES = 75, 100, 104, 120, 136, 152, 168
IN_FACE, IN_SECOND, IN_SIDE, IN_ALL = 104, 120, 136, 152
VALUES = [i for i in range(IN_ALL) if i < 101 or (i >= 104 and (i - 104) % 16 < 15)]


def derivative_matrix():
    points = np.array([-1.0, -np.sqrt(3.0 / 7.0), 0.0, np.sqrt(3.0 / 7.0), 1.0])
    gaps = points[:, None] - points[None, :] + np.eye(5)
    weights = 1.0 / gaps.prod(axis=1)
    matrix = weights[None, :] / weights[:, None] / gaps
    matrix -= np.diag(np.diag(matrix))
    return matrix - np.diag(matrix.sum(axis=1))


STEP = -0.06 * derivative_matrix()


def slope(f):
    even_a, even_b, odd_a, odd_b = f[0] + f[4], f[1] + f[3], f[0] - f[4], f[1] - f[3]
    twice = f[2] + f[2]
    even_a, even_b = even_a - twice, even_b - twice
    out = [None] * 5
    for i in (0, 1):
        minus = float(STEP[i, 0] + STEP[i, 4]) * 0.5 * even_a + float(STEP[i, 1] + STEP[i, 3]) * 0.5 * even_b
        plus = float(STEP[i, 0] - STEP[i, 4]) * 0.5 * odd_a + float(STEP[i, 1] - STEP[i, 3]) * 0.5 * odd_b
        out[i], out[4 - i] = plus + minus, plus - minus
    out[2] = float(STEP[2, 0]) * odd_a + float(STEP[2, 1]) * odd_b
    return out


def operate(src, dst, depth):
    spread = [None] * 25
    for j in range(5):
        line = [5 * j + i for i in range(5)]
        grad = slope([src[n] for n in line])
        part = slope([src[25 + n] for n in line])
        for i, n in enumerate(line):
            dst[25 + n] = depth(n) * grad[i]
            dst[n] = part[i]
    for i in range(5):
        line = [5 * j + i for j in range(5)]
        grad = slope([src[n] for n in line])
        part = slope([src[50 + n] for n in line])
        for j, n in enumerate(line):
            dst[50 + n] = depth(n) * grad[j]
            dst[n] = dst[n] + part[j]


def weighted(values, weights):
    total = weights[0] * values[0]
    for value, weight in zip(values[1:], weights[1:]):
        total = total + weight * value
    return total


def lanes(x, by):
    return x if by % 128 == 0 else pltpu.roll(x, by % 128, 1)


def subs(x, by):
    return pltpu.roll(x, by % 8, 0)


class Grid:
    def __init__(self):
        self.lane = lax.broadcasted_iota(jnp.int32, (8, 128), 1)
        self.sub = lax.broadcasted_iota(jnp.int32, (8, 128), 0)
        self.col = self.lane % 32
        self.west = self.col < 16
        self.south = self.sub < 4

    def across(self, x, face):
        if face == 0:
            return lanes(x, 1)
        if face == 1:
            return lanes(x, -1)
        if face == 2:
            y = lanes(x, 32)
            return jnp.where(self.lane < 32, subs(y, 1), y)
        y = lanes(x, -32)
        return jnp.where(self.lane >= 96, subs(y, -1), y)


def spread_ints(ref, out):
    for j in range(8):
        out[:, j, :] = ref[:, 128 * j : 128 * j + 128]


def face_facts(near, owner):
    me = lax.axis_index("curve")
    odd = me % 2
    chip = me + 1 - 2 * odd
    swap = me - 1 + 2 * odd
    walls, remotes, slots = [], [], []
    for f in range(4):
        wall = near[f] < 0
        remote = (near[f] >= 0) & (owner[f] != me)
        peer = jnp.max(jnp.where(remote, owner[f], -1).astype(F32)).astype(jnp.int32)
        walls.append(wall)
        remotes.append(remote)
        slot = jnp.where(peer == chip, 0, jnp.where(peer == swap, 1, 2))
        slots.append(jnp.where(peer < 0, 3, slot))
    return walls, remotes, slots


def flux(js, jn, jt, speed, depth, sign):
    lifted = LIFT * speed
    turn = LIFT * sign
    return lifted * js - turn * jn, lifted * jn - depth * (turn * js), lifted * jt


def first_kernel(sea, dep, near_in, owner_in, cl, ex, eo, es, dg, ps, cb, tr1, tr2, nf, cc, u, near, owner):
    grid = Grid()
    lane, sub, col = grid.lane, grid.sub, grid.col
    spread_ints(near_in, near)
    spread_ints(owner_in, owner)
    walls, remotes, slots = face_facts(near, owner)
    inner = [~(walls[f] | remotes[f]) for f in range(4)]
    u[0] = sea[...].reshape(75, 8, 128)
    ps[8 * AT_DEPTH : 8 * AT_FLAG, :] = dep[...].reshape(25, 8, 128).reshape(200, 128)

    def put(p, value):
        ps[8 * p : 8 * p + 8, :] = value

    def get(p):
        return ps[8 * p : 8 * p + 8, :]

    def depth(n):
        return get(AT_DEPTH + n)

    for k in range(4):
        operate(u.at[k], u.at[k + 1], depth)
    for v in range(3):
        for n in range(25):
            terms = [u[k, 25 * v + n] for k in range(5)]
            put(25 * v + n, terms[0] + weighted(terms[1:], HALF))
            cb[25 * v + n] = terms[0] + weighted(terms[1:], WHOLE)
            if n in PLACE:
                first = weighted(terms[:4], HALF)
                tr1[16 * v + PLACE[n]] = first
                tr2[16 * v + PLACE[n]] = weighted(terms[:4], WHOLE) - first
    for f in range(4):
        sign = -1.0 if f % 2 == 0 else 1.0
        normal, tangent = (1, 2) if f < 2 else (2, 1)
        echo = jnp.where(walls[f], -2.0, 0.0)
        for k in range(5):
            n, opposite = FACES[f][k], FACES[f ^ 1][k]
            a = [tr1[16 * v + PLACE[n]] for v in range(3)]
            b = [grid.across(tr1[16 * v + PLACE[opposite]], f) for v in range(3)]
            for v in range(3):
                nf[15 * f + 5 * v + k] = b[v]
            own = depth(n)
            other = jnp.where(inner[f], grid.across(depth(opposite), f), own)
            speed = jnp.sqrt(jnp.maximum(own, other))
            cc[5 * f + k] = speed
            js = jnp.where(inner[f], b[0] - a[0], 0.0)
            jn = jnp.where(inner[f], b[normal] - a[normal], echo * a[normal])
            jt = jnp.where(inner[f], b[tangent] - a[tangent], 0.0)
            out = flux(js, jn, jt, speed, own, sign)
            for v, part in ((0, out[0]), (normal, out[1]), (tangent, out[2])):
                put(25 * v + n, get(25 * v + n) + part)
    put(AT_FLAG, jnp.where(cl[...] == 0, 1.0, 0.0))
    for v in range(3):
        for k in range(5):
            i = 5 * v + k
            for src, x, y in ((tr1, AT_X, AT_Y), (tr2, AT_X2, AT_Y2)):
                at = [src[16 * v + PLACE[FACES[f][k]]] for f in range(4)]
                put(x + i, jnp.where(grid.west, at[0], at[1]))
                put(y + i, jnp.where(grid.south, at[2], at[3]))
    blank = jnp.zeros((8, 128), F32)
    west, east, south, north = ([blank] * 5 for _ in range(4))
    for i in VALUES:
        a, by = divmod(i, 32)
        turned = lanes(get(i), by)
        west[a] = jnp.where(col == by, turned, west[a])
        east[a] = jnp.where(col == (31 + by) % 32, turned, east[a])
    east = [lanes(x, -31) for x in east]
    for group in range(IN_ALL // 8):
        a, g = divmod(group, 4)
        base = group
        if group >= 13:
            base = {13: 17, 14: 18, 15: 19, 16: 20, 17: 13, 18: 14}[group]
        here = lane // 32 == g
        low = ps[pl.ds(64 * base, 8, stride=8), :]
        high = ps[pl.ds(64 * base + 7, 8, stride=8), :]
        south[a] = jnp.where(here, lanes(low, 32 * g), south[a])
        north[a] = jnp.where(here, lanes(high, 32 * g + 32), north[a])
    for slot, out in enumerate((ex, eo, es)):
        for a in range(5):
            out[a] = jnp.where(
                slots[0] == slot,
                west[a],
                jnp.where(slots[1] == slot, east[a], jnp.where(slots[2] == slot, south[a], north[a])),
            )
    corner = ((col == 0) | (col == 31)) & (((sub == 0) & (lane < 32)) | ((sub == 7) & (lane >= 96)))
    for which, at, low, high, mask in ((0, AT_Y, 2, 3, grid.south), (1, AT_X, 0, 1, grid.west)):
        total = blank
        for i in range(20):
            value = get(at + i) if i < 15 else jnp.where(mask, depth(FACES[low][i - 15]), depth(FACES[high][i - 15]))
            total = total + lanes(jnp.where(corner, value, 0.0), i)
        dg[which] = total


def second_kernel(
    rx, ro, rs, dx, do, ps, cb, tr1, tr2, nf, cc, near_in, owner_in, upd, se, so, hs, m, g, late, near, owner
):
    grid = Grid()
    lane, sub, col = grid.lane, grid.sub, grid.col
    spread_ints(near_in, near)
    spread_ints(owner_in, owner)
    walls, remotes, slots = face_facts(near, owner)

    def get(p):
        return ps[8 * p : 8 * p + 8, :]

    def depth(n):
        return get(AT_DEPTH + n)

    def halo(p):
        return hs[8 * p : 8 * p + 8, :]

    def halo_depth(n):
        return halo(AT_DEPTH + n)

    is_w, is_e = col == 0, col == 16
    is_x = is_w | is_e
    is_s, is_n = (sub == 0) & ~is_x, (sub == 7) & ~is_x

    def place(x, base):
        return jnp.where(lane < 16, lanes(x, 1 + base), jnp.where(lane < 32, lanes(x, 2 + base), lanes(x, 3 + base)))

    def to_halo(x, y):
        x = jnp.where(is_w, x, lanes(x, -15))
        y = place(jnp.where(sub == 7, lanes(y, 32), y), 0)
        return jnp.where(is_x, x, y)

    def from_halo(v):
        x = jnp.where(is_w, v, lanes(v, 15))
        y = jnp.where(lane < 15, lanes(v, -1), jnp.where(lane < 30, lanes(v, -2), lanes(v, -3)))
        return x, jnp.where(sub == 7, lanes(y, 96), y)

    def facing(at):
        return lambda k: jnp.where(
            is_w, at(FACES[1][k]), jnp.where(is_e, at(FACES[0][k]), jnp.where(is_s, at(FACES[3][k]), at(FACES[2][k])))
        )

    got = [
        [jnp.where(slots[f] == 0, rx[a], jnp.where(slots[f] == 1, ro[a], rs[a])) for a in range(5)] for f in range(4)
    ]
    for group in range(IN_ALL // 8):
        a, q = divmod(group, 4)
        hs[pl.ds(64 * group, 8, stride=8), :] = place(got[2][a], -32 * q)
        hs[pl.ds(64 * group + 7, 8, stride=8), :] = place(got[3][a], -32 * q)
    mixed = []
    for a in range(5):
        mixed.append(jnp.where(grid.west, got[0][a], lanes(got[1][a], 16)))
        mixed.append(jnp.where(grid.west, lanes(got[0][a], -16), got[1][a]))
    for i in VALUES:
        a, by = divmod(i, 16)
        hs[8 * i : 8 * i + 8, :] = jnp.where(is_x, lanes(mixed[a], -by), halo(i))

    for i in range(75):
        g[0, i] = halo(i)

    def raise_at(node, mask, parts):
        for v in range(3):
            g[0, 25 * v + node] = g[0, 25 * v + node] + jnp.where(mask, parts[v], 0.0)

    def jump_parts(a, b, along_x, speed, own, sign):
        j = [b[v] - a[v] for v in range(3)]
        cs, cn, ct = flux(
            j[0], jnp.where(along_x, j[1], j[2]), jnp.where(along_x, j[2], j[1]), speed, own, sign
        )
        return cs, jnp.where(along_x, cn, ct), jnp.where(along_x, ct, cn)

    inward = jnp.where(is_w | is_s, 1.0, -1.0)
    speeds = []
    for k in range(5):
        a = [halo(IN_FACE + 5 * v + k) for v in range(3)]
        b = [to_halo(get(AT_X + 5 * v + k), get(AT_Y + 5 * v + k)) for v in range(3)]
        own = facing(halo_depth)(k)
        other = to_halo(
            jnp.where(grid.west, depth(FACES[0][k]), depth(FACES[1][k])),
            jnp.where(grid.south, depth(FACES[2][k]), depth(FACES[3][k])),
        )
        speed = jnp.sqrt(jnp.maximum(own, other))
        speeds.append(speed)
        parts = jump_parts(a, b, is_x, speed, own, inward)
        for mask, face in ((is_w, 1), (is_e, 0), (is_s, 3), (is_n, 2)):
            raise_at(FACES[face][k], mask, parts)

    def diagonal(f, h, which):
        slot = jnp.where(slots[f] == 2, slots[h], slots[f])
        return jnp.where(slot == 0, dx[which], do[which])

    there = [[(slots[f] < 3) & (slots[h] < 3) for h in (2, 3)] for f in (0, 1)]

    def shifted(x, by, down):
        return subs(lanes(x, by), down)

    low = sub == 0
    side_w = jnp.where(low, shifted(diagonal(0, 2, 0), 1, 1), shifted(diagonal(0, 3, 0), 65, -1))
    side_e = jnp.where(low, shifted(diagonal(1, 2, 0), 48, 1), shifted(diagonal(1, 3, 0), 112, -1))
    side_y = jnp.where(
        lane < 30,
        jnp.where(low, shifted(diagonal(0, 2, 1), 2, 1), shifted(diagonal(0, 3, 1), 98, -1)),
        jnp.where(low, shifted(diagonal(1, 2, 1), 66, 1), shifted(diagonal(1, 3, 1), 34, -1)),
    )

    def beyond(i):
        return jnp.where(is_w, lanes(side_w, -i), jnp.where(is_e, lanes(side_e, -i), lanes(side_y, -i)))

    low, high = sub == 0, sub == 7
    at_s = low & (((lane == 0) & there[0][0]) | ((lane == 16) & there[1][0]))
    at_n = high & (((lane == 96) & there[0][1]) | ((lane == 112) & there[1][1]))
    at_w = (lane == 1) & ((low & there[0][0]) | (high & there[0][1]))
    at_e = (lane == 34) & ((low & there[1][0]) | (high & there[1][1]))
    outward = jnp.where(at_n | at_e, 1.0, -1.0)
    for k in range(5):
        a = [halo(IN_SIDE + 5 * v + k) for v in range(3)]
        b = [beyond(5 * v + k) for v in range(3)]
        own = jnp.where(
            at_s,
            halo_depth(FACES[2][k]),
            jnp.where(at_n, halo_depth(FACES[3][k]), jnp.where(at_w, halo_depth(FACES[0][k]), halo_depth(FACES[1][k]))),
        )
        speed = jnp.sqrt(jnp.maximum(own, beyond(15 + k)))
        parts = jump_parts(a, b, ~is_x, speed, own, outward)
        for mask, face in ((at_w, 0), (at_e, 1), (at_s, 2), (at_n, 3)):
            raise_at(FACES[face][k], mask, parts)

    for i in range(75):
        m[0, i] = get(i)
    for k in range(5):
        speed_x, speed_y = from_halo(speeds[k])
        sent = [from_halo(halo(IN_FACE + 5 * v + k)) for v in range(3)]
        for axis, speed, at in ((0, speed_x, AT_X), (1, speed_y, AT_Y)):
            first, last = 2 * axis, 2 * axis + 1
            side = grid.south if axis else grid.west
            normal, tangent = (2, 1) if axis else (1, 2)
            j = [sent[v][axis] - get(at + 5 * v + k) for v in range(3)]
            own = jnp.where(side, depth(FACES[first][k]), depth(FACES[last][k]))
            out = flux(j[0], j[normal], j[tangent], speed, own, jnp.where(side, -1.0, 1.0))
            for f in (first, last):
                n = FACES[f][k]
                for v, part in ((0, out[0]), (normal, out[1]), (tangent, out[2])):
                    m[0, 25 * v + n] = m[0, 25 * v + n] + jnp.where(remotes[f], part, 0.0)

    for k in range(4):
        operate(m.at[k], m.at[k + 1], depth)
    for k in range(3):
        operate(g.at[k], g.at[k + 1], halo_depth)
    fine = get(AT_FLAG) > 0.5
    halo_fine = halo(AT_FLAG) > 0.5
    halo_late = []
    for v in range(3):
        for k in range(5):
            value = facing(lambda n: weighted([g[q, 25 * v + n] for q in range(4)], HALF))(k)
            halo_late.append(from_halo(jnp.where(halo_fine, value, halo(IN_SECOND + 5 * v + k))))
    for v in range(3):
        for n in range(25):
            terms = [m[k, 25 * v + n] for k in range(5)]
            upd[25 * v + n] = jnp.where(fine, terms[0] + weighted(terms[1:], HALF), cb[25 * v + n])
            if n in PLACE:
                late[16 * v + PLACE[n]] = weighted(terms[:4], HALF)
    for f in range(4):
        sign = -1.0 if f % 2 == 0 else 1.0
        axis = f // 2
        normal, tangent = (2, 1) if axis else (1, 2)
        for k in range(5):
            n, opposite = FACES[f][k], FACES[f ^ 1][k]
            speed_out = from_halo(speeds[k])[axis]
            speed = jnp.where(remotes[f], speed_out, cc[5 * f + k])
            j, a_list = [], []
            for v in range(3):
                at, across = 16 * v + PLACE[n], 16 * v + PLACE[opposite]
                a = jnp.where(fine, late[at], tr1[at] + tr2[at])
                sent = grid.across(jnp.where(fine, late[across], tr2[across]), f)
                sent = jnp.where(remotes[f], halo_late[5 * v + k][axis], sent)
                before = jnp.where(remotes[f], from_halo(halo(IN_FACE + 5 * v + k))[axis], nf[15 * f + 5 * v + k])
                b = jnp.where(fine, sent, before + sent)
                a_list.append(a)
                j.append(b - a)
            js = jnp.where(walls[f], 0.0, j[0])
            jn = jnp.where(walls[f], -2.0 * a_list[normal], j[normal])
            jt = jnp.where(walls[f], 0.0, j[tangent])
            out = flux(js, jn, jt, speed, depth(n), sign)
            for v, part in ((0, out[0]), (normal, out[1]), (tangent, out[2])):
                upd[25 * v + n] = upd[25 * v + n] + part
    even = (lane // 32) % 2 == 0
    for p in range(38):
        one = upd[2 * p]
        two = upd[min(2 * p + 1, 74)]
        se[p] = jnp.where(even, one, lanes(two, 32))
        so[p] = jnp.where(even, lanes(two, -32), one)


def third_kernel(swap, re, ro, upd, out, buf):
    grid = Grid()
    group = grid.lane // 32
    even = group % 2 == 0
    row = grid.sub * 4 + group
    moves = jnp.zeros((8, 128), jnp.int32)
    for b in range(32):
        moves = jnp.where(row == b, swap[b], moves)
    moves = moves > 0
    for i in range(75):
        e, o = re[i // 2], ro[i // 2]
        if i % 2:
            e, o = lanes(e, -32), lanes(o, 32)
        buf[i] = jnp.where(moves, jnp.where(even, e, o), upd[i])
    out[...] = buf[...].reshape(3, 25, 1024)


VM = pl.BlockSpec(memory_space=pltpu.VMEM)
PARAMS = pltpu.CompilerParams(vmem_limit_bytes=40 * 1024 * 1024)


def planes(*counts):
    return [jax.ShapeDtypeStruct((c, 8, 128), F32) for c in counts]


def local(sea_state, water_depth, neighbours, neighbour_owner, clusters, block_swap):
    devices = lax.axis_size("curve")
    odd_swap = [(i, i + 1) for i in range(1, devices - 1, 2)] + [(i + 1, i) for i in range(1, devices - 1, 2)]
    chip_swap = [(i, i ^ 1) for i in range(devices)]
    far = devices // 2

    def passed(x, pairs):
        return lax.ppermute(x, "curve", pairs)

    ex, eo, es, dg, ps, cb, tr1, tr2, nf, cc = pl.pallas_call(
        first_kernel,
        out_shape=planes(5, 5, 5, 2) + [jax.ShapeDtypeStruct((8 * PLANES, 128), F32)] + planes(75, 48, 48, 60, 20),
        in_specs=[VM] * 5,
        out_specs=[VM] * 10,
        scratch_shapes=[pltpu.VMEM((5, 75, 8, 128), F32)] + [pltpu.VMEM((4, 8, 128), jnp.int32)] * 2,
        compiler_params=PARAMS,
        name="predict",
    )(sea_state, water_depth, neighbours, neighbour_owner, clusters.reshape(8, 128))
    ro = passed(eo, odd_swap)
    do = passed(dg, [(i, (j + far) % devices) for i, j in odd_swap])
    dx = passed(dg, [(i, (j + far) % devices) for i, j in chip_swap])
    rs = passed(es, [(i, (i + far) % devices) for i in range(devices)])
    rx = passed(ex, chip_swap)
    upd, se, so = pl.pallas_call(
        second_kernel,
        out_shape=planes(75, 38, 38),
        in_specs=[VM] * 13,
        out_specs=[VM] * 3,
        scratch_shapes=[
            pltpu.VMEM((8 * 160, 128), F32),
            pltpu.VMEM((5, 75, 8, 128), F32),
            pltpu.VMEM((4, 75, 8, 128), F32),
            pltpu.VMEM((48, 8, 128), F32),
        ]
        + [pltpu.VMEM((4, 8, 128), jnp.int32)] * 2,
        compiler_params=PARAMS,
        name="correct",
    )(rx, ro, rs, dx, do, ps, cb, tr1, tr2, nf, cc, neighbours, neighbour_owner)
    got_odd = passed(so, odd_swap)
    got_even = passed(se, chip_swap)
    return pl.pallas_call(
        third_kernel,
        out_shape=jax.ShapeDtypeStruct((3, 25, 1024), F32),
        in_specs=[pl.BlockSpec(memory_space=pltpu.SMEM)] + [VM] * 3,
        out_specs=VM,
        scratch_shapes=[pltpu.VMEM((75, 8, 128), F32)],
        compiler_params=PARAMS,
        name="migrate",
    )(block_swap, got_even, got_odd, upd)


def solution(mesh):
    return jax.shard_map(
        local,
        mesh=mesh,
        in_specs=(
            P(None, None, "curve"),
            P(None, "curve"),
            P(None, "curve"),
            P(None, "curve"),
            P("curve"),
            P("curve"),
        ),
        out_specs=P(None, None, "curve"),
        check_vma=False,
    )
```

time: 246 us -> 45.3 us (0.18)
  local copies, waits for them, and re-layouts: 111 us -> 4.03 us
  other arithmetic: 50.8 us -> 0 us
  matrix products: 29 us -> 0 us
  starting transfers between devices: 29.8 us -> 17.8 us
  Pallas kernels: 0 us -> 9.56 us
  waiting for transfers between devices: 20.3 us -> 13.5 us
  between operations: 2.66 us -> 0.1 us
    gather x32 -> x0, local copies, waits for them, and re-layouts: 73.4 us -> none  [the longest x16 44.3 us: assemble(): near_remote = jnp.take(flat_rows, remote_index, axis=1)]
    dot_general x48 -> x0, matrix products: 29 us -> none  [the longest x36 22.6 us: product_of(): jnp.dot(matrix, field, preferred_element_type=jnp.float32, precision=HIGH...]
    all_to_all x2 -> x0, starting transfers between devices: 20.3 us -> none  [deliver(): lax.all_to_all(outgoing, 'curve', split_axis=1, concat_axis=1, tiled=True)]
    reshape x22 -> x0, local copies, waits for them, and re-layouts: 11.7 us -> none  [the longest x4 3.83 us: local(): near_first = [values[0:15].reshape(3, 5, slots) for values in near_one]]
    pallas_call x0 -> x3, Pallas kernels: none -> 9.56 us  [the longest x1 6.85 us: local(): pl.pallas_call(second_kernel, out_shape=planes(75, 38, 38), in_specs=[VM]...]
    unnamed x296 -> x12, local copies, waits for them, and re-layouts: 12.9 us -> 4.03 us
    ppermute x2 -> x7, starting transfers between devices: 9.55 us -> 17.8 us  [passed(): return lax.ppermute(x, 'curve', pairs)]
    another operation x11 -> x0, other arithmetic: 7.5 us -> none  [surface_term(): jnp.stack([wave_speed * trace_jump[0] - jump_normal, wave_speed * trace_j...]
  transfers between devices with their start and end apart: 4 -> 7, of which waited for: 2 -> 2; matrix products, arithmetic and copies ran while one was open for 24% -> 0% of each run, Pallas kernels for 0% -> 0%
where the time goes in v1:
time: 45.3 us; the launch traced here: 44.9 us
  starting transfers between devices  17.8 us (39%)
  waiting for transfers between devices  13.5 us (30%)
  Pallas kernels  9.56 us (21%)
  local copies, waits for them, and re-layouts  4.03 us (9%)
    ppermute x7, starting transfers between devices, passed(): return lax.ppermute(x, 'curve', pairs)  17.8 us
    ppermute x7, waiting for transfers between devices, passed(): return lax.ppermute(x, 'curve', pairs)  13.5 us
    pallas_call x1, Pallas kernels, local(): pl.pallas_call(second_kernel, out_shape=planes(75, 38, 38), in_specs=[VM]...  6.85 us
    unnamed x12, local copies, waits for them, and re-layouts  4.03 us
    pallas_call x1, Pallas kernels, local(): pl.pallas_call(third_kernel, out_shape=jax.ShapeDtypeStruct((3, 25, 1024)...  1.44 us
    pallas_call x1, Pallas kernels, local(): pl.pallas_call(first_kernel, out_shape=planes(5, 5, 5, 2) + [jax.ShapeDty...  1.26 us
  transfers between devices with their start and end apart: 7, of which 2 were waited for; matrix products, arithmetic and copies ran while one was open for 0% of the time, Pallas kernels for 0%

profile of v1, /device:TPU:6, one launch (start us, length us, event | category | flops | bytes accessed | tf_op | source)
XLA Modules:
  0.0 44.9 jit_solution(269159633221160011)
XLA Ops:
  0.0 1.0 %copy-done = f32[3,25,1024]{2,1,0:T(8,128)S(1)} copy-done((f32[3,25,1024]{2,1,0:T(8,128)S(1)}, f32[3,25,1024]{2,1,0:T(8,128)}, u32[]{:S(2)}) %copy-start) | copy-done | bytes 307224
  1.0 0.9 %copy-done.1 = f32[25,1024]{1,0:T(8,128)S(1)} copy-done((f32[25,1024]{1,0:T(8,128)S(1)}, f32[25,1024]{1,0:T(8,128)}, u32[]{:S(2)}) %copy-start.1) | copy-done | bytes 102424
  1.9 0.7 %copy-done.2 = s32[4,1024]{1,0:T(4,128)S(1)} copy-done((s32[4,1024]{1,0:T(4,128)S(1)}, s32[4,1024]{1,0:T(4,128)}, u32[]{:S(2)}) %copy-start.2) | copy-done | bytes 16408
  2.6 0.7 %copy-done.3 = s32[4,1024]{1,0:T(4,128)S(1)} copy-done((s32[4,1024]{1,0:T(4,128)S(1)}, s32[4,1024]{1,0:T(4,128)}, u32[]{:S(2)}) %copy-start.3) | copy-done | bytes 16408
  3.3 0.7 %copy-done.4 = s32[1024]{0:T(1024)S(1)} copy-done((s32[1024]{0:T(1024)S(1)}, s32[1024]{0:T(1024)}, u32[]{:S(2)}) %copy-start.4) | copy-done | bytes 4120
  4.0 1.3 %predict.1 = (f32[5,8,128]{2,1,0:T(8,128)S(1)}, f32[5,8,128]{2,1,0:T(8,128)S(1)}, f32[5,8,128]{2,1,0:T(8,128)S(1)}, f32[2,8,128]{2,1,0:T(8,128)S(1)}, f32[1344,1...) custom-call(f32[3,25,1024]{2,1,0:T(8,128)S(1)} %copy-done, ...), custom_call_target="tpu_custom_call" | custom-call | tf_op jit(solution)/shard_map/predict/pallas_call | solution.py:449
  5.3 0.1 collective-permute-start
  5.4 8.8 %collective-permute-start.1 = (f32[5,8,128]{2,1,0:T(8,128)S(1)}, f32[5,8,128]{2,1,0:T(8,128)S(1)}, u32[]{:S(2)}, u32[]{:S(2)}) collective-permute-start(f32[5,8,128]{2,1,0:T(8,128)S(1)} %get-tuple-element.19), channel_id=1, source_target_pairs={{1,2},{3,4},{5,6},{7,8},{9,10},{11,12},{13,14},{15,16},{17,18},{19... | collective-permute-start | bytes 61448 | tf_op jit(solution)/shard_map/ppermute | solution.py:447
  14.1 1.2 %collective-permute-start.2 = (f32[5,8,128]{2,1,0:T(8,128)S(1)}, f32[5,8,128]{2,1,0:T(8,128)S(1)}, u32[]{:S(2)}, u32[]{:S(2)}) collective-permute-start(f32[5,8,128]{2,1,0:T(8,128)S(1)} %get-tuple-element.20), channel_id=1, source_target_pairs={{0,64},{1,65},{2,66},{3,67},{4,68},{5,69},{6,70},{7,71},{8,72},{9,... | collective-permute-start | bytes 61448 | tf_op jit(solution)/shard_map/ppermute | solution.py:447
  15.3 3.2 %collective-permute-start.4 = (f32[2,8,128]{2,1,0:T(8,128)S(1)}, f32[2,8,128]{2,1,0:T(8,128)S(1)}, u32[]{:S(2)}, u32[]{:S(2)}) collective-permute-start(f32[2,8,128]{2,1,0:T(8,128)S(1)} %get-tuple-element.21), channel_id=1, source_target_pairs={{1,66},{3,68},{5,70},{7,72},{9,74},{11,76},{13,78},{15,80},{17,82}... | collective-permute-start | bytes 24584 | tf_op jit(solution)/shard_map/ppermute | solution.py:447
  18.5 0.1 collective-permute-start.3
  18.6 7.1 %collective-permute-done.4.do = f32[2,8,128]{2,1,0:T(8,128)S(1)} collective-permute-done((f32[2,8,128]{2,1,0:T(8,128)S(1)}, f32[2,8,128]{2,1,0:T(8,128)S(1)}, u32[]{:S(2)}, u32[]{:S(2)}) %collective-permute-start.4) | collective-permute-done | bytes 8224 | tf_op jit(solution)/shard_map/ppermute | solution.py:447
  25.7 0.0 collective-permute-done.3.dx
  25.7 0.0 collective-permute-done.rx
  25.7 0.0 collective-permute-done.1.ro
  25.7 0.0 collective-permute-done.2.rs
  25.8 6.9 %correct.1 = (f32[75,8,128]{2,1,0:T(8,128)S(1)}, f32[38,8,128]{2,1,0:T(8,128)S(1)}, f32[38,8,128]{2,1,0:T(8,128)S(1)}) custom-call(f32[5,8,128]{2,1,0:T(8,128)S(1)} %collective-permute-done.rx, f32[5,8,128]{2,1,0:T(8,128)S(1)} %collective-permute-done.1.ro, f32[5,8,128]{2,1,0:T(8,128)S(1)} %collective-permute-done.2.rs, ...), custom_call_target="tpu_custom_call" | custom-call | tf_op jit(solution)/shard_map/correct/pallas_call | solution.py:463
  32.6 0.1 collective-permute-start.5
  32.7 0.0 copy-start.5
  32.7 4.4 %collective-permute-start.6 = (f32[38,8,128]{2,1,0:T(8,128)S(1)}, f32[38,8,128]{2,1,0:T(8,128)S(1)}, u32[]{:S(2)}, u32[]{:S(2)}) collective-permute-start(f32[38,8,128]{2,1,0:T(8,128)S(1)} %get-tuple-element.29), channel_id=1, source_target_pairs={{1,2},{3,4},{5,6},{7,8},{9,10},{11,12},{13,14},{15,16},{17,18},{19... | collective-permute-start | bytes 466952 | tf_op jit(solution)/shard_map/ppermute | solution.py:447
  37.1 0.0 collective-permute-done.5.re
  37.1 6.4 %collective-permute-done.6.ro = f32[38,8,128]{2,1,0:T(8,128)S(1)} collective-permute-done((f32[38,8,128]{2,1,0:T(8,128)S(1)}, f32[38,8,128]{2,1,0:T(8,128)S(1)}, u32[]{:S(2)}, u32[]{:S(2)}) %collective-permute-start.6) | collective-permute-done | bytes 155680 | tf_op jit(solution)/shard_map/ppermute | solution.py:447
  43.5 0.0 copy-done.5
  43.5 1.4 %migrate.1 = f32[3,25,1024]{2,1,0:T(8,128)} custom-call(s32[32]{0:T(128)S(1)} %copy-done.5, f32[38,8,128]{2,1,0:T(8,128)S(1)} %collective-permute-done.5.re, f32[38,8,128]{2,1,0:T(8,128)S(1)} %collective-permute-done.6.ro, f32[75,8,128]{2,1,0:T(8,128)S(1)} %get-tuple-element.30.upd), custom_call_target="tpu_custom_call" | custom-call | tf_op jit(solution)/shard_map/migrate/pallas_call | solution.py:480
  (5 shorter events, 0.0 us)
Async XLA Ops:
  0.0 1.0 %copy-start = (f32[3,25,1024]{2,1,0:T(8,128)S(1)}, f32[3,25,1024]{2,1,0:T(8,128)}, u32[]{:S(2)}) copy-start(f32[3,25,1024]{2,1,0:T(8,128)} %sea.1) | copy-start | bytes 921604
  1.0 0.9 %copy-start.1 = (f32[25,1024]{1,0:T(8,128)S(1)}, f32[25,1024]{1,0:T(8,128)}, u32[]{:S(2)}) copy-start(f32[25,1024]{1,0:T(8,128)} %dep.1) | copy-start | bytes 307204
  1.9 0.7 %copy-start.2 = (s32[4,1024]{1,0:T(4,128)S(1)}, s32[4,1024]{1,0:T(4,128)}, u32[]{:S(2)}) copy-start(s32[4,1024]{1,0:T(4,128)} %near_in.3) | copy-start | bytes 49156
  2.6 0.7 %copy-start.3 = (s32[4,1024]{1,0:T(4,128)S(1)}, s32[4,1024]{1,0:T(4,128)}, u32[]{:S(2)}) copy-start(s32[4,1024]{1,0:T(4,128)} %owner_in.3) | copy-start | bytes 49156
  3.3 0.7 %copy-start.4 = (s32[1024]{0:T(1024)S(1)}, s32[1024]{0:T(1024)}, u32[]{:S(2)}) copy-start(s32[1024]{0:T(1024)} %param.10) | copy-start | bytes 12292
  5.3 20.4 %collective-permute-start = (f32[5,8,128]{2,1,0:T(8,128)S(1)}, f32[5,8,128]{2,1,0:T(8,128)S(1)}, u32[]{:S(2)}, u32[]{:S(2)}) collective-permute-start(f32[5,8,128]{2,1,0:T(8,128)S(1)} %get-tuple-element.18), channel_id=1, source_target_pairs={{0,1},{1,0},{2,3},{3,2},{4,5},{5,4},{6,7},{7,6},{8,9},{9,8},{10,11... | collective-permute-start | bytes 61448 | tf_op jit(solution)/shard_map/ppermute | solution.py:447
  5.4 20.3 %collective-permute-start.1 = (f32[5,8,128]{2,1,0:T(8,128)S(1)}, f32[5,8,128]{2,1,0:T(8,128)S(1)}, u32[]{:S(2)}, u32[]{:S(2)}) collective-permute-start(f32[5,8,128]{2,1,0:T(8,128)S(1)} %get-tuple-element.19), channel_id=1, source_target_pairs={{1,2},{3,4},{5,6},{7,8},{9,10},{11,12},{13,14},{15,16},{17,18},{19... | collective-permute-start | bytes 61448 | tf_op jit(solution)/shard_map/ppermute | solution.py:447
  14.1 11.6 %collective-permute-start.2 = (f32[5,8,128]{2,1,0:T(8,128)S(1)}, f32[5,8,128]{2,1,0:T(8,128)S(1)}, u32[]{:S(2)}, u32[]{:S(2)}) collective-permute-start(f32[5,8,128]{2,1,0:T(8,128)S(1)} %get-tuple-element.20), channel_id=1, source_target_pairs={{0,64},{1,65},{2,66},{3,67},{4,68},{5,69},{6,70},{7,71},{8,72},{9,... | collective-permute-start | bytes 61448 | tf_op jit(solution)/shard_map/ppermute | solution.py:447
  15.3 10.4 %collective-permute-start.4 = (f32[2,8,128]{2,1,0:T(8,128)S(1)}, f32[2,8,128]{2,1,0:T(8,128)S(1)}, u32[]{:S(2)}, u32[]{:S(2)}) collective-permute-start(f32[2,8,128]{2,1,0:T(8,128)S(1)} %get-tuple-element.21), channel_id=1, source_target_pairs={{1,66},{3,68},{5,70},{7,72},{9,74},{11,76},{13,78},{15,80},{17,82}... | collective-permute-start | bytes 24584 | tf_op jit(solution)/shard_map/ppermute | solution.py:447
  18.5 7.2 %collective-permute-start.3 = (f32[2,8,128]{2,1,0:T(8,128)S(1)}, f32[2,8,128]{2,1,0:T(8,128)S(1)}, u32[]{:S(2)}, u32[]{:S(2)}) collective-permute-start(f32[2,8,128]{2,1,0:T(8,128)S(1)} %get-tuple-element.21), channel_id=1, source_target_pairs={{0,65},{1,64},{2,67},{3,66},{4,69},{5,68},{6,71},{7,70},{8,73},{9,... | collective-permute-start | bytes 24584 | tf_op jit(solution)/shard_map/ppermute | solution.py:447
  32.6 4.5 %collective-permute-start.5 = (f32[38,8,128]{2,1,0:T(8,128)S(1)}, f32[38,8,128]{2,1,0:T(8,128)S(1)}, u32[]{:S(2)}, u32[]{:S(2)}) collective-permute-start(f32[38,8,128]{2,1,0:T(8,128)S(1)} %get-tuple-element.28), channel_id=1, source_target_pairs={{0,1},{1,0},{2,3},{3,2},{4,5},{5,4},{6,7},{7,6},{8,9},{9,8},{10,11... | collective-permute-start | bytes 466952 | tf_op jit(solution)/shard_map/ppermute | solution.py:447
  32.7 10.8 %copy-start.5 = (s32[32]{0:T(128)S(1)}, s32[32]{0:T(128)}, u32[]{:S(2)}) copy-start(s32[32]{0:T(128)} %swap.1) | copy-start | bytes 388
  32.7 10.8 %collective-permute-start.6 = (f32[38,8,128]{2,1,0:T(8,128)S(1)}, f32[38,8,128]{2,1,0:T(8,128)S(1)}, u32[]{:S(2)}, u32[]{:S(2)}) collective-permute-start(f32[38,8,128]{2,1,0:T(8,128)S(1)} %get-tuple-element.29), channel_id=1, source_target_pairs={{1,2},{3,4},{5,6},{7,8},{9,10},{11,12},{13,14},{15,16},{17,18},{19... | collective-permute-start | bytes 466952 | tf_op jit(solution)/shard_map/ppermute | solution.py:447

commit v2 on v1

--- a/solution.py
+++ b/solution.py
@@ -126,11 +126,21 @@
     return lifted * js - turn * jn, lifted * jn - depth * (turn * js), lifted * jt
 
 
-def first_kernel(sea, dep, near_in, owner_in, cl, ex, eo, es, dg, ps, cb, tr1, tr2, nf, cc, u, near, owner):
+def first_kernel(
+    sea_in, dep_in, near_in, owner_in, cl_in, ex, eo, es, ps, cb, tr1, tr2, nf, cc, near, owner, u, sea, dep, nb, ow, cl, sems
+):
+    copies = [
+        pltpu.make_async_copy(src, dst, sems.at[i])
+        for i, (src, dst) in enumerate(((sea_in, sea), (dep_in, dep), (near_in, nb), (owner_in, ow), (cl_in, cl)))
+    ]
+    for copy in copies:
+        copy.start()
     grid = Grid()
     lane, sub, col = grid.lane, grid.sub, grid.col
-    spread_ints(near_in, near)
-    spread_ints(owner_in, owner)
+    for copy in copies:
+        copy.wait()
+    spread_ints(nb, near)
+    spread_ints(ow, owner)
     walls, remotes, slots = face_facts(near, owner)
     inner = [~(walls[f] | remotes[f]) for f in range(4)]
     u[0] = sea[...].reshape(75, 8, 128)
@@ -188,6 +198,7 @@
     west, east, south, north = ([blank] * 5 for _ in range(4))
     for i in VALUES:
         a, by = divmod(i, 32)
+        by = 2 * by if by < 16 else 2 * by - 31
         turned = lanes(get(i), by)
         west[a] = jnp.where(col == by, turned, west[a])
         east[a] = jnp.where(col == (31 + by) % 32, turned, east[a])
@@ -215,16 +226,14 @@
         for i in range(20):
             value = get(at + i) if i < 15 else jnp.where(mask, depth(FACES[low][i - 15]), depth(FACES[high][i - 15]))
             total = total + lanes(jnp.where(corner, value, 0.0), i)
-        dg[which] = total
+        es[5 + which] = total
 
 
 def second_kernel(
-    rx, ro, rs, dx, do, ps, cb, tr1, tr2, nf, cc, near_in, owner_in, upd, se, so, hs, m, g, late, near, owner
+    rx, ro, rs, ps, cb, tr1, tr2, nf, cc, near, owner, upd, se, so, hx, hy, m, gx, gy, late, before, after, fast
 ):
     grid = Grid()
-    lane, sub, col = grid.lane, grid.sub, grid.col
-    spread_ints(near_in, near)
-    spread_ints(owner_in, owner)
+    lane, sub = grid.lane, grid.sub
     walls, remotes, slots = face_facts(near, owner)
 
     def get(p):
@@ -232,148 +241,113 @@
 
     def depth(n):
         return get(AT_DEPTH + n)
-
-    def halo(p):
-        return hs[8 * p : 8 * p + 8, :]
-
-    def halo_depth(n):
-        return halo(AT_DEPTH + n)
-
-    is_w, is_e = col == 0, col == 16
-    is_x = is_w | is_e
-    is_s, is_n = (sub == 0) & ~is_x, (sub == 7) & ~is_x
-
-    def place(x, base):
-        return jnp.where(lane < 16, lanes(x, 1 + base), jnp.where(lane < 32, lanes(x, 2 + base), lanes(x, 3 + base)))
-
-    def to_halo(x, y):
-        x = jnp.where(is_w, x, lanes(x, -15))
-        y = place(jnp.where(sub == 7, lanes(y, 32), y), 0)
-        return jnp.where(is_x, x, y)
-
-    def from_halo(v):
-        x = jnp.where(is_w, v, lanes(v, 15))
-        y = jnp.where(lane < 15, lanes(v, -1), jnp.where(lane < 30, lanes(v, -2), lanes(v, -3)))
-        return x, jnp.where(sub == 7, lanes(y, 96), y)
-
-    def facing(at):
-        return lambda k: jnp.where(
-            is_w, at(FACES[1][k]), jnp.where(is_e, at(FACES[0][k]), jnp.where(is_s, at(FACES[3][k]), at(FACES[2][k])))
-        )
 
     got = [
         [jnp.where(slots[f] == 0, rx[a], jnp.where(slots[f] == 1, ro[a], rs[a])) for a in range(5)] for f in range(4)
     ]
+    for a in range(5):
+        pair = (
+            jnp.where(lane % 2 == 0, got[0][a], lanes(got[1][a], 31)),
+            jnp.where(lane % 2 == 0, lanes(got[0][a], -1), lanes(got[1][a], 30)),
+        )
+        for i in VALUES:
+            if i // 32 == a:
+                hx[8 * i : 8 * i + 8, :] = lanes(pair[i % 32 // 16], -2 * (i % 16))
     for group in range(IN_ALL // 8):
         a, q = divmod(group, 4)
-        hs[pl.ds(64 * group, 8, stride=8), :] = place(got[2][a], -32 * q)
-        hs[pl.ds(64 * group + 7, 8, stride=8), :] = place(got[3][a], -32 * q)
-    mixed = []
-    for a in range(5):
-        mixed.append(jnp.where(grid.west, got[0][a], lanes(got[1][a], 16)))
-        mixed.append(jnp.where(grid.west, lanes(got[0][a], -16), got[1][a]))
-    for i in VALUES:
-        a, by = divmod(i, 16)
-        hs[8 * i : 8 * i + 8, :] = jnp.where(is_x, lanes(mixed[a], -by), halo(i))
-
-    for i in range(75):
-        g[0, i] = halo(i)
-
-    def raise_at(node, mask, parts):
-        for v in range(3):
-            g[0, 25 * v + node] = g[0, 25 * v + node] + jnp.where(mask, parts[v], 0.0)
-
-    def jump_parts(a, b, along_x, speed, own, sign):
-        j = [b[v] - a[v] for v in range(3)]
-        cs, cn, ct = flux(
-            j[0], jnp.where(along_x, j[1], j[2]), jnp.where(along_x, j[2], j[1]), speed, own, sign
-        )
-        return cs, jnp.where(along_x, cn, ct), jnp.where(along_x, ct, cn)
-
-    inward = jnp.where(is_w | is_s, 1.0, -1.0)
-    speeds = []
-    for k in range(5):
-        a = [halo(IN_FACE + 5 * v + k) for v in range(3)]
-        b = [to_halo(get(AT_X + 5 * v + k), get(AT_Y + 5 * v + k)) for v in range(3)]
-        own = facing(halo_depth)(k)
-        other = to_halo(
-            jnp.where(grid.west, depth(FACES[0][k]), depth(FACES[1][k])),
-            jnp.where(grid.south, depth(FACES[2][k]), depth(FACES[3][k])),
-        )
-        speed = jnp.sqrt(jnp.maximum(own, other))
-        speeds.append(speed)
-        parts = jump_parts(a, b, is_x, speed, own, inward)
-        for mask, face in ((is_w, 1), (is_e, 0), (is_s, 3), (is_n, 2)):
-            raise_at(FACES[face][k], mask, parts)
+        hy[pl.ds(64 * group, 8, stride=8), :] = lanes(got[2][a], -32 * q)
+        hy[pl.ds(64 * group + 7, 8, stride=8), :] = lanes(got[3][a], 96 - 32 * q)
 
     def diagonal(f, h, which):
         slot = jnp.where(slots[f] == 2, slots[h], slots[f])
-        return jnp.where(slot == 0, dx[which], do[which])
+        return jnp.where(slot == 0, rx[5 + which], ro[5 + which])
 
     there = [[(slots[f] < 3) & (slots[h] < 3) for h in (2, 3)] for f in (0, 1)]
-
-    def shifted(x, by, down):
-        return subs(lanes(x, by), down)
-
-    low = sub == 0
-    side_w = jnp.where(low, shifted(diagonal(0, 2, 0), 1, 1), shifted(diagonal(0, 3, 0), 65, -1))
-    side_e = jnp.where(low, shifted(diagonal(1, 2, 0), 48, 1), shifted(diagonal(1, 3, 0), 112, -1))
-    side_y = jnp.where(
-        lane < 30,
-        jnp.where(low, shifted(diagonal(0, 2, 1), 2, 1), shifted(diagonal(0, 3, 1), 98, -1)),
-        jnp.where(low, shifted(diagonal(1, 2, 1), 66, 1), shifted(diagonal(1, 3, 1), 34, -1)),
-    )
-
-    def beyond(i):
-        return jnp.where(is_w, lanes(side_w, -i), jnp.where(is_e, lanes(side_e, -i), lanes(side_y, -i)))
-
     low, high = sub == 0, sub == 7
-    at_s = low & (((lane == 0) & there[0][0]) | ((lane == 16) & there[1][0]))
-    at_n = high & (((lane == 96) & there[0][1]) | ((lane == 112) & there[1][1]))
-    at_w = (lane == 1) & ((low & there[0][0]) | (high & there[0][1]))
-    at_e = (lane == 34) & ((low & there[1][0]) | (high & there[1][1]))
-    outward = jnp.where(at_n | at_e, 1.0, -1.0)
-    for k in range(5):
-        a = [halo(IN_SIDE + 5 * v + k) for v in range(3)]
-        b = [beyond(5 * v + k) for v in range(3)]
-        own = jnp.where(
-            at_s,
-            halo_depth(FACES[2][k]),
-            jnp.where(at_n, halo_depth(FACES[3][k]), jnp.where(at_w, halo_depth(FACES[0][k]), halo_depth(FACES[1][k]))),
+    corners = []
+    for which in (0, 1):
+        corners.append(
+            jnp.where(
+                grid.south,
+                subs(jnp.where(lane < 25, lanes(diagonal(0, 2, which), 1), lanes(diagonal(1, 2, which), 63)), 1),
+                subs(
+                    jnp.where(
+                        (lane >= 96) & (lane < 120), lanes(diagonal(0, 3, which), 65), lanes(diagonal(1, 3, which), 127)
+                    ),
+                    -1,
+                ),
+            )
         )
-        speed = jnp.sqrt(jnp.maximum(own, beyond(15 + k)))
-        parts = jump_parts(a, b, ~is_x, speed, own, outward)
-        for mask, face in ((at_w, 0), (at_e, 1), (at_s, 2), (at_n, 3)):
-            raise_at(FACES[face][k], mask, parts)
+    corner_w = (low & (lane == 0) & there[0][0]) | (high & (lane == 96) & there[0][1])
+    corner_e = (low & (lane == 31) & there[1][0]) | (high & (lane == 127) & there[1][1])
+    corner_s = low & (corner_w | corner_e)
+    corner_n = high & (corner_w | corner_e)
 
     for i in range(75):
         m[0, i] = get(i)
-    for k in range(5):
-        speed_x, speed_y = from_halo(speeds[k])
-        sent = [from_halo(halo(IN_FACE + 5 * v + k)) for v in range(3)]
-        for axis, speed, at in ((0, speed_x, AT_X), (1, speed_y, AT_Y)):
-            first, last = 2 * axis, 2 * axis + 1
-            side = grid.south if axis else grid.west
-            normal, tangent = (2, 1) if axis else (1, 2)
-            j = [sent[v][axis] - get(at + 5 * v + k) for v in range(3)]
-            own = jnp.where(side, depth(FACES[first][k]), depth(FACES[last][k]))
-            out = flux(j[0], j[normal], j[tangent], speed, own, jnp.where(side, -1.0, 1.0))
+    for axis, h, g, side, at in ((0, hx, gx, grid.west, AT_X), (1, hy, gy, grid.south, AT_Y)):
+        first, last = 2 * axis, 2 * axis + 1
+        normal, tangent = (2, 1) if axis else (1, 2)
+        sign = jnp.where(side, 1.0, -1.0)
+
+        def halo(p, h=h):
+            return h[8 * p : 8 * p + 8, :]
+
+        def halo_depth(n, halo=halo):
+            return halo(AT_DEPTH + n)
+
+        for i in range(75):
+            g[0, i] = halo(i)
+        for k in range(5):
+            n, opposite = FACES[first][k], FACES[last][k]
+            a = [halo(IN_FACE + 5 * v + k) for v in range(3)]
+            b = [get(at + 5 * v + k) for v in range(3)]
+            own = jnp.where(side, depth(n), depth(opposite))
+            other = jnp.where(side, halo_depth(opposite), halo_depth(n))
+            speed = jnp.sqrt(jnp.maximum(own, other))
+            j = [b[v] - a[v] for v in range(3)]
+            out = flux(j[0], j[normal], j[tangent], speed, other, sign)
+            for v, part in ((0, out[0]), (normal, out[1]), (tangent, out[2])):
+                g[0, 25 * v + opposite] = g[0, 25 * v + opposite] + jnp.where(side, part, 0.0)
+                g[0, 25 * v + n] = g[0, 25 * v + n] + jnp.where(side, 0.0, part)
+            out = flux(-j[0], -j[normal], -j[tangent], speed, own, -sign)
             for f in (first, last):
-                n = FACES[f][k]
+                node = FACES[f][k]
+                fast[5 * f + k] = jnp.where(remotes[f], speed, cc[5 * f + k])
+                for v in range(3):
+                    before[15 * f + 5 * v + k] = jnp.where(remotes[f], a[v], nf[15 * f + 5 * v + k])
                 for v, part in ((0, out[0]), (normal, out[1]), (tangent, out[2])):
-                    m[0, 25 * v + n] = m[0, 25 * v + n] + jnp.where(remotes[f], part, 0.0)
+                    m[0, 25 * v + node] = m[0, 25 * v + node] + jnp.where(remotes[f], part, 0.0)
+        first, last = 2 - first, 3 - first
+        on_first, on_last = (corner_w, corner_e) if axis else (corner_s, corner_n)
+        side = grid.west if axis else grid.south
+        sign = jnp.where(side, -1.0, 1.0)
+        for k in range(5):
+            a = [halo(IN_SIDE + 5 * v + k) for v in range(3)]
+            b = [lanes(corners[axis], -(5 * v + k)) for v in range(3)]
+            own = jnp.where(side, halo_depth(FACES[first][k]), halo_depth(FACES[last][k]))
+            speed = jnp.sqrt(jnp.maximum(own, lanes(corners[axis], -(15 + k))))
+            j = [b[v] - a[v] for v in range(3)]
+            out = flux(j[0], j[tangent], j[normal], speed, own, sign)
+            for v, part in ((0, out[0]), (tangent, out[1]), (normal, out[2])):
+                for f, mask in ((first, on_first), (last, on_last)):
+                    at_node = 25 * v + FACES[f][k]
+                    g[0, at_node] = g[0, at_node] + jnp.where(mask, part, 0.0)
+        for k in range(3):
+            operate(g.at[k], g.at[k + 1], halo_depth)
+        side = grid.south if axis else grid.west
+        halo_fine = halo(AT_FLAG) > 0.5
+        for v in range(3):
+            for k in range(5):
+                n, opposite = FACES[2 * axis][k], FACES[2 * axis + 1][k]
+                terms = [jnp.where(side, g[q, 25 * v + opposite], g[q, 25 * v + n]) for q in range(4)]
+                after[15 * axis + 5 * v + k] = jnp.where(
+                    halo_fine, weighted(terms, HALF), halo(IN_SECOND + 5 * v + k)
+                )
 
     for k in range(4):
         operate(m.at[k], m.at[k + 1], depth)
-    for k in range(3):
-        operate(g.at[k], g.at[k + 1], halo_depth)
     fine = get(AT_FLAG) > 0.5
-    halo_fine = halo(AT_FLAG) > 0.5
-    halo_late = []
-    for v in range(3):
-        for k in range(5):
-            value = facing(lambda n: weighted([g[q, 25 * v + n] for q in range(4)], HALF))(k)
-            halo_late.append(from_halo(jnp.where(halo_fine, value, halo(IN_SECOND + 5 * v + k))))
     for v in range(3):
         for n in range(25):
             terms = [m[k, 25 * v + n] for k in range(5)]
@@ -386,16 +360,14 @@
         normal, tangent = (2, 1) if axis else (1, 2)
         for k in range(5):
             n, opposite = FACES[f][k], FACES[f ^ 1][k]
-            speed_out = from_halo(speeds[k])[axis]
-            speed = jnp.where(remotes[f], speed_out, cc[5 * f + k])
+            speed = fast[5 * f + k]
             j, a_list = [], []
             for v in range(3):
                 at, across = 16 * v + PLACE[n], 16 * v + PLACE[opposite]
                 a = jnp.where(fine, late[at], tr1[at] + tr2[at])
                 sent = grid.across(jnp.where(fine, late[across], tr2[across]), f)
-                sent = jnp.where(remotes[f], halo_late[5 * v + k][axis], sent)
-                before = jnp.where(remotes[f], from_halo(halo(IN_FACE + 5 * v + k))[axis], nf[15 * f + 5 * v + k])
-                b = jnp.where(fine, sent, before + sent)
+                sent = jnp.where(remotes[f], after[15 * axis + 5 * v + k], sent)
+                b = jnp.where(fine, sent, before[15 * f + 5 * v + k] + sent)
                 a_list.append(a)
                 j.append(b - a)
             js = jnp.where(walls[f], 0.0, j[0])
@@ -430,7 +402,12 @@
 
 
 VM = pl.BlockSpec(memory_space=pltpu.VMEM)
+ANY = pl.BlockSpec(memory_space=pltpu.HBM)
 PARAMS = pltpu.CompilerParams(vmem_limit_bytes=40 * 1024 * 1024)
+
+
+def in_hbm(x):
+    return pltpu.with_memory_space_constraint(x, pltpu.HBM)
 
 
 def planes(*counts):
@@ -446,35 +423,48 @@
     def passed(x, pairs):
         return lax.ppermute(x, "curve", pairs)
 
-    ex, eo, es, dg, ps, cb, tr1, tr2, nf, cc = pl.pallas_call(
+    ex, eo, es, ps, cb, tr1, tr2, nf, cc, near, owner = pl.pallas_call(
         first_kernel,
-        out_shape=planes(5, 5, 5, 2) + [jax.ShapeDtypeStruct((8 * PLANES, 128), F32)] + planes(75, 48, 48, 60, 20),
-        in_specs=[VM] * 5,
-        out_specs=[VM] * 10,
-        scratch_shapes=[pltpu.VMEM((5, 75, 8, 128), F32)] + [pltpu.VMEM((4, 8, 128), jnp.int32)] * 2,
+        out_shape=planes(7, 7, 7)
+        + [jax.ShapeDtypeStruct((8 * PLANES, 128), F32)]
+        + planes(75, 48, 48, 60, 20)
+        + [jax.ShapeDtypeStruct((4, 8, 128), jnp.int32)] * 2,
+        in_specs=[ANY] * 5,
+        out_specs=[VM] * 11,
+        scratch_shapes=[
+            pltpu.VMEM((5, 75, 8, 128), F32),
+            pltpu.VMEM((3, 25, 1024), F32),
+            pltpu.VMEM((25, 1024), F32),
+            pltpu.VMEM((4, 1024), jnp.int32),
+            pltpu.VMEM((4, 1024), jnp.int32),
+            pltpu.VMEM((8, 128), jnp.int32),
+            pltpu.SemaphoreType.DMA((5,)),
+        ],
         compiler_params=PARAMS,
         name="predict",
-    )(sea_state, water_depth, neighbours, neighbour_owner, clusters.reshape(8, 128))
-    ro = passed(eo, odd_swap)
-    do = passed(dg, [(i, (j + far) % devices) for i, j in odd_swap])
-    dx = passed(dg, [(i, (j + far) % devices) for i, j in chip_swap])
+    )(*(in_hbm(x) for x in (sea_state, water_depth, neighbours, neighbour_owner, clusters.reshape(8, 128))))
     rs = passed(es, [(i, (i + far) % devices) for i in range(devices)])
-    rx = passed(ex, chip_swap)
+    ro = passed(lax.dynamic_update_slice(eo, rs[5:], (5, 0, 0)), odd_swap)
+    rx = passed(lax.dynamic_update_slice(ex, rs[5:], (5, 0, 0)), chip_swap)
     upd, se, so = pl.pallas_call(
         second_kernel,
         out_shape=planes(75, 38, 38),
-        in_specs=[VM] * 13,
+        in_specs=[VM] * 11,
         out_specs=[VM] * 3,
         scratch_shapes=[
             pltpu.VMEM((8 * 160, 128), F32),
+            pltpu.VMEM((8 * 160, 128), F32),
             pltpu.VMEM((5, 75, 8, 128), F32),
             pltpu.VMEM((4, 75, 8, 128), F32),
+            pltpu.VMEM((4, 75, 8, 128), F32),
             pltpu.VMEM((48, 8, 128), F32),
-        ]
-        + [pltpu.VMEM((4, 8, 128), jnp.int32)] * 2,
+            pltpu.VMEM((60, 8, 128), F32),
+            pltpu.VMEM((30, 8, 128), F32),
+            pltpu.VMEM((20, 8, 128), F32),
+        ],
         compiler_params=PARAMS,
         name="correct",
-    )(rx, ro, rs, dx, do, ps, cb, tr1, tr2, nf, cc, neighbours, neighbour_owner)
+    )(rx, ro, rs, ps, cb, tr1, tr2, nf, cc, near, owner)
     got_odd = passed(so, odd_swap)
     got_even = passed(se, chip_swap)
     return pl.pallas_call(

time: 45.3 us -> 31.3 us (0.69)
  Pallas kernels: 9.56 us -> 5.37 us
  local copies, waits for them, and re-layouts: 4.03 us -> 0.01 us
  waiting for transfers between devices: 13.5 us -> 10.1 us
  starting transfers between devices: 17.8 us -> 15.5 us
    pallas_call x1, Pallas kernels: 6.85 us -> 1.6 us  [local(): pl.pallas_call(second_kernel, out_shape=planes(75, 38, 38), in_specs=[VM]...]
    unnamed x12 -> x2, local copies, waits for them, and re-layouts: 4.03 us -> 0.01 us
    ppermute x7 -> x5, waiting for transfers between devices: 13.5 us -> 10.1 us  [passed(): return lax.ppermute(x, 'curve', pairs)]
    ppermute x7 -> x5, starting transfers between devices: 17.8 us -> 15.5 us  [passed(): return lax.ppermute(x, 'curve', pairs)]
    pallas_call x1, Pallas kernels: 1.26 us -> 2.34 us  [local(): pl.pallas_call(first_kernel, out_shape=planes(7, 7, 7) + [jax.ShapeDtypeS...]
  transfers between devices with their start and end apart: 7 -> 5, of which waited for: 2 -> 3; matrix products, arithmetic and copies ran while one was open for 0% -> 0% of each run, Pallas kernels for 0% -> 0%
where the time goes in v2:
time: 31.3 us; the launch traced here: 31.1 us
  starting transfers between devices  15.5 us (50%)
  waiting for transfers between devices  10.1 us (32%)
  Pallas kernels  5.37 us (17%)
    ppermute x5, starting transfers between devices, passed(): return lax.ppermute(x, 'curve', pairs)  15.5 us
    ppermute x5, waiting for transfers between devices, passed(): return lax.ppermute(x, 'curve', pairs)  10.1 us
    pallas_call x1, Pallas kernels, local(): pl.pallas_call(first_kernel, out_shape=planes(7, 7, 7) + [jax.ShapeDtypeS...  2.34 us
    pallas_call x1, Pallas kernels, local(): pl.pallas_call(second_kernel, out_shape=planes(75, 38, 38), in_specs=[VM]...  1.6 us
    pallas_call x1, Pallas kernels, local(): pl.pallas_call(third_kernel, out_shape=jax.ShapeDtypeStruct((3, 25, 1024)...  1.44 us
  transfers between devices with their start and end apart: 5, of which 3 were waited for; matrix products, arithmetic and copies ran while one was open for 0% of the time, Pallas kernels for 0%

profile of v2, /device:TPU:6, one launch (start us, length us, event | category | flops | bytes accessed | tf_op | source)
XLA Modules:
  0.0 31.1 jit_solution(11398816194915295730)
XLA Ops:
  0.0 2.3 %predict.1 = (f32[7,8,128]{2,1,0:T(8,128)S(1)}, f32[7,8,128]{2,1,0:T(8,128)S(1)}, f32[7,8,128]{2,1,0:T(8,128)S(1)}, f32[1344,128]{1,0:T(8,128)S(1)}, f32[75,8,12...) custom-call(f32[3,25,1024]{2,1,0:T(8,128)} %sea_in.1, ...), custom_call_target="tpu_custom_call" | custom-call | tf_op jit(solution)/shard_map/predict/pallas_call | solution.py:426
  2.3 1.5 %collective-permute-start = (f32[7,8,128]{2,1,0:T(8,128)S(1)}, f32[7,8,128]{2,1,0:T(8,128)S(1)}, u32[]{:S(2)}, u32[]{:S(2)}) collective-permute-start(f32[7,8,128]{2,1,0:T(8,128)S(1)} %get-tuple-element.20), channel_id=1, source_target_pairs={{0,64},{1,65},{2,66},{3,67},{4,68},{5,69},{6,70},{7,71},{8,72},{9,... | collective-permute-start | bytes 86024 | tf_op jit(solution)/shard_map/ppermute | solution.py:424
  3.8 4.0 %collective-permute-done.rs = f32[7,8,128]{2,1,0:T(8,128)S(1)} collective-permute-done((f32[7,8,128]{2,1,0:T(8,128)S(1)}, f32[7,8,128]{2,1,0:T(8,128)S(1)}, u32[]{:S(2)}, u32[]{:S(2)}) %collective-permute-start) | collective-permute-done | bytes 28704 | tf_op jit(solution)/shard_map/ppermute | solution.py:424
  7.8 6.9 %collective-permute-start.2 = (f32[7,8,128]{2,1,0:T(8,128)S(1)}, f32[7,8,128]{2,1,0:T(8,128)S(1)}, u32[]{:S(2)}, u32[]{:S(2)}) collective-permute-start(f32[7,8,128]{2,1,0:T(8,128)S(1)} %get-tuple-element.33), channel_id=1, source_target_pairs={{1,2},{3,4},{5,6},{7,8},{9,10},{11,12},{13,14},{15,16},{17,18},{19... | collective-permute-start | bytes 86024 | tf_op jit(solution)/shard_map/ppermute | solution.py:424
  14.7 0.1 collective-permute-start.1
  14.8 2.4 %collective-permute-done.2.ro = f32[7,8,128]{2,1,0:T(8,128)S(1)} collective-permute-done((f32[7,8,128]{2,1,0:T(8,128)S(1)}, f32[7,8,128]{2,1,0:T(8,128)S(1)}, u32[]{:S(2)}, u32[]{:S(2)}) %collective-permute-start.2) | collective-permute-done | bytes 28704 | tf_op jit(solution)/shard_map/ppermute | solution.py:424
  17.2 0.0 collective-permute-done.1.rx
  17.2 1.6 %correct.1 = (f32[75,8,128]{2,1,0:T(8,128)S(1)}, f32[38,8,128]{2,1,0:T(8,128)S(1)}, f32[38,8,128]{2,1,0:T(8,128)S(1)}) custom-call(f32[7,8,128]{2,1,0:T(8,128)S(1)} %collective-permute-done.1.rx, f32[7,8,128]{2,1,0:T(8,128)S(1)} %collective-permute-done.2.ro, f32[7,8,128]{2,1,0:T(8,128)S(1)} %collective-permute-done.rs, ...), custom_call_target="tpu_custom_call" | custom-call | tf_op jit(solution)/shard_map/correct/pallas_call | solution.py:449
  18.8 0.1 collective-permute-start.3
  18.9 0.0 copy-start
  18.9 7.0 %collective-permute-start.4 = (f32[38,8,128]{2,1,0:T(8,128)S(1)}, f32[38,8,128]{2,1,0:T(8,128)S(1)}, u32[]{:S(2)}, u32[]{:S(2)}) collective-permute-start(f32[38,8,128]{2,1,0:T(8,128)S(1)} %get-tuple-element.31), channel_id=1, source_target_pairs={{1,2},{3,4},{5,6},{7,8},{9,10},{11,12},{13,14},{15,16},{17,18},{19... | collective-permute-start | bytes 466952 | tf_op jit(solution)/shard_map/ppermute | solution.py:424
  25.9 0.0 collective-permute-done.3.re
  25.9 3.8 %collective-permute-done.4.ro = f32[38,8,128]{2,1,0:T(8,128)S(1)} collective-permute-done((f32[38,8,128]{2,1,0:T(8,128)S(1)}, f32[38,8,128]{2,1,0:T(8,128)S(1)}, u32[]{:S(2)}, u32[]{:S(2)}) %collective-permute-start.4) | collective-permute-done | bytes 155680 | tf_op jit(solution)/shard_map/ppermute | solution.py:424
  29.7 0.0 copy-done
  29.7 1.4 %migrate.1 = f32[3,25,1024]{2,1,0:T(8,128)} custom-call(s32[32]{0:T(128)S(1)} %copy-done, f32[38,8,128]{2,1,0:T(8,128)S(1)} %collective-permute-done.3.re, f32[38,8,128]{2,1,0:T(8,128)S(1)} %collective-permute-done.4.ro, f32[75,8,128]{2,1,0:T(8,128)S(1)} %get-tuple-element.32.upd), custom_call_target="tpu_custom_call" | custom-call | tf_op jit(solution)/shard_map/migrate/pallas_call | solution.py:470
  (1 shorter events, 0.0 us)
Async XLA Ops:
  2.3 5.5 %collective-permute-start = (f32[7,8,128]{2,1,0:T(8,128)S(1)}, f32[7,8,128]{2,1,0:T(8,128)S(1)}, u32[]{:S(2)}, u32[]{:S(2)}) collective-permute-start(f32[7,8,128]{2,1,0:T(8,128)S(1)} %get-tuple-element.20), channel_id=1, source_target_pairs={{0,64},{1,65},{2,66},{3,67},{4,68},{5,69},{6,70},{7,71},{8,72},{9,... | collective-permute-start | bytes 86024 | tf_op jit(solution)/shard_map/ppermute | solution.py:424
  7.8 9.4 %collective-permute-start.2 = (f32[7,8,128]{2,1,0:T(8,128)S(1)}, f32[7,8,128]{2,1,0:T(8,128)S(1)}, u32[]{:S(2)}, u32[]{:S(2)}) collective-permute-start(f32[7,8,128]{2,1,0:T(8,128)S(1)} %get-tuple-element.33), channel_id=1, source_target_pairs={{1,2},{3,4},{5,6},{7,8},{9,10},{11,12},{13,14},{15,16},{17,18},{19... | collective-permute-start | bytes 86024 | tf_op jit(solution)/shard_map/ppermute | solution.py:424
  14.7 2.5 %collective-permute-start.1 = (f32[7,8,128]{2,1,0:T(8,128)S(1)}, f32[7,8,128]{2,1,0:T(8,128)S(1)}, u32[]{:S(2)}, u32[]{:S(2)}) collective-permute-start(f32[7,8,128]{2,1,0:T(8,128)S(1)} %get-tuple-element.34), channel_id=1, source_target_pairs={{0,1},{1,0},{2,3},{3,2},{4,5},{5,4},{6,7},{7,6},{8,9},{9,8},{10,11... | collective-permute-start | bytes 86024 | tf_op jit(solution)/shard_map/ppermute | solution.py:424
  18.8 7.1 %collective-permute-start.3 = (f32[38,8,128]{2,1,0:T(8,128)S(1)}, f32[38,8,128]{2,1,0:T(8,128)S(1)}, u32[]{:S(2)}, u32[]{:S(2)}) collective-permute-start(f32[38,8,128]{2,1,0:T(8,128)S(1)} %get-tuple-element.30), channel_id=1, source_target_pairs={{0,1},{1,0},{2,3},{3,2},{4,5},{5,4},{6,7},{7,6},{8,9},{9,8},{10,11... | collective-permute-start | bytes 466952 | tf_op jit(solution)/shard_map/ppermute | solution.py:424
  18.9 10.8 %copy-start = (s32[32]{0:T(128)S(1)}, s32[32]{0:T(128)}, u32[]{:S(2)}) copy-start(s32[32]{0:T(128)} %swap.1) | copy-start | bytes 388
  18.9 10.8 %collective-permute-start.4 = (f32[38,8,128]{2,1,0:T(8,128)S(1)}, f32[38,8,128]{2,1,0:T(8,128)S(1)}, u32[]{:S(2)}, u32[]{:S(2)}) collective-permute-start(f32[38,8,128]{2,1,0:T(8,128)S(1)} %get-tuple-element.31), channel_id=1, source_target_pairs={{1,2},{3,4},{5,6},{7,8},{9,10},{11,12},{13,14},{15,16},{17,18},{19... | collective-permute-start | bytes 466952 | tf_op jit(solution)/shard_map/ppermute | solution.py:424

commit v3 on v2

--- a/solution.py
+++ b/solution.py
@@ -103,21 +103,26 @@
         out[:, j, :] = ref[:, 128 * j : 128 * j + 128]
 
 
-def face_facts(near, owner):
+def face_facts(near, owner, facts):
     me = lax.axis_index("curve")
     odd = me % 2
     chip = me + 1 - 2 * odd
     swap = me - 1 + 2 * odd
-    walls, remotes, slots = [], [], []
     for f in range(4):
         wall = near[f] < 0
         remote = (near[f] >= 0) & (owner[f] != me)
-        peer = jnp.max(jnp.where(remote, owner[f], -1).astype(F32)).astype(jnp.int32)
-        walls.append(wall)
-        remotes.append(remote)
+        peer = jnp.where(remote, owner[f], -1).astype(F32)
+        peer = jnp.max(jnp.max(peer, axis=1, keepdims=True), axis=0, keepdims=True).astype(jnp.int32)
+        peer = jnp.broadcast_to(peer, (8, 128))
         slot = jnp.where(peer == chip, 0, jnp.where(peer == swap, 1, 2))
-        slots.append(jnp.where(peer < 0, 3, slot))
-    return walls, remotes, slots
+        facts[f] = jnp.where(peer < 0, 3, slot)
+        facts[4 + f] = jnp.where(wall, 1, jnp.where(remote, 2, 0))
+
+
+def read_facts(facts):
+    walls = [facts[4 + f] == 1 for f in range(4)]
+    remotes = [facts[4 + f] == 2 for f in range(4)]
+    return walls, remotes, [facts[f] for f in range(4)]
 
 
 def flux(js, jn, jt, speed, depth, sign):
@@ -126,8 +131,34 @@
     return lifted * js - turn * jn, lifted * jn - depth * (turn * js), lifted * jt
 
 
+def side_edges(grid, get):
+    blank = jnp.zeros((8, 128), F32)
+    west, east = [blank] * 5, [blank] * 5
+    for i in VALUES:
+        a, by = divmod(i, 32)
+        by = 2 * by if by < 16 else 2 * by - 31
+        turned = lanes(get(i), by)
+        west[a] = jnp.where(grid.col == by, turned, west[a])
+        east[a] = jnp.where(grid.col == (31 + by) % 32, turned, east[a])
+    return west, [lanes(x, -31) for x in east]
+
+
+def row_edges(grid, ps):
+    blank = jnp.zeros((8, 128), F32)
+    south, north = [blank] * 5, [blank] * 5
+    for group in range(IN_ALL // 8):
+        a, g = divmod(group, 4)
+        base = {13: 17, 14: 18, 15: 19, 16: 20, 17: 13, 18: 14}.get(group, group)
+        here = grid.lane // 32 == g
+        low = ps[pl.ds(64 * base, 8, stride=8), :]
+        high = ps[pl.ds(64 * base + 7, 8, stride=8), :]
+        south[a] = jnp.where(here, lanes(low, 32 * g), south[a])
+        north[a] = jnp.where(here, lanes(high, 32 * g + 32), north[a])
+    return south, north
+
+
 def first_kernel(
-    sea_in, dep_in, near_in, owner_in, cl_in, ex, eo, es, ps, cb, tr1, tr2, nf, cc, near, owner, u, sea, dep, nb, ow, cl, sems
+    sea_in, dep_in, near_in, owner_in, cl_in, ex, eo, ps, u, tr1, tr2, nf, cc, facts, sea, dep, nb, ow, cl, near, owner, sems
 ):
     copies = [
         pltpu.make_async_copy(src, dst, sems.at[i])
@@ -141,7 +172,8 @@
         copy.wait()
     spread_ints(nb, near)
     spread_ints(ow, owner)
-    walls, remotes, slots = face_facts(near, owner)
+    face_facts(near, owner, facts)
+    walls, remotes, slots = read_facts(facts)
     inner = [~(walls[f] | remotes[f]) for f in range(4)]
     u[0] = sea[...].reshape(75, 8, 128)
     ps[8 * AT_DEPTH : 8 * AT_FLAG, :] = dep[...].reshape(25, 8, 128).reshape(200, 128)
@@ -161,7 +193,6 @@
         for n in range(25):
             terms = [u[k, 25 * v + n] for k in range(5)]
             put(25 * v + n, terms[0] + weighted(terms[1:], HALF))
-            cb[25 * v + n] = terms[0] + weighted(terms[1:], WHOLE)
             if n in PLACE:
                 first = weighted(terms[:4], HALF)
                 tr1[16 * v + PLACE[n]] = first
@@ -194,65 +225,85 @@
                 at = [src[16 * v + PLACE[FACES[f][k]]] for f in range(4)]
                 put(x + i, jnp.where(grid.west, at[0], at[1]))
                 put(y + i, jnp.where(grid.south, at[2], at[3]))
+    west, east = side_edges(grid, get)
+    for slot, out in ((0, ex), (1, eo)):
+        for a in range(5):
+            out[a] = jnp.where(slots[0] == slot, west[a], east[a])
+    turned = jnp.max(jnp.where((slots[2] < 2) | (slots[3] < 2), 1.0, 0.0)) > 0.5
+
+    @pl.when(turned)
+    def _():
+        south, north = row_edges(grid, ps)
+        for slot, out in ((0, ex), (1, eo)):
+            for a in range(5):
+                out[a] = jnp.where(slots[2] == slot, south[a], jnp.where(slots[3] == slot, north[a], out[a]))
+
     blank = jnp.zeros((8, 128), F32)
-    west, east, south, north = ([blank] * 5 for _ in range(4))
-    for i in VALUES:
-        a, by = divmod(i, 32)
-        by = 2 * by if by < 16 else 2 * by - 31
-        turned = lanes(get(i), by)
-        west[a] = jnp.where(col == by, turned, west[a])
-        east[a] = jnp.where(col == (31 + by) % 32, turned, east[a])
-    east = [lanes(x, -31) for x in east]
-    for group in range(IN_ALL // 8):
-        a, g = divmod(group, 4)
-        base = group
-        if group >= 13:
-            base = {13: 17, 14: 18, 15: 19, 16: 20, 17: 13, 18: 14}[group]
-        here = lane // 32 == g
-        low = ps[pl.ds(64 * base, 8, stride=8), :]
-        high = ps[pl.ds(64 * base + 7, 8, stride=8), :]
-        south[a] = jnp.where(here, lanes(low, 32 * g), south[a])
-        north[a] = jnp.where(here, lanes(high, 32 * g + 32), north[a])
-    for slot, out in enumerate((ex, eo, es)):
-        for a in range(5):
-            out[a] = jnp.where(
-                slots[0] == slot,
-                west[a],
-                jnp.where(slots[1] == slot, east[a], jnp.where(slots[2] == slot, south[a], north[a])),
-            )
     corner = ((col == 0) | (col == 31)) & (((sub == 0) & (lane < 32)) | ((sub == 7) & (lane >= 96)))
     for which, at, low, high, mask in ((0, AT_Y, 2, 3, grid.south), (1, AT_X, 0, 1, grid.west)):
         total = blank
         for i in range(20):
             value = get(at + i) if i < 15 else jnp.where(mask, depth(FACES[low][i - 15]), depth(FACES[high][i - 15]))
             total = total + lanes(jnp.where(corner, value, 0.0), i)
-        es[5 + which] = total
-
-
-def second_kernel(
-    rx, ro, rs, ps, cb, tr1, tr2, nf, cc, near, owner, upd, se, so, hx, hy, m, gx, gy, late, before, after, fast
-):
+        ex[5 + which] = total
+        eo[5 + which] = total
+
+
+def messages_kernel(ps, u, facts, es, cb):
     grid = Grid()
-    lane, sub = grid.lane, grid.sub
-    walls, remotes, slots = face_facts(near, owner)
-
-    def get(p):
-        return ps[8 * p : 8 * p + 8, :]
-
-    def depth(n):
-        return get(AT_DEPTH + n)
-
-    got = [
-        [jnp.where(slots[f] == 0, rx[a], jnp.where(slots[f] == 1, ro[a], rs[a])) for a in range(5)] for f in range(4)
-    ]
+    _, _, slots = read_facts(facts)
+    south, north = row_edges(grid, ps)
+    for a in range(5):
+        es[a] = jnp.where(slots[2] == 2, south[a], north[a])
+    for i in range(75):
+        cb[i] = u[0, i] + weighted([u[k, i] for k in range(1, 5)], WHOLE)
+    turned = jnp.max(jnp.where((slots[0] == 2) | (slots[1] == 2), 1.0, 0.0)) > 0.5
+
+    @pl.when(turned)
+    def _():
+        west, east = side_edges(grid, lambda p: ps[8 * p : 8 * p + 8, :])
+        for a in range(5):
+            es[a] = jnp.where(slots[0] == 2, west[a], jnp.where(slots[1] == 2, east[a], es[a]))
+
+
+def unpack_sides(grid, got, hx):
     for a in range(5):
         pair = (
-            jnp.where(lane % 2 == 0, got[0][a], lanes(got[1][a], 31)),
-            jnp.where(lane % 2 == 0, lanes(got[0][a], -1), lanes(got[1][a], 30)),
+            jnp.where(grid.lane % 2 == 0, got[0][a], lanes(got[1][a], 31)),
+            jnp.where(grid.lane % 2 == 0, lanes(got[0][a], -1), lanes(got[1][a], 30)),
         )
         for i in VALUES:
             if i // 32 == a:
                 hx[8 * i : 8 * i + 8, :] = lanes(pair[i % 32 // 16], -2 * (i % 16))
+
+
+def sides_kernel(rx, ro, facts, hx):
+    _, _, slots = read_facts(facts)
+    unpack_sides(Grid(), [[jnp.where(slots[f] == 0, rx[a], ro[a]) for a in range(5)] for f in (0, 1)], hx)
+
+
+def second_kernel(
+    rx, ro, rs, ps, cb, tr1, tr2, nf, cc, facts, hx_in, upd, se, so, hx, hy, m, gx, gy, late, before, after, fast
+):
+    grid = Grid()
+    lane, sub = grid.lane, grid.sub
+    walls, remotes, slots = read_facts(facts)
+
+    def get(p):
+        return ps[8 * p : 8 * p + 8, :]
+
+    def depth(n):
+        return get(AT_DEPTH + n)
+
+    got = [
+        [jnp.where(slots[f] == 0, rx[a], jnp.where(slots[f] == 1, ro[a], rs[a])) for a in range(5)] for f in range(4)
+    ]
+    turned = jnp.max(jnp.where((slots[0] == 2) | (slots[1] == 2), 1.0, 0.0)) > 0.5
+
+    @pl.when(turned)
+    def _():
+        unpack_sides(grid, got, hx)
+
     for group in range(IN_ALL // 8):
         a, q = divmod(group, 4)
         hy[pl.ds(64 * group, 8, stride=8), :] = lanes(got[2][a], -32 * q)
@@ -260,7 +311,7 @@
 
     def diagonal(f, h, which):
         slot = jnp.where(slots[f] == 2, slots[h], slots[f])
-        return jnp.where(slot == 0, rx[5 + which], ro[5 + which])
+        return jnp.where(slot == 0, rs[5 + which], rs[7 + which])
 
     there = [[(slots[f] < 3) & (slots[h] < 3) for h in (2, 3)] for f in (0, 1)]
     low, high = sub == 0, sub == 7
@@ -384,7 +435,7 @@
         so[p] = jnp.where(even, lanes(two, -32), one)
 
 
-def third_kernel(swap, re, ro, upd, out, buf):
+def third_kernel(swap, re, ro, upd, out, buf, flat, sems):
     grid = Grid()
     group = grid.lane // 32
     even = group % 2 == 0
@@ -393,12 +444,16 @@
     for b in range(32):
         moves = jnp.where(row == b, swap[b], moves)
     moves = moves > 0
-    for i in range(75):
-        e, o = re[i // 2], ro[i // 2]
-        if i % 2:
-            e, o = lanes(e, -32), lanes(o, 32)
-        buf[i] = jnp.where(moves, jnp.where(even, e, o), upd[i])
-    out[...] = buf[...].reshape(3, 25, 1024)
+    for v in range(3):
+        for i in range(25 * v, 25 * v + 25):
+            e, o = re[i // 2], ro[i // 2]
+            if i % 2:
+                e, o = lanes(e, -32), lanes(o, 32)
+            buf[i] = jnp.where(moves, jnp.where(even, e, o), upd[i])
+        flat[v] = buf[25 * v : 25 * v + 25].reshape(25, 1024)
+        pltpu.make_async_copy(flat.at[v], out.at[v], sems.at[v]).start()
+    for v in range(3):
+        pltpu.make_async_copy(flat.at[v], out.at[v], sems.at[v]).wait()
 
 
 VM = pl.BlockSpec(memory_space=pltpu.VMEM)
@@ -423,36 +478,56 @@
     def passed(x, pairs):
         return lax.ppermute(x, "curve", pairs)
 
-    ex, eo, es, ps, cb, tr1, tr2, nf, cc, near, owner = pl.pallas_call(
+    ex, eo, ps, u, tr1, tr2, nf, cc, facts = pl.pallas_call(
         first_kernel,
-        out_shape=planes(7, 7, 7)
-        + [jax.ShapeDtypeStruct((8 * PLANES, 128), F32)]
-        + planes(75, 48, 48, 60, 20)
-        + [jax.ShapeDtypeStruct((4, 8, 128), jnp.int32)] * 2,
+        out_shape=planes(7, 7)
+        + [jax.ShapeDtypeStruct((8 * PLANES, 128), F32), jax.ShapeDtypeStruct((5, 75, 8, 128), F32)]
+        + planes(48, 48, 60, 20)
+        + [jax.ShapeDtypeStruct((8, 8, 128), jnp.int32)],
         in_specs=[ANY] * 5,
-        out_specs=[VM] * 11,
+        out_specs=[VM] * 9,
         scratch_shapes=[
-            pltpu.VMEM((5, 75, 8, 128), F32),
             pltpu.VMEM((3, 25, 1024), F32),
             pltpu.VMEM((25, 1024), F32),
             pltpu.VMEM((4, 1024), jnp.int32),
             pltpu.VMEM((4, 1024), jnp.int32),
             pltpu.VMEM((8, 128), jnp.int32),
+            pltpu.VMEM((4, 8, 128), jnp.int32),
+            pltpu.VMEM((4, 8, 128), jnp.int32),
             pltpu.SemaphoreType.DMA((5,)),
         ],
         compiler_params=PARAMS,
         name="predict",
     )(*(in_hbm(x) for x in (sea_state, water_depth, neighbours, neighbour_owner, clusters.reshape(8, 128))))
+    es, cb = pl.pallas_call(
+        messages_kernel,
+        out_shape=planes(9, 75),
+        in_specs=[VM] * 3,
+        out_specs=[VM] * 2,
+        compiler_params=PARAMS,
+        cost_estimate=pl.CostEstimate(flops=2_000_000, bytes_accessed=4_000_000, transcendentals=0),
+        name="messages",
+    )(ps, u, facts)
+    ro = passed(eo, odd_swap)
+    rx = passed(ex, chip_swap)
+    es = lax.dynamic_update_slice(lax.dynamic_update_slice(es, ro[5:], (7, 0, 0)), rx[5:], (5, 0, 0))
     rs = passed(es, [(i, (i + far) % devices) for i in range(devices)])
-    ro = passed(lax.dynamic_update_slice(eo, rs[5:], (5, 0, 0)), odd_swap)
-    rx = passed(lax.dynamic_update_slice(ex, rs[5:], (5, 0, 0)), chip_swap)
-    upd, se, so = pl.pallas_call(
+    hx = pl.pallas_call(
+        sides_kernel,
+        out_shape=jax.ShapeDtypeStruct((8 * IN_ALL, 128), F32),
+        in_specs=[VM] * 3,
+        out_specs=VM,
+        compiler_params=PARAMS,
+        cost_estimate=pl.CostEstimate(flops=2_000_000, bytes_accessed=4_000_000, transcendentals=0),
+        name="sides",
+    )(rx, ro, facts)
+    upd, se, so, _ = pl.pallas_call(
         second_kernel,
-        out_shape=planes(75, 38, 38),
+        out_shape=planes(75, 38, 38) + [jax.ShapeDtypeStruct((8 * IN_ALL, 128), F32)],
         in_specs=[VM] * 11,
-        out_specs=[VM] * 3,
+        out_specs=[VM] * 4,
+        input_output_aliases={10: 3},
         scratch_shapes=[
-            pltpu.VMEM((8 * 160, 128), F32),
             pltpu.VMEM((8 * 160, 128), F32),
             pltpu.VMEM((5, 75, 8, 128), F32),
             pltpu.VMEM((4, 75, 8, 128), F32),
@@ -464,15 +539,19 @@
         ],
         compiler_params=PARAMS,
         name="correct",
-    )(rx, ro, rs, ps, cb, tr1, tr2, nf, cc, near, owner)
+    )(rx, ro, rs, ps, cb, tr1, tr2, nf, cc, facts, hx)
     got_odd = passed(so, odd_swap)
     got_even = passed(se, chip_swap)
     return pl.pallas_call(
         third_kernel,
         out_shape=jax.ShapeDtypeStruct((3, 25, 1024), F32),
         in_specs=[pl.BlockSpec(memory_space=pltpu.SMEM)] + [VM] * 3,
-        out_specs=VM,
-        scratch_shapes=[pltpu.VMEM((75, 8, 128), F32)],
+        out_specs=ANY,
+        scratch_shapes=[
+            pltpu.VMEM((75, 8, 128), F32),
+            pltpu.VMEM((3, 25, 1024), F32),
+            pltpu.SemaphoreType.DMA((3,)),
+        ],
         compiler_params=PARAMS,
         name="migrate",
     )(block_swap, got_even, got_odd, upd)

time: 31.3 us -> 31.5 us (level)
  waiting for transfers between devices: 10.1 us -> 9.26 us
  starting transfers between devices: 15.5 us -> 16.2 us
  Pallas kernels: 5.37 us -> 5.79 us
    ppermute x5, waiting for transfers between devices: 10.1 us -> 9.26 us  [passed(): return lax.ppermute(x, 'curve', pairs)]
    ppermute x5, starting transfers between devices: 15.5 us -> 16.2 us  [passed(): return lax.ppermute(x, 'curve', pairs)]
    pallas_call x2 -> x4, Pallas kernels: 3.93 us -> 4.39 us  [the longest x1 2.35 us: local(): pl.pallas_call(first_kernel, out_shape=planes(7, 7) + [jax.ShapeDtypeStru...]
  transfers between devices with their start and end apart: 5 -> 5, of which waited for: 3 -> 3; matrix products, arithmetic and copies ran while one was open for 0% -> 0% of each run, Pallas kernels for 0% -> 2%
where the time goes in v3:
time: 31.5 us; the launch traced here: 31.4 us
  starting transfers between devices  16.2 us (51%)
  waiting for transfers between devices  9.26 us (29%)
  Pallas kernels  5.79 us (18%)
    ppermute x5, starting transfers between devices, passed(): return lax.ppermute(x, 'curve', pairs)  16.2 us
    ppermute x5, waiting for transfers between devices, passed(): return lax.ppermute(x, 'curve', pairs)  9.26 us
    pallas_call x1, Pallas kernels, local(): pl.pallas_call(first_kernel, out_shape=planes(7, 7) + [jax.ShapeDtypeStru...  2.35 us
    pallas_call x1, Pallas kernels, local(): pl.pallas_call(second_kernel, out_shape=planes(75, 38, 38) + [jax.ShapeDt...  1.52 us
    pallas_call x1, Pallas kernels, local(): pl.pallas_call(third_kernel, out_shape=jax.ShapeDtypeStruct((3, 25, 1024)...  1.41 us
  transfers between devices with their start and end apart: 5, of which 3 were waited for; matrix products, arithmetic and copies ran while one was open for 0% of the time, Pallas kernels for 2%

profile of v3, /device:TPU:6, one launch (start us, length us, event | category | flops | bytes accessed | tf_op | source)
XLA Modules:
  0.0 31.4 jit_solution(11665818595766223749)
XLA Ops:
  0.0 2.4 %predict.1 = (f32[7,8,128]{2,1,0:T(8,128)S(1)}, f32[7,8,128]{2,1,0:T(8,128)S(1)}, f32[1344,128]{1,0:T(8,128)S(1)}, f32[5,75,8,128]{3,2,1,0:T(8,128)S(1)}, f32[48...) custom-call(f32[3,25,1024]{2,1,0:T(8,128)} %sea_in.1, ...), custom_call_target="tpu_custom_call" | custom-call | tf_op jit(solution)/shard_map/predict/pallas_call | solution.py:481
  2.4 8.1 %collective-permute-start.1 = (f32[7,8,128]{2,1,0:T(8,128)S(1)}, f32[7,8,128]{2,1,0:T(8,128)S(1)}, u32[]{:S(2)}, u32[]{:S(2)}) collective-permute-start(f32[7,8,128]{2,1,0:T(8,128)S(1)} %get-tuple-element.20), channel_id=1, source_target_pairs={{1,2},{3,4},{5,6},{7,8},{9,10},{11,12},{13,14},{15,16},{17,18},{19... | collective-permute-start | bytes 86024 | tf_op jit(solution)/shard_map/ppermute | solution.py:479
  10.5 0.1 collective-permute-start
  10.6 0.1 messages.1
  10.7 1.3 %collective-permute-done.1.ro = f32[7,8,128]{2,1,0:T(8,128)S(1)} collective-permute-done((f32[7,8,128]{2,1,0:T(8,128)S(1)}, f32[7,8,128]{2,1,0:T(8,128)S(1)}, u32[]{:S(2)}, u32[]{:S(2)}) %collective-permute-start.1) | collective-permute-done | bytes 28704 | tf_op jit(solution)/shard_map/ppermute | solution.py:479
  12.0 0.0 collective-permute-done.rx
  12.0 0.0 copy-start
  12.0 1.2 %collective-permute-start.2 = (f32[9,8,128]{2,1,0:T(8,128)S(1)}, f32[9,8,128]{2,1,0:T(8,128)S(1)}, u32[]{:S(2)}, u32[]{:S(2)}) collective-permute-start(f32[9,8,128]{2,1,0:T(8,128)S(1)} %slice_dynamic-update-slice_fusion), channel_id=1, source_target_pairs={{0,64},{1,65},{2,66},{3,67},{4,68},{5,69},{6,70},{7,71},{8,72},{9,... | collective-permute-start | bytes 110600 | tf_op jit(solution)/shard_map/ppermute | solution.py:479
  13.3 0.4 %sides.1.hx_in = f32[1216,128]{1,0:T(8,128)S(1)} custom-call(f32[7,8,128]{2,1,0:T(8,128)S(1)} %collective-permute-done.rx, f32[7,8,128]{2,1,0:T(8,128)S(1)} %collective-permute-done.1.ro, s32[8,8,128]{2,1,0:T(8,128)S(1)} %get-tuple-element.23.facts), custom_call_target="tpu_custom_call" | custom-call | flops 2000000 | bytes 4000000 | tf_op jit(solution)/shard_map/sides/pallas_call | solution.py:515
  13.7 3.9 %collective-permute-done.2.rs = f32[9,8,128]{2,1,0:T(8,128)S(1)} collective-permute-done((f32[9,8,128]{2,1,0:T(8,128)S(1)}, f32[9,8,128]{2,1,0:T(8,128)S(1)}, u32[]{:S(2)}, u32[]{:S(2)}) %collective-permute-start.2) | collective-permute-done | bytes 36896 | tf_op jit(solution)/shard_map/ppermute | solution.py:479
  17.6 1.5 %correct.1 = (f32[75,8,128]{2,1,0:T(8,128)S(1)}, f32[38,8,128]{2,1,0:T(8,128)S(1)}, f32[38,8,128]{2,1,0:T(8,128)S(1)}, f32[1216,128]{1,0:T(8,128)S(1)}) custom-call(f32[7,8,128]{2,1,0:T(8,128)S(1)} %collective-permute-done.rx, f32[7,8,128]{2,1,0:T(8,128)S(1)} %collective-permute-done.1.ro, ...), custom_call_target="tpu_custom_call", output_to_operand_aliasing={{3}: (10, {})} | custom-call | tf_op jit(solution)/shard_map/correct/pallas_call | solution.py:524
  19.1 0.1 collective-permute-start.3
  19.2 6.7 %collective-permute-start.4 = (f32[38,8,128]{2,1,0:T(8,128)S(1)}, f32[38,8,128]{2,1,0:T(8,128)S(1)}, u32[]{:S(2)}, u32[]{:S(2)}) collective-permute-start(f32[38,8,128]{2,1,0:T(8,128)S(1)} %get-tuple-element.31), channel_id=1, source_target_pairs={{1,2},{3,4},{5,6},{7,8},{9,10},{11,12},{13,14},{15,16},{17,18},{19... | collective-permute-start | bytes 466952 | tf_op jit(solution)/shard_map/ppermute | solution.py:479
  25.9 0.0 collective-permute-done.3.re
  25.9 4.0 %collective-permute-done.4.ro = f32[38,8,128]{2,1,0:T(8,128)S(1)} collective-permute-done((f32[38,8,128]{2,1,0:T(8,128)S(1)}, f32[38,8,128]{2,1,0:T(8,128)S(1)}, u32[]{:S(2)}, u32[]{:S(2)}) %collective-permute-start.4) | collective-permute-done | bytes 155680 | tf_op jit(solution)/shard_map/ppermute | solution.py:479
  30.0 0.0 copy-done
  30.0 1.4 %migrate.1 = f32[3,25,1024]{2,1,0:T(8,128)} custom-call(s32[32]{0:T(128)S(1)} %copy-done, f32[38,8,128]{2,1,0:T(8,128)S(1)} %collective-permute-done.3.re, f32[38,8,128]{2,1,0:T(8,128)S(1)} %collective-permute-done.4.ro, f32[75,8,128]{2,1,0:T(8,128)S(1)} %get-tuple-element.32.upd), custom_call_target="tpu_custom_call" | custom-call | tf_op jit(solution)/shard_map/migrate/pallas_call | solution.py:545
  (2 shorter events, 0.0 us)
Async XLA Ops:
  2.4 9.6 %collective-permute-start.1 = (f32[7,8,128]{2,1,0:T(8,128)S(1)}, f32[7,8,128]{2,1,0:T(8,128)S(1)}, u32[]{:S(2)}, u32[]{:S(2)}) collective-permute-start(f32[7,8,128]{2,1,0:T(8,128)S(1)} %get-tuple-element.20), channel_id=1, source_target_pairs={{1,2},{3,4},{5,6},{7,8},{9,10},{11,12},{13,14},{15,16},{17,18},{19... | collective-permute-start | bytes 86024 | tf_op jit(solution)/shard_map/ppermute | solution.py:479
  10.5 1.5 %collective-permute-start = (f32[7,8,128]{2,1,0:T(8,128)S(1)}, f32[7,8,128]{2,1,0:T(8,128)S(1)}, u32[]{:S(2)}, u32[]{:S(2)}) collective-permute-start(f32[7,8,128]{2,1,0:T(8,128)S(1)} %get-tuple-element.19), channel_id=1, source_target_pairs={{0,1},{1,0},{2,3},{3,2},{4,5},{5,4},{6,7},{7,6},{8,9},{9,8},{10,11... | collective-permute-start | bytes 86024 | tf_op jit(solution)/shard_map/ppermute | solution.py:479
  12.0 17.9 %copy-start = (s32[32]{0:T(128)S(1)}, s32[32]{0:T(128)}, u32[]{:S(2)}) copy-start(s32[32]{0:T(128)} %swap.1) | copy-start | bytes 388
  12.0 5.5 %collective-permute-start.2 = (f32[9,8,128]{2,1,0:T(8,128)S(1)}, f32[9,8,128]{2,1,0:T(8,128)S(1)}, u32[]{:S(2)}, u32[]{:S(2)}) collective-permute-start(f32[9,8,128]{2,1,0:T(8,128)S(1)} %slice_dynamic-update-slice_fusion), channel_id=1, source_target_pairs={{0,64},{1,65},{2,66},{3,67},{4,68},{5,69},{6,70},{7,71},{8,72},{9,... | collective-permute-start | bytes 110600 | tf_op jit(solution)/shard_map/ppermute | solution.py:479
  19.1 6.8 %collective-permute-start.3 = (f32[38,8,128]{2,1,0:T(8,128)S(1)}, f32[38,8,128]{2,1,0:T(8,128)S(1)}, u32[]{:S(2)}, u32[]{:S(2)}) collective-permute-start(f32[38,8,128]{2,1,0:T(8,128)S(1)} %get-tuple-element.30), channel_id=1, source_target_pairs={{0,1},{1,0},{2,3},{3,2},{4,5},{5,4},{6,7},{7,6},{8,9},{9,8},{10,11... | collective-permute-start | bytes 466952 | tf_op jit(solution)/shard_map/ppermute | solution.py:479
  19.2 10.8 %collective-permute-start.4 = (f32[38,8,128]{2,1,0:T(8,128)S(1)}, f32[38,8,128]{2,1,0:T(8,128)S(1)}, u32[]{:S(2)}, u32[]{:S(2)}) collective-permute-start(f32[38,8,128]{2,1,0:T(8,128)S(1)} %get-tuple-element.31), channel_id=1, source_target_pairs={{1,2},{3,4},{5,6},{7,8},{9,10},{11,12},{13,14},{15,16},{17,18},{19... | collective-permute-start | bytes 466952 | tf_op jit(solution)/shard_map/ppermute | solution.py:479

commit v4 on v3

--- a/solution.py
+++ b/solution.py
@@ -1,5 +1,3 @@
-import math
-
 import jax
 import jax.numpy as jnp
 import numpy as np
@@ -13,8 +11,8 @@
 EDGE = tuple(sorted({n for face in FACES for n in face}))
 PLACE = {n: i for i, n in enumerate(EDGE)}
 LIFT = 0.06 * 10.0 * 0.5
-HALF = [0.5 ** (k + 1) / math.factorial(k + 1) for k in range(4)]
-WHOLE = [1.0 / math.factorial(k + 1) for k in range(4)]
+RATIO = (1.0 / 8.0, 1.0 / 6.0, 1.0 / 8.0)
+HALF, SECOND, WHOLE = (0.5, 1.0, 1.0, 1.0), (0.5, 3.0, 7.0, 15.0), (1.0, 4.0, 8.0, 16.0)
 AT_DEPTH, AT_FLAG, AT_X, AT_X2, AT_Y, AT_Y2, PLANES = 75, 100, 104, 120, 136, 152, 168
 IN_FACE, IN_SECOND, IN_SIDE, IN_ALL = 104, 120, 136, 152
 VALUES = [i for i in range(IN_ALL) if i < 101 or (i >= 104 and (i - 104) % 16 < 15)]
@@ -32,41 +30,49 @@
 STEP = -0.06 * derivative_matrix()
 
 
-def slope(f):
+def slope(f, scale, ends=False):
+    step = scale * STEP
     even_a, even_b, odd_a, odd_b = f[0] + f[4], f[1] + f[3], f[0] - f[4], f[1] - f[3]
     twice = f[2] + f[2]
     even_a, even_b = even_a - twice, even_b - twice
     out = [None] * 5
-    for i in (0, 1):
-        minus = float(STEP[i, 0] + STEP[i, 4]) * 0.5 * even_a + float(STEP[i, 1] + STEP[i, 3]) * 0.5 * even_b
-        plus = float(STEP[i, 0] - STEP[i, 4]) * 0.5 * odd_a + float(STEP[i, 1] - STEP[i, 3]) * 0.5 * odd_b
+    for i in (0,) if ends else (0, 1):
+        minus = float(step[i, 0] + step[i, 4]) * 0.5 * even_a + float(step[i, 1] + step[i, 3]) * 0.5 * even_b
+        plus = float(step[i, 0] - step[i, 4]) * 0.5 * odd_a + float(step[i, 1] - step[i, 3]) * 0.5 * odd_b
         out[i], out[4 - i] = plus + minus, plus - minus
-    out[2] = float(STEP[2, 0]) * odd_a + float(STEP[2, 1]) * odd_b
+    if not ends:
+        out[2] = float(step[2, 0]) * odd_a + float(step[2, 1]) * odd_b
     return out
 
 
-def operate(src, dst, depth):
-    spread = [None] * 25
+def operate(src, dst, depth, scale=1.0, axis=None):
     for j in range(5):
+        if axis == 1 and 0 < j < 4:
+            continue
         line = [5 * j + i for i in range(5)]
-        grad = slope([src[n] for n in line])
-        part = slope([src[25 + n] for n in line])
+        grad = slope([src[n] for n in line], scale, axis == 0)
+        part = slope([src[25 + n] for n in line], scale, axis == 0)
         for i, n in enumerate(line):
-            dst[25 + n] = depth(n) * grad[i]
-            dst[n] = part[i]
+            if grad[i] is not None:
+                dst[25 + n] = depth(n) * grad[i]
+                dst[n] = part[i]
     for i in range(5):
+        if axis == 0 and 0 < i < 4:
+            continue
         line = [5 * j + i for j in range(5)]
-        grad = slope([src[n] for n in line])
-        part = slope([src[50 + n] for n in line])
+        grad = slope([src[n] for n in line], scale, axis == 1)
+        part = slope([src[50 + n] for n in line], scale, axis == 1)
         for j, n in enumerate(line):
-            dst[50 + n] = depth(n) * grad[j]
-            dst[n] = dst[n] + part[j]
+            if grad[j] is not None:
+                dst[50 + n] = depth(n) * grad[j]
+                dst[n] = dst[n] + part[j]
 
 
 def weighted(values, weights):
-    total = weights[0] * values[0]
-    for value, weight in zip(values[1:], weights[1:]):
-        total = total + weight * value
+    total = None
+    for value, weight in zip(values, weights):
+        value = value if weight == 1.0 else weight * value
+        total = value if total is None else total + value
     return total
 
 
@@ -158,7 +164,7 @@
 
 
 def first_kernel(
-    sea_in, dep_in, near_in, owner_in, cl_in, ex, eo, ps, u, tr1, tr2, nf, cc, facts, sea, dep, nb, ow, cl, near, owner, sems
+    sea_in, dep_in, near_in, owner_in, cl_in, ex, eo, ps, u, tr1, tr2, nf, cc, facts, sea, dep, nb, ow, cl, near, owner, change, sems
 ):
     copies = [
         pltpu.make_async_copy(src, dst, sems.at[i])
@@ -187,16 +193,18 @@
     def depth(n):
         return get(AT_DEPTH + n)
 
-    for k in range(4):
-        operate(u.at[k], u.at[k + 1], depth)
+    for k in range(3):
+        operate(u.at[k], u.at[k + 1], depth, RATIO[k])
     for v in range(3):
         for n in range(25):
-            terms = [u[k, 25 * v + n] for k in range(5)]
-            put(25 * v + n, terms[0] + weighted(terms[1:], HALF))
+            terms = [u[k, 25 * v + n] for k in range(4)]
+            u[4, 25 * v + n] = weighted(terms, HALF)
             if n in PLACE:
-                first = weighted(terms[:4], HALF)
-                tr1[16 * v + PLACE[n]] = first
-                tr2[16 * v + PLACE[n]] = weighted(terms[:4], WHOLE) - first
+                tr1[16 * v + PLACE[n]] = weighted(terms, HALF)
+                tr2[16 * v + PLACE[n]] = weighted(terms, SECOND)
+    operate(u.at[4], change, depth)
+    for i in range(75):
+        put(i, u[0, i] + change[i])
     for f in range(4):
         sign = -1.0 if f % 2 == 0 else 1.0
         normal, tangent = (1, 2) if f < 2 else (2, 1)
@@ -249,14 +257,17 @@
         eo[5 + which] = total
 
 
-def messages_kernel(ps, u, facts, es, cb):
+def messages_kernel(ps, u, facts, es, cb, whole):
     grid = Grid()
     _, _, slots = read_facts(facts)
     south, north = row_edges(grid, ps)
     for a in range(5):
         es[a] = jnp.where(slots[2] == 2, south[a], north[a])
     for i in range(75):
-        cb[i] = u[0, i] + weighted([u[k, i] for k in range(1, 5)], WHOLE)
+        whole[i] = weighted([u[k, i] for k in range(4)], WHOLE)
+    operate(whole, cb, lambda n: ps[8 * (AT_DEPTH + n) : 8 * (AT_DEPTH + n) + 8, :])
+    for i in range(75):
+        cb[i] = cb[i] + u[0, i]
     turned = jnp.max(jnp.where((slots[0] == 2) | (slots[1] == 2), 1.0, 0.0)) > 0.5
 
     @pl.when(turned)
@@ -385,7 +396,7 @@
                     at_node = 25 * v + FACES[f][k]
                     g[0, at_node] = g[0, at_node] + jnp.where(mask, part, 0.0)
         for k in range(3):
-            operate(g.at[k], g.at[k + 1], halo_depth)
+            operate(g.at[k], g.at[k + 1], halo_depth, RATIO[k], axis if k == 2 else None)
         side = grid.south if axis else grid.west
         halo_fine = halo(AT_FLAG) > 0.5
         for v in range(3):
@@ -396,15 +407,18 @@
                     halo_fine, weighted(terms, HALF), halo(IN_SECOND + 5 * v + k)
                 )
 
-    for k in range(4):
-        operate(m.at[k], m.at[k + 1], depth)
-    fine = get(AT_FLAG) > 0.5
+    for k in range(3):
+        operate(m.at[k], m.at[k + 1], depth, RATIO[k])
     for v in range(3):
         for n in range(25):
-            terms = [m[k, 25 * v + n] for k in range(5)]
-            upd[25 * v + n] = jnp.where(fine, terms[0] + weighted(terms[1:], HALF), cb[25 * v + n])
+            value = weighted([m[k, 25 * v + n] for k in range(4)], HALF)
+            m[4, 25 * v + n] = value
             if n in PLACE:
-                late[16 * v + PLACE[n]] = weighted(terms[:4], HALF)
+                late[16 * v + PLACE[n]] = value
+    operate(m.at[4], m.at[1], depth)
+    fine = get(AT_FLAG) > 0.5
+    for i in range(75):
+        upd[i] = jnp.where(fine, m[0, i] + m[1, i], cb[i])
     for f in range(4):
         sign = -1.0 if f % 2 == 0 else 1.0
         axis = f // 2
@@ -494,6 +508,7 @@
             pltpu.VMEM((8, 128), jnp.int32),
             pltpu.VMEM((4, 8, 128), jnp.int32),
             pltpu.VMEM((4, 8, 128), jnp.int32),
+            pltpu.VMEM((75, 8, 128), F32),
             pltpu.SemaphoreType.DMA((5,)),
         ],
         compiler_params=PARAMS,
@@ -504,6 +519,7 @@
         out_shape=planes(9, 75),
         in_specs=[VM] * 3,
         out_specs=[VM] * 2,
+        scratch_shapes=[pltpu.VMEM((75, 8, 128), F32)],
         compiler_params=PARAMS,
         cost_estimate=pl.CostEstimate(flops=2_000_000, bytes_accessed=4_000_000, transcendentals=0),
         name="messages",

time: 31.5 us -> 31.4 us (level)
  no operation moved by 1% of the time
where the time goes in v4:
time: 31.4 us; the launch traced here: 31.2 us
  starting transfers between devices  16.2 us (52%)
  waiting for transfers between devices  9.16 us (29%)
  Pallas kernels  5.75 us (18%)
    ppermute x5, starting transfers between devices, passed(): return lax.ppermute(x, 'curve', pairs)  16.2 us
    ppermute x5, waiting for transfers between devices, passed(): return lax.ppermute(x, 'curve', pairs)  9.16 us
    pallas_call x1, Pallas kernels, local(): pl.pallas_call(first_kernel, out_shape=planes(7, 7) + [jax.ShapeDtypeStru...  2.28 us
    pallas_call x1, Pallas kernels, local(): pl.pallas_call(second_kernel, out_shape=planes(75, 38, 38) + [jax.ShapeDt...  1.45 us
    pallas_call x1, Pallas kernels, local(): pl.pallas_call(third_kernel, out_shape=jax.ShapeDtypeStruct((3, 25, 1024)...  1.41 us
  transfers between devices with their start and end apart: 5, of which 3 were waited for; matrix products, arithmetic and copies ran while one was open for 0% of the time, Pallas kernels for 2%

profile of v4, /device:TPU:6, one launch (start us, length us, event | category | flops | bytes accessed | tf_op | source)
XLA Modules:
  0.0 31.2 jit_solution(1784164529718058646)
XLA Ops:
  0.0 2.3 %predict.1 = (f32[7,8,128]{2,1,0:T(8,128)S(1)}, f32[7,8,128]{2,1,0:T(8,128)S(1)}, f32[1344,128]{1,0:T(8,128)S(1)}, f32[5,75,8,128]{3,2,1,0:T(8,128)S(1)}, f32[48...) custom-call(f32[3,25,1024]{2,1,0:T(8,128)} %sea_in.1, ...), custom_call_target="tpu_custom_call" | custom-call | tf_op jit(solution)/shard_map/predict/pallas_call | solution.py:495
  2.3 8.1 %collective-permute-start.1 = (f32[7,8,128]{2,1,0:T(8,128)S(1)}, f32[7,8,128]{2,1,0:T(8,128)S(1)}, u32[]{:S(2)}, u32[]{:S(2)}) collective-permute-start(f32[7,8,128]{2,1,0:T(8,128)S(1)} %get-tuple-element.20), channel_id=1, source_target_pairs={{1,2},{3,4},{5,6},{7,8},{9,10},{11,12},{13,14},{15,16},{17,18},{19... | collective-permute-start | bytes 86024 | tf_op jit(solution)/shard_map/ppermute | solution.py:493
  10.4 0.1 collective-permute-start
  10.5 0.2 messages.1
  10.7 1.2 %collective-permute-done.1.ro = f32[7,8,128]{2,1,0:T(8,128)S(1)} collective-permute-done((f32[7,8,128]{2,1,0:T(8,128)S(1)}, f32[7,8,128]{2,1,0:T(8,128)S(1)}, u32[]{:S(2)}, u32[]{:S(2)}) %collective-permute-start.1) | collective-permute-done | bytes 28704 | tf_op jit(solution)/shard_map/ppermute | solution.py:493
  11.9 0.0 collective-permute-done.rx
  11.9 0.0 copy-start
  12.0 1.2 %collective-permute-start.2 = (f32[9,8,128]{2,1,0:T(8,128)S(1)}, f32[9,8,128]{2,1,0:T(8,128)S(1)}, u32[]{:S(2)}, u32[]{:S(2)}) collective-permute-start(f32[9,8,128]{2,1,0:T(8,128)S(1)} %slice_dynamic-update-slice_fusion), channel_id=1, source_target_pairs={{0,64},{1,65},{2,66},{3,67},{4,68},{5,69},{6,70},{7,71},{8,72},{9,... | collective-permute-start | bytes 110600 | tf_op jit(solution)/shard_map/ppermute | solution.py:493
  13.2 0.4 %sides.1.hx_in = f32[1216,128]{1,0:T(8,128)S(1)} custom-call(f32[7,8,128]{2,1,0:T(8,128)S(1)} %collective-permute-done.rx, f32[7,8,128]{2,1,0:T(8,128)S(1)} %collective-permute-done.1.ro, s32[8,8,128]{2,1,0:T(8,128)S(1)} %get-tuple-element.23.facts), custom_call_target="tpu_custom_call" | custom-call | flops 2000000 | bytes 4000000 | tf_op jit(solution)/shard_map/sides/pallas_call | solution.py:531
  13.6 3.9 %collective-permute-done.2.rs = f32[9,8,128]{2,1,0:T(8,128)S(1)} collective-permute-done((f32[9,8,128]{2,1,0:T(8,128)S(1)}, f32[9,8,128]{2,1,0:T(8,128)S(1)}, u32[]{:S(2)}, u32[]{:S(2)}) %collective-permute-start.2) | collective-permute-done | bytes 36896 | tf_op jit(solution)/shard_map/ppermute | solution.py:493
  17.5 1.5 %correct.1 = (f32[75,8,128]{2,1,0:T(8,128)S(1)}, f32[38,8,128]{2,1,0:T(8,128)S(1)}, f32[38,8,128]{2,1,0:T(8,128)S(1)}, f32[1216,128]{1,0:T(8,128)S(1)}) custom-call(f32[7,8,128]{2,1,0:T(8,128)S(1)} %collective-permute-done.rx, f32[7,8,128]{2,1,0:T(8,128)S(1)} %collective-permute-done.1.ro, ...), custom_call_target="tpu_custom_call", output_to_operand_aliasing={{3}: (10, {})} | custom-call | tf_op jit(solution)/shard_map/correct/pallas_call | solution.py:540
  19.0 0.1 collective-permute-start.3
  19.1 6.7 %collective-permute-start.4 = (f32[38,8,128]{2,1,0:T(8,128)S(1)}, f32[38,8,128]{2,1,0:T(8,128)S(1)}, u32[]{:S(2)}, u32[]{:S(2)}) collective-permute-start(f32[38,8,128]{2,1,0:T(8,128)S(1)} %get-tuple-element.31), channel_id=1, source_target_pairs={{1,2},{3,4},{5,6},{7,8},{9,10},{11,12},{13,14},{15,16},{17,18},{19... | collective-permute-start | bytes 466952 | tf_op jit(solution)/shard_map/ppermute | solution.py:493
  25.8 0.0 collective-permute-done.3.re
  25.8 4.0 %collective-permute-done.4.ro = f32[38,8,128]{2,1,0:T(8,128)S(1)} collective-permute-done((f32[38,8,128]{2,1,0:T(8,128)S(1)}, f32[38,8,128]{2,1,0:T(8,128)S(1)}, u32[]{:S(2)}, u32[]{:S(2)}) %collective-permute-start.4) | collective-permute-done | bytes 155680 | tf_op jit(solution)/shard_map/ppermute | solution.py:493
  29.8 0.0 copy-done
  29.8 1.4 %migrate.1 = f32[3,25,1024]{2,1,0:T(8,128)} custom-call(s32[32]{0:T(128)S(1)} %copy-done, f32[38,8,128]{2,1,0:T(8,128)S(1)} %collective-permute-done.3.re, f32[38,8,128]{2,1,0:T(8,128)S(1)} %collective-permute-done.4.ro, f32[75,8,128]{2,1,0:T(8,128)S(1)} %get-tuple-element.32.upd), custom_call_target="tpu_custom_call" | custom-call | tf_op jit(solution)/shard_map/migrate/pallas_call | solution.py:561
  (2 shorter events, 0.0 us)
Async XLA Ops:
  2.3 9.6 %collective-permute-start.1 = (f32[7,8,128]{2,1,0:T(8,128)S(1)}, f32[7,8,128]{2,1,0:T(8,128)S(1)}, u32[]{:S(2)}, u32[]{:S(2)}) collective-permute-start(f32[7,8,128]{2,1,0:T(8,128)S(1)} %get-tuple-element.20), channel_id=1, source_target_pairs={{1,2},{3,4},{5,6},{7,8},{9,10},{11,12},{13,14},{15,16},{17,18},{19... | collective-permute-start | bytes 86024 | tf_op jit(solution)/shard_map/ppermute | solution.py:493
  10.4 1.5 %collective-permute-start = (f32[7,8,128]{2,1,0:T(8,128)S(1)}, f32[7,8,128]{2,1,0:T(8,128)S(1)}, u32[]{:S(2)}, u32[]{:S(2)}) collective-permute-start(f32[7,8,128]{2,1,0:T(8,128)S(1)} %get-tuple-element.19), channel_id=1, source_target_pairs={{0,1},{1,0},{2,3},{3,2},{4,5},{5,4},{6,7},{7,6},{8,9},{9,8},{10,11... | collective-permute-start | bytes 86024 | tf_op jit(solution)/shard_map/ppermute | solution.py:493
  11.9 17.9 %copy-start = (s32[32]{0:T(128)S(1)}, s32[32]{0:T(128)}, u32[]{:S(2)}) copy-start(s32[32]{0:T(128)} %swap.1) | copy-start | bytes 388
  12.0 5.5 %collective-permute-start.2 = (f32[9,8,128]{2,1,0:T(8,128)S(1)}, f32[9,8,128]{2,1,0:T(8,128)S(1)}, u32[]{:S(2)}, u32[]{:S(2)}) collective-permute-start(f32[9,8,128]{2,1,0:T(8,128)S(1)} %slice_dynamic-update-slice_fusion), channel_id=1, source_target_pairs={{0,64},{1,65},{2,66},{3,67},{4,68},{5,69},{6,70},{7,71},{8,72},{9,... | collective-permute-start | bytes 110600 | tf_op jit(solution)/shard_map/ppermute | solution.py:493
  19.0 6.8 %collective-permute-start.3 = (f32[38,8,128]{2,1,0:T(8,128)S(1)}, f32[38,8,128]{2,1,0:T(8,128)S(1)}, u32[]{:S(2)}, u32[]{:S(2)}) collective-permute-start(f32[38,8,128]{2,1,0:T(8,128)S(1)} %get-tuple-element.30), channel_id=1, source_target_pairs={{0,1},{1,0},{2,3},{3,2},{4,5},{5,4},{6,7},{7,6},{8,9},{9,8},{10,11... | collective-permute-start | bytes 466952 | tf_op jit(solution)/shard_map/ppermute | solution.py:493
  19.1 10.8 %collective-permute-start.4 = (f32[38,8,128]{2,1,0:T(8,128)S(1)}, f32[38,8,128]{2,1,0:T(8,128)S(1)}, u32[]{:S(2)}, u32[]{:S(2)}) collective-permute-start(f32[38,8,128]{2,1,0:T(8,128)S(1)} %get-tuple-element.31), channel_id=1, source_target_pairs={{1,2},{3,4},{5,6},{7,8},{9,10},{11,12},{13,14},{15,16},{17,18},{19... | collective-permute-start | bytes 466952 | tf_op jit(solution)/shard_map/ppermute | solution.py:493

commit v5 on v4

--- a/solution.py
+++ b/solution.py
@@ -233,19 +233,6 @@
                 at = [src[16 * v + PLACE[FACES[f][k]]] for f in range(4)]
                 put(x + i, jnp.where(grid.west, at[0], at[1]))
                 put(y + i, jnp.where(grid.south, at[2], at[3]))
-    west, east = side_edges(grid, get)
-    for slot, out in ((0, ex), (1, eo)):
-        for a in range(5):
-            out[a] = jnp.where(slots[0] == slot, west[a], east[a])
-    turned = jnp.max(jnp.where((slots[2] < 2) | (slots[3] < 2), 1.0, 0.0)) > 0.5
-
-    @pl.when(turned)
-    def _():
-        south, north = row_edges(grid, ps)
-        for slot, out in ((0, ex), (1, eo)):
-            for a in range(5):
-                out[a] = jnp.where(slots[2] == slot, south[a], jnp.where(slots[3] == slot, north[a], out[a]))
-
     blank = jnp.zeros((8, 128), F32)
     corner = ((col == 0) | (col == 31)) & (((sub == 0) & (lane < 32)) | ((sub == 7) & (lane >= 96)))
     for which, at, low, high, mask in ((0, AT_Y, 2, 3, grid.south), (1, AT_X, 0, 1, grid.west)):
@@ -255,6 +242,19 @@
             total = total + lanes(jnp.where(corner, value, 0.0), i)
         ex[5 + which] = total
         eo[5 + which] = total
+
+    west, east = side_edges(grid, get)
+    for slot, out in ((0, ex), (1, eo)):
+        for a in range(5):
+            out[a] = jnp.where(slots[0] == slot, west[a], east[a])
+    turned = jnp.max(jnp.where((slots[2] < 2) | (slots[3] < 2), 1.0, 0.0)) > 0.5
+
+    @pl.when(turned)
+    def _():
+        south, north = row_edges(grid, ps)
+        for slot, out in ((0, ex), (1, eo)):
+            for a in range(5):
+                out[a] = jnp.where(slots[2] == slot, south[a], jnp.where(slots[3] == slot, north[a], out[a]))
 
 
 def messages_kernel(ps, u, facts, es, cb, whole):
@@ -310,11 +310,6 @@
         [jnp.where(slots[f] == 0, rx[a], jnp.where(slots[f] == 1, ro[a], rs[a])) for a in range(5)] for f in range(4)
     ]
     turned = jnp.max(jnp.where((slots[0] == 2) | (slots[1] == 2), 1.0, 0.0)) > 0.5
-
-    @pl.when(turned)
-    def _():
-        unpack_sides(grid, got, hx)
-
     for group in range(IN_ALL // 8):
         a, q = divmod(group, 4)
         hy[pl.ds(64 * group, 8, stride=8), :] = lanes(got[2][a], -32 * q)
@@ -347,7 +342,13 @@
 
     for i in range(75):
         m[0, i] = get(i)
-    for axis, h, g, side, at in ((0, hx, gx, grid.west, AT_X), (1, hy, gy, grid.south, AT_Y)):
+    for axis, h, g, side, at in ((1, hy, gy, grid.south, AT_Y), (0, hx, gx, grid.west, AT_X)):
+        if axis == 0:
+
+            @pl.when(turned)
+            def _():
+                unpack_sides(grid, got, hx)
+
         first, last = 2 * axis, 2 * axis + 1
         normal, tangent = (2, 1) if axis else (1, 2)
         sign = jnp.where(side, 1.0, -1.0)
@@ -449,7 +450,7 @@
         so[p] = jnp.where(even, lanes(two, -32), one)
 
 
-def third_kernel(swap, re, ro, upd, out, buf, flat, sems):
+def settle_kernel(swap, re, upd, kept, take):
     grid = Grid()
     group = grid.lane // 32
     even = group % 2 == 0
@@ -458,12 +459,18 @@
     for b in range(32):
         moves = jnp.where(row == b, swap[b], moves)
     moves = moves > 0
+    take[0] = jnp.where(moves & ~even, 1.0, 0.0)
+    for i in range(75):
+        e = lanes(re[i // 2], -32) if i % 2 else re[i // 2]
+        kept[i] = jnp.where(moves & even, e, upd[i])
+
+
+def third_kernel(ro, kept, take, out, buf, flat, sems):
+    moves = take[0] > 0.5
     for v in range(3):
         for i in range(25 * v, 25 * v + 25):
-            e, o = re[i // 2], ro[i // 2]
-            if i % 2:
-                e, o = lanes(e, -32), lanes(o, 32)
-            buf[i] = jnp.where(moves, jnp.where(even, e, o), upd[i])
+            o = lanes(ro[i // 2], 32) if i % 2 else ro[i // 2]
+            buf[i] = jnp.where(moves, o, kept[i])
         flat[v] = buf[25 * v : 25 * v + 25].reshape(25, 1024)
         pltpu.make_async_copy(flat.at[v], out.at[v], sems.at[v]).start()
     for v in range(3):
@@ -558,10 +565,19 @@
     )(rx, ro, rs, ps, cb, tr1, tr2, nf, cc, facts, hx)
     got_odd = passed(so, odd_swap)
     got_even = passed(se, chip_swap)
+    kept, take = pl.pallas_call(
+        settle_kernel,
+        out_shape=planes(75, 1),
+        in_specs=[pl.BlockSpec(memory_space=pltpu.SMEM)] + [VM] * 2,
+        out_specs=[VM] * 2,
+        compiler_params=PARAMS,
+        cost_estimate=pl.CostEstimate(flops=2_000_000, bytes_accessed=4_000_000, transcendentals=0),
+        name="settle",
+    )(block_swap, got_even, upd)
     return pl.pallas_call(
         third_kernel,
         out_shape=jax.ShapeDtypeStruct((3, 25, 1024), F32),
-        in_specs=[pl.BlockSpec(memory_space=pltpu.SMEM)] + [VM] * 3,
+        in_specs=[VM] * 3,
         out_specs=ANY,
         scratch_shapes=[
             pltpu.VMEM((75, 8, 128), F32),
@@ -570,7 +586,7 @@
         ],
         compiler_params=PARAMS,
         name="migrate",
-    )(block_swap, got_even, got_odd, upd)
+    )(got_odd, kept, take)
 
 
 def solution(mesh):

time: 31.4 us -> 30.6 us (0.975)
  waiting for transfers between devices: 9.16 us -> 8.5 us
    ppermute x5, waiting for transfers between devices: 9.16 us -> 8.5 us  [passed(): return lax.ppermute(x, 'curve', pairs)]
    pallas_call x0 -> x1, Pallas kernels: none -> 0.65 us  [local(): pl.pallas_call(settle_kernel, out_shape=planes(75, 1), in_specs=[pl.Block...]
    pallas_call x1, Pallas kernels: 1.41 us -> 0.86 us  [local(): pl.pallas_call(third_kernel, out_shape=jax.ShapeDtypeStruct((3, 25, 1024)...]
  transfers between devices with their start and end apart: 5 -> 5, of which waited for: 3 -> 3; matrix products, arithmetic and copies ran while one was open for 0% -> 0% of each run, Pallas kernels for 2% -> 4%
where the time goes in v5:
time: 30.6 us; the launch traced here: 30.5 us
  starting transfers between devices  16.2 us (53%)
  waiting for transfers between devices  8.5 us (28%)
  Pallas kernels  5.66 us (18%)
    ppermute x5, starting transfers between devices, passed(): return lax.ppermute(x, 'curve', pairs)  16.2 us
    ppermute x5, waiting for transfers between devices, passed(): return lax.ppermute(x, 'curve', pairs)  8.5 us
    pallas_call x1, Pallas kernels, local(): pl.pallas_call(first_kernel, out_shape=planes(7, 7) + [jax.ShapeDtypeStru...  2.18 us
    pallas_call x1, Pallas kernels, local(): pl.pallas_call(second_kernel, out_shape=planes(75, 38, 38) + [jax.ShapeDt...  1.36 us
    pallas_call x1, Pallas kernels, local(): pl.pallas_call(third_kernel, out_shape=jax.ShapeDtypeStruct((3, 25, 1024)...  0.86 us
    pallas_call x1, Pallas kernels, local(): pl.pallas_call(settle_kernel, out_shape=planes(75, 1), in_specs=[pl.Block...  0.65 us
  transfers between devices with their start and end apart: 5, of which 3 were waited for; matrix products, arithmetic and copies ran while one was open for 0% of the time, Pallas kernels for 4%

profile of v5, /device:TPU:6, one launch (start us, length us, event | category | flops | bytes accessed | tf_op | source)
XLA Modules:
  0.0 30.5 jit_solution(16860129231317363521)
XLA Ops:
  0.0 2.2 %predict.1 = (f32[7,8,128]{2,1,0:T(8,128)S(1)}, f32[7,8,128]{2,1,0:T(8,128)S(1)}, f32[1344,128]{1,0:T(8,128)S(1)}, f32[5,75,8,128]{3,2,1,0:T(8,128)S(1)}, f32[48...) custom-call(f32[3,25,1024]{2,1,0:T(8,128)} %sea_in.1, ...), custom_call_target="tpu_custom_call" | custom-call | tf_op jit(solution)/shard_map/predict/pallas_call | solution.py:502
  2.2 8.1 %collective-permute-start.1 = (f32[7,8,128]{2,1,0:T(8,128)S(1)}, f32[7,8,128]{2,1,0:T(8,128)S(1)}, u32[]{:S(2)}, u32[]{:S(2)}) collective-permute-start(f32[7,8,128]{2,1,0:T(8,128)S(1)} %get-tuple-element.22), channel_id=1, source_target_pairs={{1,2},{3,4},{5,6},{7,8},{9,10},{11,12},{13,14},{15,16},{17,18},{19... | collective-permute-start | bytes 86024 | tf_op jit(solution)/shard_map/ppermute | solution.py:500
  10.3 0.1 collective-permute-start
  10.4 0.2 messages.1
  10.6 1.2 %collective-permute-done.1.ro = f32[7,8,128]{2,1,0:T(8,128)S(1)} collective-permute-done((f32[7,8,128]{2,1,0:T(8,128)S(1)}, f32[7,8,128]{2,1,0:T(8,128)S(1)}, u32[]{:S(2)}, u32[]{:S(2)}) %collective-permute-start.1) | collective-permute-done | bytes 28704 | tf_op jit(solution)/shard_map/ppermute | solution.py:500
  11.8 0.0 collective-permute-done.rx
  11.8 0.0 copy-start
  11.9 1.2 %collective-permute-start.2 = (f32[9,8,128]{2,1,0:T(8,128)S(1)}, f32[9,8,128]{2,1,0:T(8,128)S(1)}, u32[]{:S(2)}, u32[]{:S(2)}) collective-permute-start(f32[9,8,128]{2,1,0:T(8,128)S(1)} %slice_dynamic-update-slice_fusion), channel_id=1, source_target_pairs={{0,64},{1,65},{2,66},{3,67},{4,68},{5,69},{6,70},{7,71},{8,72},{9,... | collective-permute-start | bytes 110600 | tf_op jit(solution)/shard_map/ppermute | solution.py:500
  13.1 0.4 %sides.1.hx_in = f32[1216,128]{1,0:T(8,128)S(1)} custom-call(f32[7,8,128]{2,1,0:T(8,128)S(1)} %collective-permute-done.rx, f32[7,8,128]{2,1,0:T(8,128)S(1)} %collective-permute-done.1.ro, s32[8,8,128]{2,1,0:T(8,128)S(1)} %get-tuple-element.25.facts), custom_call_target="tpu_custom_call" | custom-call | flops 2000000 | bytes 4000000 | tf_op jit(solution)/shard_map/sides/pallas_call | solution.py:538
  13.5 3.9 %collective-permute-done.2.rs = f32[9,8,128]{2,1,0:T(8,128)S(1)} collective-permute-done((f32[9,8,128]{2,1,0:T(8,128)S(1)}, f32[9,8,128]{2,1,0:T(8,128)S(1)}, u32[]{:S(2)}, u32[]{:S(2)}) %collective-permute-start.2) | collective-permute-done | bytes 36896 | tf_op jit(solution)/shard_map/ppermute | solution.py:500
  17.4 1.4 %correct.1 = (f32[75,8,128]{2,1,0:T(8,128)S(1)}, f32[38,8,128]{2,1,0:T(8,128)S(1)}, f32[38,8,128]{2,1,0:T(8,128)S(1)}, f32[1216,128]{1,0:T(8,128)S(1)}) custom-call(f32[7,8,128]{2,1,0:T(8,128)S(1)} %collective-permute-done.rx, f32[7,8,128]{2,1,0:T(8,128)S(1)} %collective-permute-done.1.ro, ...), custom_call_target="tpu_custom_call", output_to_operand_aliasing={{3}: (10, {})} | custom-call | tf_op jit(solution)/shard_map/correct/pallas_call | solution.py:547
  18.8 0.1 collective-permute-start.4
  18.9 6.7 %collective-permute-start.3 = (f32[38,8,128]{2,1,0:T(8,128)S(1)}, f32[38,8,128]{2,1,0:T(8,128)S(1)}, u32[]{:S(2)}, u32[]{:S(2)}) collective-permute-start(f32[38,8,128]{2,1,0:T(8,128)S(1)} %get-tuple-element.32), channel_id=1, source_target_pairs={{1,2},{3,4},{5,6},{7,8},{9,10},{11,12},{13,14},{15,16},{17,18},{19... | collective-permute-start | bytes 466952 | tf_op jit(solution)/shard_map/ppermute | solution.py:500
  25.6 0.0 collective-permute-done.4.re
  25.6 0.0 copy-done
  25.6 0.6 %settle.1 = (f32[75,8,128]{2,1,0:T(8,128)S(1)}, f32[1,8,128]{2,1,0:T(8,128)S(1)}) custom-call(s32[32]{0:T(128)S(1)} %copy-done, f32[38,8,128]{2,1,0:T(8,128)S(1)} %collective-permute-done.4.re, f32[75,8,128]{2,1,0:T(8,128)S(1)} %get-tuple-element.34.upd), custom_call_target="tpu_custom_call" | custom-call | flops 2000000 | bytes 4000000 | tf_op jit(solution)/shard_map/settle/pallas_call | solution.py:568
  26.2 3.4 %collective-permute-done.3.ro = f32[38,8,128]{2,1,0:T(8,128)S(1)} collective-permute-done((f32[38,8,128]{2,1,0:T(8,128)S(1)}, f32[38,8,128]{2,1,0:T(8,128)S(1)}, u32[]{:S(2)}, u32[]{:S(2)}) %collective-permute-start.3) | collective-permute-done | bytes 155680 | tf_op jit(solution)/shard_map/ppermute | solution.py:500
  29.6 0.9 %migrate.1 = f32[3,25,1024]{2,1,0:T(8,128)} custom-call(f32[38,8,128]{2,1,0:T(8,128)S(1)} %collective-permute-done.3.ro, f32[75,8,128]{2,1,0:T(8,128)S(1)} %get-tuple-element.35.kept, f32[1,8,128]{2,1,0:T(8,128)S(1)} %get-tuple-element.36.take), custom_call_target="tpu_custom_call" | custom-call | tf_op jit(solution)/shard_map/migrate/pallas_call | solution.py:577
  (2 shorter events, 0.0 us)
Async XLA Ops:
  2.2 9.6 %collective-permute-start.1 = (f32[7,8,128]{2,1,0:T(8,128)S(1)}, f32[7,8,128]{2,1,0:T(8,128)S(1)}, u32[]{:S(2)}, u32[]{:S(2)}) collective-permute-start(f32[7,8,128]{2,1,0:T(8,128)S(1)} %get-tuple-element.22), channel_id=1, source_target_pairs={{1,2},{3,4},{5,6},{7,8},{9,10},{11,12},{13,14},{15,16},{17,18},{19... | collective-permute-start | bytes 86024 | tf_op jit(solution)/shard_map/ppermute | solution.py:500
  10.3 1.5 %collective-permute-start = (f32[7,8,128]{2,1,0:T(8,128)S(1)}, f32[7,8,128]{2,1,0:T(8,128)S(1)}, u32[]{:S(2)}, u32[]{:S(2)}) collective-permute-start(f32[7,8,128]{2,1,0:T(8,128)S(1)} %get-tuple-element.21), channel_id=1, source_target_pairs={{0,1},{1,0},{2,3},{3,2},{4,5},{5,4},{6,7},{7,6},{8,9},{9,8},{10,11... | collective-permute-start | bytes 86024 | tf_op jit(solution)/shard_map/ppermute | solution.py:500
  11.8 13.7 %copy-start = (s32[32]{0:T(128)S(1)}, s32[32]{0:T(128)}, u32[]{:S(2)}) copy-start(s32[32]{0:T(128)} %swap.1) | copy-start | bytes 388
  11.9 5.5 %collective-permute-start.2 = (f32[9,8,128]{2,1,0:T(8,128)S(1)}, f32[9,8,128]{2,1,0:T(8,128)S(1)}, u32[]{:S(2)}, u32[]{:S(2)}) collective-permute-start(f32[9,8,128]{2,1,0:T(8,128)S(1)} %slice_dynamic-update-slice_fusion), channel_id=1, source_target_pairs={{0,64},{1,65},{2,66},{3,67},{4,68},{5,69},{6,70},{7,71},{8,72},{9,... | collective-permute-start | bytes 110600 | tf_op jit(solution)/shard_map/ppermute | solution.py:500
  18.8 6.8 %collective-permute-start.4 = (f32[38,8,128]{2,1,0:T(8,128)S(1)}, f32[38,8,128]{2,1,0:T(8,128)S(1)}, u32[]{:S(2)}, u32[]{:S(2)}) collective-permute-start(f32[38,8,128]{2,1,0:T(8,128)S(1)} %get-tuple-element.33), channel_id=1, source_target_pairs={{0,1},{1,0},{2,3},{3,2},{4,5},{5,4},{6,7},{7,6},{8,9},{9,8},{10,11... | collective-permute-start | bytes 466952 | tf_op jit(solution)/shard_map/ppermute | solution.py:500
  18.9 10.8 %collective-permute-start.3 = (f32[38,8,128]{2,1,0:T(8,128)S(1)}, f32[38,8,128]{2,1,0:T(8,128)S(1)}, u32[]{:S(2)}, u32[]{:S(2)}) collective-permute-start(f32[38,8,128]{2,1,0:T(8,128)S(1)} %get-tuple-element.32), channel_id=1, source_target_pairs={{1,2},{3,4},{5,6},{7,8},{9,10},{11,12},{13,14},{15,16},{17,18},{19... | collective-permute-start | bytes 466952 | tf_op jit(solution)/shard_map/ppermute | solution.py:500

commit v6 on v5

--- a/solution.py
+++ b/solution.py
@@ -288,13 +288,57 @@
                 hx[8 * i : 8 * i + 8, :] = lanes(pair[i % 32 // 16], -2 * (i % 16))
 
 
-def sides_kernel(rx, ro, facts, hx):
-    _, _, slots = read_facts(facts)
-    unpack_sides(Grid(), [[jnp.where(slots[f] == 0, rx[a], ro[a]) for a in range(5)] for f in (0, 1)], hx)
+def touch(grid, axis, h, g, m, ps, masks, fast, before):
+    first, last = 2 * axis, 2 * axis + 1
+    normal, tangent = (2, 1) if axis else (1, 2)
+    side, at = (grid.south, AT_Y) if axis else (grid.west, AT_X)
+    sign = jnp.where(side, 1.0, -1.0)
+
+    def get(p):
+        return ps[8 * p : 8 * p + 8, :]
+
+    def halo(p):
+        return h[8 * p : 8 * p + 8, :]
+
+    for i in range(75):
+        g[0, i] = halo(i)
+    for k in range(5):
+        n, opposite = FACES[first][k], FACES[last][k]
+        a = [halo(IN_FACE + 5 * v + k) for v in range(3)]
+        b = [get(at + 5 * v + k) for v in range(3)]
+        own = jnp.where(side, get(AT_DEPTH + n), get(AT_DEPTH + opposite))
+        other = jnp.where(side, halo(AT_DEPTH + opposite), halo(AT_DEPTH + n))
+        speed = jnp.sqrt(jnp.maximum(own, other))
+        j = [b[v] - a[v] for v in range(3)]
+        out = flux(j[0], j[normal], j[tangent], speed, other, sign)
+        for v, part in ((0, out[0]), (normal, out[1]), (tangent, out[2])):
+            g[0, 25 * v + opposite] = g[0, 25 * v + opposite] + jnp.where(side, part, 0.0)
+            g[0, 25 * v + n] = g[0, 25 * v + n] + jnp.where(side, 0.0, part)
+        out = flux(-j[0], -j[normal], -j[tangent], speed, own, -sign)
+        for f in (first, last):
+            node = FACES[f][k]
+            fast[5 * f + k] = jnp.where(masks[f], speed, fast[5 * f + k])
+            for v in range(3):
+                before[15 * f + 5 * v + k] = jnp.where(masks[f], a[v], before[15 * f + 5 * v + k])
+            for v, part in ((0, out[0]), (normal, out[1]), (tangent, out[2])):
+                m[0, 25 * v + node] = m[0, 25 * v + node] + jnp.where(masks[f], part, 0.0)
+
+
+def sides_kernel(rx, ro, facts, ps, nf, cc, hx, gx, m, before, fast):
+    grid = Grid()
+    _, remotes, slots = read_facts(facts)
+    unpack_sides(grid, [[jnp.where(slots[f] == 0, rx[a], ro[a]) for a in range(5)] for f in (0, 1)], hx)
+    for i in range(75):
+        m[0, i] = ps[8 * i : 8 * i + 8, :]
+    for i in range(60):
+        before[i] = nf[i]
+    for i in range(20):
+        fast[i] = cc[i]
+    touch(grid, 0, hx, gx, m, ps, [remotes[f] & (slots[f] != 2) for f in (0, 1)], fast, before)
 
 
 def second_kernel(
-    rx, ro, rs, ps, cb, tr1, tr2, nf, cc, facts, hx_in, upd, se, so, hx, hy, m, gx, gy, late, before, after, fast
+    rx, ro, rs, ps, cb, tr1, tr2, facts, _hx, _gx, _m, _before, _fast, upd, se, so, hx, gx, m, before, fast, hy, gy, late, after
 ):
     grid = Grid()
     lane, sub = grid.lane, grid.sub
@@ -340,18 +384,16 @@
     corner_s = low & (corner_w | corner_e)
     corner_n = high & (corner_w | corner_e)
 
-    for i in range(75):
-        m[0, i] = get(i)
-    for axis, h, g, side, at in ((1, hy, gy, grid.south, AT_Y), (0, hx, gx, grid.west, AT_X)):
-        if axis == 0:
-
-            @pl.when(turned)
-            def _():
-                unpack_sides(grid, got, hx)
-
+    touch(grid, 1, hy, gy, m, ps, remotes, fast, before)
+
+    @pl.when(turned)
+    def _():
+        unpack_sides(grid, got, hx)
+        touch(grid, 0, hx, gx, m, ps, [remotes[f] & (slots[f] == 2) for f in (0, 1)], fast, before)
+
+    for axis, h, g in ((1, hy, gy), (0, hx, gx)):
         first, last = 2 * axis, 2 * axis + 1
         normal, tangent = (2, 1) if axis else (1, 2)
-        sign = jnp.where(side, 1.0, -1.0)
 
         def halo(p, h=h):
             return h[8 * p : 8 * p + 8, :]
@@ -359,28 +401,6 @@
         def halo_depth(n, halo=halo):
             return halo(AT_DEPTH + n)
 
-        for i in range(75):
-            g[0, i] = halo(i)
-        for k in range(5):
-            n, opposite = FACES[first][k], FACES[last][k]
-            a = [halo(IN_FACE + 5 * v + k) for v in range(3)]
-            b = [get(at + 5 * v + k) for v in range(3)]
-            own = jnp.where(side, depth(n), depth(opposite))
-            other = jnp.where(side, halo_depth(opposite), halo_depth(n))
-            speed = jnp.sqrt(jnp.maximum(own, other))
-            j = [b[v] - a[v] for v in range(3)]
-            out = flux(j[0], j[normal], j[tangent], speed, other, sign)
-            for v, part in ((0, out[0]), (normal, out[1]), (tangent, out[2])):
-                g[0, 25 * v + opposite] = g[0, 25 * v + opposite] + jnp.where(side, part, 0.0)
-                g[0, 25 * v + n] = g[0, 25 * v + n] + jnp.where(side, 0.0, part)
-            out = flux(-j[0], -j[normal], -j[tangent], speed, own, -sign)
-            for f in (first, last):
-                node = FACES[f][k]
-                fast[5 * f + k] = jnp.where(remotes[f], speed, cc[5 * f + k])
-                for v in range(3):
-                    before[15 * f + 5 * v + k] = jnp.where(remotes[f], a[v], nf[15 * f + 5 * v + k])
-                for v, part in ((0, out[0]), (normal, out[1]), (tangent, out[2])):
-                    m[0, 25 * v + node] = m[0, 25 * v + node] + jnp.where(remotes[f], part, 0.0)
         first, last = 2 - first, 3 - first
         on_first, on_last = (corner_w, corner_e) if axis else (corner_s, corner_n)
         side = grid.west if axis else grid.south
@@ -535,34 +555,35 @@
     rx = passed(ex, chip_swap)
     es = lax.dynamic_update_slice(lax.dynamic_update_slice(es, ro[5:], (7, 0, 0)), rx[5:], (5, 0, 0))
     rs = passed(es, [(i, (i + far) % devices) for i in range(devices)])
-    hx = pl.pallas_call(
+    kept_on = [
+        jax.ShapeDtypeStruct((8 * IN_ALL, 128), F32),
+        jax.ShapeDtypeStruct((4, 75, 8, 128), F32),
+        jax.ShapeDtypeStruct((5, 75, 8, 128), F32),
+    ] + planes(60, 20)
+    sides = pl.pallas_call(
         sides_kernel,
-        out_shape=jax.ShapeDtypeStruct((8 * IN_ALL, 128), F32),
-        in_specs=[VM] * 3,
-        out_specs=VM,
+        out_shape=kept_on,
+        in_specs=[VM] * 6,
+        out_specs=[VM] * 5,
         compiler_params=PARAMS,
         cost_estimate=pl.CostEstimate(flops=2_000_000, bytes_accessed=4_000_000, transcendentals=0),
         name="sides",
-    )(rx, ro, facts)
-    upd, se, so, _ = pl.pallas_call(
+    )(rx, ro, facts, ps, nf, cc)
+    upd, se, so, *_ = pl.pallas_call(
         second_kernel,
-        out_shape=planes(75, 38, 38) + [jax.ShapeDtypeStruct((8 * IN_ALL, 128), F32)],
-        in_specs=[VM] * 11,
-        out_specs=[VM] * 4,
-        input_output_aliases={10: 3},
+        out_shape=planes(75, 38, 38) + kept_on,
+        in_specs=[VM] * 13,
+        out_specs=[VM] * 8,
+        input_output_aliases={8 + i: 3 + i for i in range(5)},
         scratch_shapes=[
             pltpu.VMEM((8 * 160, 128), F32),
-            pltpu.VMEM((5, 75, 8, 128), F32),
-            pltpu.VMEM((4, 75, 8, 128), F32),
             pltpu.VMEM((4, 75, 8, 128), F32),
             pltpu.VMEM((48, 8, 128), F32),
-            pltpu.VMEM((60, 8, 128), F32),
             pltpu.VMEM((30, 8, 128), F32),
-            pltpu.VMEM((20, 8, 128), F32),
         ],
         compiler_params=PARAMS,
         name="correct",
-    )(rx, ro, rs, ps, cb, tr1, tr2, nf, cc, facts, hx)
+    )(rx, ro, rs, ps, cb, tr1, tr2, facts, *sides)
     got_odd = passed(so, odd_swap)
     got_even = passed(se, chip_swap)
     kept, take = pl.pallas_call(

time: 30.6 us -> 30.6 us (level)
  no operation moved by 1% of the time
where the time goes in v6:
time: 30.6 us; the launch traced here: 30.4 us
  starting transfers between devices  16.2 us (53%)
  waiting for transfers between devices  8.54 us (28%)
  Pallas kernels  5.57 us (18%)
    ppermute x5, starting transfers between devices, passed(): return lax.ppermute(x, 'curve', pairs)  16.2 us
    ppermute x5, waiting for transfers between devices, passed(): return lax.ppermute(x, 'curve', pairs)  8.54 us
    pallas_call x1, Pallas kernels, local(): pl.pallas_call(first_kernel, out_shape=planes(7, 7) + [jax.ShapeDtypeStru...  2.19 us
    pallas_call x1, Pallas kernels, local(): pl.pallas_call(second_kernel, out_shape=planes(75, 38, 38) + kept_on, in_...  1.3 us
    pallas_call x1, Pallas kernels, local(): pl.pallas_call(third_kernel, out_shape=jax.ShapeDtypeStruct((3, 25, 1024)...  0.86 us
    pallas_call x1, Pallas kernels, local(): pl.pallas_call(settle_kernel, out_shape=planes(75, 1), in_specs=[pl.Block...  0.65 us
  transfers between devices with their start and end apart: 5, of which 3 were waited for; matrix products, arithmetic and copies ran while one was open for 0% of the time, Pallas kernels for 4%

profile of v6, /device:TPU:6, one launch (start us, length us, event | category | flops | bytes accessed | tf_op | source)
XLA Modules:
  0.0 30.4 jit_solution(3093618857471298399)
XLA Ops:
  0.0 2.2 %predict.1 = (f32[7,8,128]{2,1,0:T(8,128)S(1)}, f32[7,8,128]{2,1,0:T(8,128)S(1)}, f32[1344,128]{1,0:T(8,128)S(1)}, f32[5,75,8,128]{3,2,1,0:T(8,128)S(1)}, f32[48...) custom-call(f32[3,25,1024]{2,1,0:T(8,128)} %sea_in.1, ...), custom_call_target="tpu_custom_call" | custom-call | tf_op jit(solution)/shard_map/predict/pallas_call | solution.py:522
  2.2 8.1 %collective-permute-start.1 = (f32[7,8,128]{2,1,0:T(8,128)S(1)}, f32[7,8,128]{2,1,0:T(8,128)S(1)}, u32[]{:S(2)}, u32[]{:S(2)}) collective-permute-start(f32[7,8,128]{2,1,0:T(8,128)S(1)} %get-tuple-element.27), channel_id=1, source_target_pairs={{1,2},{3,4},{5,6},{7,8},{9,10},{11,12},{13,14},{15,16},{17,18},{19... | collective-permute-start | bytes 86024 | tf_op jit(solution)/shard_map/ppermute | solution.py:520
  10.3 0.1 collective-permute-start
  10.4 0.2 messages.1
  10.6 1.2 %collective-permute-done.1.ro = f32[7,8,128]{2,1,0:T(8,128)S(1)} collective-permute-done((f32[7,8,128]{2,1,0:T(8,128)S(1)}, f32[7,8,128]{2,1,0:T(8,128)S(1)}, u32[]{:S(2)}, u32[]{:S(2)}) %collective-permute-start.1) | collective-permute-done | bytes 28704 | tf_op jit(solution)/shard_map/ppermute | solution.py:520
  11.8 0.0 collective-permute-done.rx
  11.9 1.2 %collective-permute-start.2 = (f32[9,8,128]{2,1,0:T(8,128)S(1)}, f32[9,8,128]{2,1,0:T(8,128)S(1)}, u32[]{:S(2)}, u32[]{:S(2)}) collective-permute-start(f32[9,8,128]{2,1,0:T(8,128)S(1)} %slice_dynamic-update-slice_fusion), channel_id=1, source_target_pairs={{0,64},{1,65},{2,66},{3,67},{4,68},{5,69},{6,70},{7,71},{8,72},{9,... | collective-permute-start | bytes 110600 | tf_op jit(solution)/shard_map/ppermute | solution.py:520
  13.1 0.3 %sides.1 = (f32[1216,128]{1,0:T(8,128)S(1)}, f32[4,75,8,128]{3,2,1,0:T(8,128)S(1)}, f32[5,75,8,128]{3,2,1,0:T(8,128)S(1)}, f32[60,8,128]{2,1,0:T(8,128)S(1)}, f32[20,8,128]{2,1,0:T(8,128)S(1)}) custom-call(f32[7,8,128]{2,1,0:T(8,128)S(1)} %collective-permute-done.rx, f32[7,8,128]{2,1,0:T(8,128)S(1)} %collective-permute-done.1.ro, ...), custom_call_target="tpu_custom_call" | custom-call | flops 2000000 | bytes 4000000 | tf_op jit(solution)/shard_map/sides/pallas_call | solution.py:563
  13.4 4.0 %collective-permute-done.2.rs = f32[9,8,128]{2,1,0:T(8,128)S(1)} collective-permute-done((f32[9,8,128]{2,1,0:T(8,128)S(1)}, f32[9,8,128]{2,1,0:T(8,128)S(1)}, u32[]{:S(2)}, u32[]{:S(2)}) %collective-permute-start.2) | collective-permute-done | bytes 36896 | tf_op jit(solution)/shard_map/ppermute | solution.py:520
  17.4 0.0 copy-start
  17.4 1.3 %correct.1 = (f32[75,8,128]{2,1,0:T(8,128)S(1)}, f32[38,8,128]{2,1,0:T(8,128)S(1)}, f32[38,8,128]{2,1,0:T(8,128)S(1)}, f32[1216,128]{1,0:T(8,128)S(1)}, f32[4,75...) custom-call(f32[7,8,128]{2,1,0:T(8,128)S(1)} %collective-permute-don, ...), custom_call_target="tpu_custom_call", output_to_operand_aliasing={{3}: (8, {}), {4}: (9, {}), {5}: (10, {}), {6}: (11, {}), {... | custom-call | tf_op jit(solution)/shard_map/correct/pallas_call | solution.py:572
  18.7 0.1 collective-permute-start.4
  18.8 6.7 %collective-permute-start.3 = (f32[38,8,128]{2,1,0:T(8,128)S(1)}, f32[38,8,128]{2,1,0:T(8,128)S(1)}, u32[]{:S(2)}, u32[]{:S(2)}) collective-permute-start(f32[38,8,128]{2,1,0:T(8,128)S(1)} %get-tuple-element.42), channel_id=1, source_target_pairs={{1,2},{3,4},{5,6},{7,8},{9,10},{11,12},{13,14},{15,16},{17,18},{19... | collective-permute-start | bytes 466952 | tf_op jit(solution)/shard_map/ppermute | solution.py:520
  25.5 0.0 collective-permute-done.4.re
  25.5 0.0 copy-done
  25.5 0.6 %settle.1 = (f32[75,8,128]{2,1,0:T(8,128)S(1)}, f32[1,8,128]{2,1,0:T(8,128)S(1)}) custom-call(s32[32]{0:T(128)S(1)} %copy-done, f32[38,8,128]{2,1,0:T(8,128)S(1)} %collective-permute-done.4.re, f32[75,8,128]{2,1,0:T(8,128)S(1)} %get-tuple-element.44.upd), custom_call_target="tpu_custom_call" | custom-call | flops 2000000 | bytes 4000000 | tf_op jit(solution)/shard_map/settle/pallas_call | solution.py:589
  26.2 3.4 %collective-permute-done.3.ro = f32[38,8,128]{2,1,0:T(8,128)S(1)} collective-permute-done((f32[38,8,128]{2,1,0:T(8,128)S(1)}, f32[38,8,128]{2,1,0:T(8,128)S(1)}, u32[]{:S(2)}, u32[]{:S(2)}) %collective-permute-start.3) | collective-permute-done | bytes 155680 | tf_op jit(solution)/shard_map/ppermute | solution.py:520
  29.6 0.9 %migrate.1 = f32[3,25,1024]{2,1,0:T(8,128)} custom-call(f32[38,8,128]{2,1,0:T(8,128)S(1)} %collective-permute-done.3.ro, f32[75,8,128]{2,1,0:T(8,128)S(1)} %get-tuple-element.45.kept, f32[1,8,128]{2,1,0:T(8,128)S(1)} %get-tuple-element.46.take), custom_call_target="tpu_custom_call" | custom-call | tf_op jit(solution)/shard_map/migrate/pallas_call | solution.py:598
  (2 shorter events, 0.0 us)
Async XLA Ops:
  2.2 9.6 %collective-permute-start.1 = (f32[7,8,128]{2,1,0:T(8,128)S(1)}, f32[7,8,128]{2,1,0:T(8,128)S(1)}, u32[]{:S(2)}, u32[]{:S(2)}) collective-permute-start(f32[7,8,128]{2,1,0:T(8,128)S(1)} %get-tuple-element.27), channel_id=1, source_target_pairs={{1,2},{3,4},{5,6},{7,8},{9,10},{11,12},{13,14},{15,16},{17,18},{19... | collective-permute-start | bytes 86024 | tf_op jit(solution)/shard_map/ppermute | solution.py:520
  10.3 1.5 %collective-permute-start = (f32[7,8,128]{2,1,0:T(8,128)S(1)}, f32[7,8,128]{2,1,0:T(8,128)S(1)}, u32[]{:S(2)}, u32[]{:S(2)}) collective-permute-start(f32[7,8,128]{2,1,0:T(8,128)S(1)} %get-tuple-element.26), channel_id=1, source_target_pairs={{0,1},{1,0},{2,3},{3,2},{4,5},{5,4},{6,7},{7,6},{8,9},{9,8},{10,11... | collective-permute-start | bytes 86024 | tf_op jit(solution)/shard_map/ppermute | solution.py:520
  11.9 5.5 %collective-permute-start.2 = (f32[9,8,128]{2,1,0:T(8,128)S(1)}, f32[9,8,128]{2,1,0:T(8,128)S(1)}, u32[]{:S(2)}, u32[]{:S(2)}) collective-permute-start(f32[9,8,128]{2,1,0:T(8,128)S(1)} %slice_dynamic-update-slice_fusion), channel_id=1, source_target_pairs={{0,64},{1,65},{2,66},{3,67},{4,68},{5,69},{6,70},{7,71},{8,72},{9,... | collective-permute-start | bytes 110600 | tf_op jit(solution)/shard_map/ppermute | solution.py:520
  17.4 8.1 %copy-start = (s32[32]{0:T(128)S(1)}, s32[32]{0:T(128)}, u32[]{:S(2)}) copy-start(s32[32]{0:T(128)} %swap.1) | copy-start | bytes 388
  18.7 6.8 %collective-permute-start.4 = (f32[38,8,128]{2,1,0:T(8,128)S(1)}, f32[38,8,128]{2,1,0:T(8,128)S(1)}, u32[]{:S(2)}, u32[]{:S(2)}) collective-permute-start(f32[38,8,128]{2,1,0:T(8,128)S(1)} %get-tuple-element.43), channel_id=1, source_target_pairs={{0,1},{1,0},{2,3},{3,2},{4,5},{5,4},{6,7},{7,6},{8,9},{9,8},{10,11... | collective-permute-start | bytes 466952 | tf_op jit(solution)/shard_map/ppermute | solution.py:520
  18.8 10.8 %collective-permute-start.3 = (f32[38,8,128]{2,1,0:T(8,128)S(1)}, f32[38,8,128]{2,1,0:T(8,128)S(1)}, u32[]{:S(2)}, u32[]{:S(2)}) collective-permute-start(f32[38,8,128]{2,1,0:T(8,128)S(1)} %get-tuple-element.42), channel_id=1, source_target_pairs={{1,2},{3,4},{5,6},{7,8},{9,10},{11,12},{13,14},{15,16},{17,18},{19... | collective-permute-start | bytes 466952 | tf_op jit(solution)/shard_map/ppermute | solution.py:520

commit v7 on v6

--- a/solution.py
+++ b/solution.py
@@ -174,11 +174,13 @@
         copy.start()
     grid = Grid()
     lane, sub, col = grid.lane, grid.sub, grid.col
-    for copy in copies:
+    for copy in copies[2:]:
         copy.wait()
     spread_ints(nb, near)
     spread_ints(ow, owner)
     face_facts(near, owner, facts)
+    for copy in copies[:2]:
+        copy.wait()
     walls, remotes, slots = read_facts(facts)
     inner = [~(walls[f] | remotes[f]) for f in range(4)]
     u[0] = sea[...].reshape(75, 8, 128)

time: 30.6 us -> 30.6 us (level)
  no operation moved by 1% of the time
where the time goes in v7:
time: 30.6 us; the launch traced here: 30.4 us
  starting transfers between devices  16.2 us (53%)
  waiting for transfers between devices  8.54 us (28%)
  Pallas kernels  5.55 us (18%)
    ppermute x5, starting transfers between devices, passed(): return lax.ppermute(x, 'curve', pairs)  16.2 us
    ppermute x5, waiting for transfers between devices, passed(): return lax.ppermute(x, 'curve', pairs)  8.54 us
    pallas_call x1, Pallas kernels, local(): pl.pallas_call(first_kernel, out_shape=planes(7, 7) + [jax.ShapeDtypeStru...  2.16 us
    pallas_call x1, Pallas kernels, local(): pl.pallas_call(second_kernel, out_shape=planes(75, 38, 38) + kept_on, in_...  1.3 us
    pallas_call x1, Pallas kernels, local(): pl.pallas_call(third_kernel, out_shape=jax.ShapeDtypeStruct((3, 25, 1024)...  0.86 us
    pallas_call x1, Pallas kernels, local(): pl.pallas_call(settle_kernel, out_shape=planes(75, 1), in_specs=[pl.Block...  0.65 us
  transfers between devices with their start and end apart: 5, of which 3 were waited for; matrix products, arithmetic and copies ran while one was open for 0% of the time, Pallas kernels for 4%

profile of v7, /device:TPU:6, one launch (start us, length us, event | category | flops | bytes accessed | tf_op | source)
XLA Modules:
  0.0 30.4 jit_solution(4363333948441216107)
XLA Ops:
  0.0 2.2 %predict.1 = (f32[7,8,128]{2,1,0:T(8,128)S(1)}, f32[7,8,128]{2,1,0:T(8,128)S(1)}, f32[1344,128]{1,0:T(8,128)S(1)}, f32[5,75,8,128]{3,2,1,0:T(8,128)S(1)}, f32[48...) custom-call(f32[3,25,1024]{2,1,0:T(8,128)} %sea_in.1, ...), custom_call_target="tpu_custom_call" | custom-call | tf_op jit(solution)/shard_map/predict/pallas_call | solution.py:524
  2.2 8.1 %collective-permute-start.1 = (f32[7,8,128]{2,1,0:T(8,128)S(1)}, f32[7,8,128]{2,1,0:T(8,128)S(1)}, u32[]{:S(2)}, u32[]{:S(2)}) collective-permute-start(f32[7,8,128]{2,1,0:T(8,128)S(1)} %get-tuple-element.27), channel_id=1, source_target_pairs={{1,2},{3,4},{5,6},{7,8},{9,10},{11,12},{13,14},{15,16},{17,18},{19... | collective-permute-start | bytes 86024 | tf_op jit(solution)/shard_map/ppermute | solution.py:522
  10.3 0.1 collective-permute-start
  10.4 0.2 messages.1
  10.6 1.2 %collective-permute-done.1.ro = f32[7,8,128]{2,1,0:T(8,128)S(1)} collective-permute-done((f32[7,8,128]{2,1,0:T(8,128)S(1)}, f32[7,8,128]{2,1,0:T(8,128)S(1)}, u32[]{:S(2)}, u32[]{:S(2)}) %collective-permute-start.1) | collective-permute-done | bytes 28704 | tf_op jit(solution)/shard_map/ppermute | solution.py:522
  11.8 0.0 collective-permute-done.rx
  11.8 1.2 %collective-permute-start.2 = (f32[9,8,128]{2,1,0:T(8,128)S(1)}, f32[9,8,128]{2,1,0:T(8,128)S(1)}, u32[]{:S(2)}, u32[]{:S(2)}) collective-permute-start(f32[9,8,128]{2,1,0:T(8,128)S(1)} %slice_dynamic-update-slice_fusion), channel_id=1, source_target_pairs={{0,64},{1,65},{2,66},{3,67},{4,68},{5,69},{6,70},{7,71},{8,72},{9,... | collective-permute-start | bytes 110600 | tf_op jit(solution)/shard_map/ppermute | solution.py:522
  13.1 0.3 %sides.1 = (f32[1216,128]{1,0:T(8,128)S(1)}, f32[4,75,8,128]{3,2,1,0:T(8,128)S(1)}, f32[5,75,8,128]{3,2,1,0:T(8,128)S(1)}, f32[60,8,128]{2,1,0:T(8,128)S(1)}, f32[20,8,128]{2,1,0:T(8,128)S(1)}) custom-call(f32[7,8,128]{2,1,0:T(8,128)S(1)} %collective-permute-done.rx, f32[7,8,128]{2,1,0:T(8,128)S(1)} %collective-permute-done.1.ro, ...), custom_call_target="tpu_custom_call" | custom-call | flops 2000000 | bytes 4000000 | tf_op jit(solution)/shard_map/sides/pallas_call | solution.py:565
  13.4 4.0 %collective-permute-done.2.rs = f32[9,8,128]{2,1,0:T(8,128)S(1)} collective-permute-done((f32[9,8,128]{2,1,0:T(8,128)S(1)}, f32[9,8,128]{2,1,0:T(8,128)S(1)}, u32[]{:S(2)}, u32[]{:S(2)}) %collective-permute-start.2) | collective-permute-done | bytes 36896 | tf_op jit(solution)/shard_map/ppermute | solution.py:522
  17.4 0.0 copy-start
  17.4 1.3 %correct.1 = (f32[75,8,128]{2,1,0:T(8,128)S(1)}, f32[38,8,128]{2,1,0:T(8,128)S(1)}, f32[38,8,128]{2,1,0:T(8,128)S(1)}, f32[1216,128]{1,0:T(8,128)S(1)}, f32[4,75...) custom-call(f32[7,8,128]{2,1,0:T(8,128)S(1)} %collective-permute-don, ...), custom_call_target="tpu_custom_call", output_to_operand_aliasing={{3}: (8, {}), {4}: (9, {}), {5}: (10, {}), {6}: (11, {}), {... | custom-call | tf_op jit(solution)/shard_map/correct/pallas_call | solution.py:574
  18.7 0.1 collective-permute-start.4
  18.8 6.7 %collective-permute-start.3 = (f32[38,8,128]{2,1,0:T(8,128)S(1)}, f32[38,8,128]{2,1,0:T(8,128)S(1)}, u32[]{:S(2)}, u32[]{:S(2)}) collective-permute-start(f32[38,8,128]{2,1,0:T(8,128)S(1)} %get-tuple-element.42), channel_id=1, source_target_pairs={{1,2},{3,4},{5,6},{7,8},{9,10},{11,12},{13,14},{15,16},{17,18},{19... | collective-permute-start | bytes 466952 | tf_op jit(solution)/shard_map/ppermute | solution.py:522
  25.5 0.0 collective-permute-done.4.re
  25.5 0.0 copy-done
  25.5 0.6 %settle.1 = (f32[75,8,128]{2,1,0:T(8,128)S(1)}, f32[1,8,128]{2,1,0:T(8,128)S(1)}) custom-call(s32[32]{0:T(128)S(1)} %copy-done, f32[38,8,128]{2,1,0:T(8,128)S(1)} %collective-permute-done.4.re, f32[75,8,128]{2,1,0:T(8,128)S(1)} %get-tuple-element.44.upd), custom_call_target="tpu_custom_call" | custom-call | flops 2000000 | bytes 4000000 | tf_op jit(solution)/shard_map/settle/pallas_call | solution.py:591
  26.2 3.4 %collective-permute-done.3.ro = f32[38,8,128]{2,1,0:T(8,128)S(1)} collective-permute-done((f32[38,8,128]{2,1,0:T(8,128)S(1)}, f32[38,8,128]{2,1,0:T(8,128)S(1)}, u32[]{:S(2)}, u32[]{:S(2)}) %collective-permute-start.3) | collective-permute-done | bytes 155680 | tf_op jit(solution)/shard_map/ppermute | solution.py:522
  29.5 0.9 %migrate.1 = f32[3,25,1024]{2,1,0:T(8,128)} custom-call(f32[38,8,128]{2,1,0:T(8,128)S(1)} %collective-permute-done.3.ro, f32[75,8,128]{2,1,0:T(8,128)S(1)} %get-tuple-element.45.kept, f32[1,8,128]{2,1,0:T(8,128)S(1)} %get-tuple-element.46.take), custom_call_target="tpu_custom_call" | custom-call | tf_op jit(solution)/shard_map/migrate/pallas_call | solution.py:600
  (2 shorter events, 0.0 us)
Async XLA Ops:
  2.2 9.6 %collective-permute-start.1 = (f32[7,8,128]{2,1,0:T(8,128)S(1)}, f32[7,8,128]{2,1,0:T(8,128)S(1)}, u32[]{:S(2)}, u32[]{:S(2)}) collective-permute-start(f32[7,8,128]{2,1,0:T(8,128)S(1)} %get-tuple-element.27), channel_id=1, source_target_pairs={{1,2},{3,4},{5,6},{7,8},{9,10},{11,12},{13,14},{15,16},{17,18},{19... | collective-permute-start | bytes 86024 | tf_op jit(solution)/shard_map/ppermute | solution.py:522
  10.3 1.5 %collective-permute-start = (f32[7,8,128]{2,1,0:T(8,128)S(1)}, f32[7,8,128]{2,1,0:T(8,128)S(1)}, u32[]{:S(2)}, u32[]{:S(2)}) collective-permute-start(f32[7,8,128]{2,1,0:T(8,128)S(1)} %get-tuple-element.26), channel_id=1, source_target_pairs={{0,1},{1,0},{2,3},{3,2},{4,5},{5,4},{6,7},{7,6},{8,9},{9,8},{10,11... | collective-permute-start | bytes 86024 | tf_op jit(solution)/shard_map/ppermute | solution.py:522
  11.8 5.5 %collective-permute-start.2 = (f32[9,8,128]{2,1,0:T(8,128)S(1)}, f32[9,8,128]{2,1,0:T(8,128)S(1)}, u32[]{:S(2)}, u32[]{:S(2)}) collective-permute-start(f32[9,8,128]{2,1,0:T(8,128)S(1)} %slice_dynamic-update-slice_fusion), channel_id=1, source_target_pairs={{0,64},{1,65},{2,66},{3,67},{4,68},{5,69},{6,70},{7,71},{8,72},{9,... | collective-permute-start | bytes 110600 | tf_op jit(solution)/shard_map/ppermute | solution.py:522
  17.4 8.1 %copy-start = (s32[32]{0:T(128)S(1)}, s32[32]{0:T(128)}, u32[]{:S(2)}) copy-start(s32[32]{0:T(128)} %swap.1) | copy-start | bytes 388
  18.7 6.8 %collective-permute-start.4 = (f32[38,8,128]{2,1,0:T(8,128)S(1)}, f32[38,8,128]{2,1,0:T(8,128)S(1)}, u32[]{:S(2)}, u32[]{:S(2)}) collective-permute-start(f32[38,8,128]{2,1,0:T(8,128)S(1)} %get-tuple-element.43), channel_id=1, source_target_pairs={{0,1},{1,0},{2,3},{3,2},{4,5},{5,4},{6,7},{7,6},{8,9},{9,8},{10,11... | collective-permute-start | bytes 466952 | tf_op jit(solution)/shard_map/ppermute | solution.py:522
  18.8 10.8 %collective-permute-start.3 = (f32[38,8,128]{2,1,0:T(8,128)S(1)}, f32[38,8,128]{2,1,0:T(8,128)S(1)}, u32[]{:S(2)}, u32[]{:S(2)}) collective-permute-start(f32[38,8,128]{2,1,0:T(8,128)S(1)} %get-tuple-element.42), channel_id=1, source_target_pairs={{1,2},{3,4},{5,6},{7,8},{9,10},{11,12},{13,14},{15,16},{17,18},{19... | collective-permute-start | bytes 466952 | tf_op jit(solution)/shard_map/ppermute | solution.py:522
